TPU v7x, 256 devices: a whole 4x4x8 slice. The times are simulated.
256 devices in a mesh: ctx: 32 (over x, z), head: 8 (over y, core).
Axes of the slice: x: 4, y: 4, z: 8, core: 2. Of those that a mesh axis runs over, the one named last changes fastest.
Arguments:
- signal: bfloat16 [49152, 5120], P(('ctx', 'head')), may hold values from -0.125 to 0.125
- cotangent: bfloat16 [49152, 5120], P(('ctx', 'head')), may hold values from -0.125 to 0.125
- input_map: bfloat16 [49152, 128], P('ctx'), may hold values from -1.75 to 1.75
- output_map: bfloat16 [49152, 128], P('ctx'), may hold values from -1.75 to 1.75
- log_decay: float32 [49152, 80], P('ctx', 'head'), may hold values from -1 to 0, as said below
- skip_gain: float32 [80], P('head'), may hold values from 0.5 to 2
Outputs:
- scan_out: bfloat16 [49152, 5120], P(('ctx', 'head'))
- grad_signal: bfloat16 [49152, 5120], P(('ctx', 'head'))
- grad_input_map: float32 [49152, 128], P('ctx')
- grad_output_map: float32 [49152, 128], P('ctx')
- grad_decay: float32 [49152, 80], P('ctx', 'head')
Inputs may be any that keep to these rules, and one draw needn't show every extreme that they name: `log_decay`: every entry is negative.
All inputs are finite; a program needn't handle non-finite values.
Results may differ from a plain program's by a relative error of at most 0.0027.
Values may be sent and summed in bfloat16 or wider, within the bound.
No kernel may reach another device: no remote copies, remote signals or barrier semaphores. Data moves between devices by JAX's collectives and lax.ppermute only.
A program may use at most 192 MiB of HBM per device.

v0:
```python
import jax
import jax.numpy as jnp
from jax import lax
from jax.experimental import pallas as pl
from jax.experimental.pallas import tpu as pltpu
from jax.sharding import Mesh
from jax.sharding import PartitionSpec as P

ROWS = 192
N = 128
HEAD = 64
HG = 10
GC = HG * HEAD
GROUPS = 8
PAIRS = GC // 128
F32, BF16 = jnp.float32, jnp.bfloat16
SWAP = [(0, 1), (1, 0)]
NN = (((1,), (0,)), ((), ()))
NT = (((1,), (1,)), ((), ()))
TN = (((0,), (0,)), ((), ()))


def dot(a, b, dims=NN):
    return lax.dot_general(a, b, dims, preferred_element_type=F32)


def halves(v):
    high = v.astype(BF16)
    return high, (v - high.astype(F32)).astype(BF16)


def thirds(v):
    high = v.astype(BF16)
    rest = v - high.astype(F32)
    middle = rest.astype(BF16)
    return high, middle, (rest - middle.astype(F32)).astype(BF16)


def spread(columns):
    rows = columns.shape[0]
    first = lax.broadcasted_iota(jnp.int32, (rows, 128), 1) < HEAD
    return jnp.concatenate(
        [
            jnp.where(
                first,
                jnp.broadcast_to(columns[:, 2 * p : 2 * p + 1], (rows, 128)),
                jnp.broadcast_to(columns[:, 2 * p + 1 : 2 * p + 2], (rows, 128)),
            )
            for p in range(PAIRS)
        ],
        axis=1,
    )


def states_kernel(core, x_ref, dy_ref, cum_ref, bt_ref, ct_ref, s_ref, g_ref):
    cum = cum_ref[0]
    to_end = jnp.exp(cum[ROWS - 1 : ROWS, :] - cum)
    high, low = halves(x_ref[...].astype(F32) * spread(to_end))
    bt = bt_ref[...]
    s_ref[0, 0] = dot(bt, high) + dot(bt, low)
    high, low = halves(dy_ref[...].astype(F32) * spread(jnp.exp(cum)))
    ct = ct_ref[...]
    g_ref[0, 0] = dot(ct, high) + dot(ct, low)


def local_states(core, x, dy, cum, bt, ct):
    def group(s, core):
        return 2 * (s % 4) + (core[0] + 1 + s // 4) % 2

    state = jax.ShapeDtypeStruct((2, 4, N, GC), F32)
    whole = lambda s, core: (0, 0)
    return pl.pallas_call(
        states_kernel,
        grid_spec=pltpu.PrefetchScalarGridSpec(
            num_scalar_prefetch=1,
            grid=(GROUPS,),
            in_specs=[
                pl.BlockSpec((ROWS, GC), lambda s, core: (0, group(s, core))),
                pl.BlockSpec((ROWS, GC), lambda s, core: (0, group(s, core))),
                pl.BlockSpec((1, ROWS, 16), lambda s, core: (group(s, core), 0, 0)),
                pl.BlockSpec((N, ROWS), whole),
                pl.BlockSpec((N, ROWS), whole),
            ],
            out_specs=[
                pl.BlockSpec((1, 1, N, GC), lambda s, core: (s // 4, s % 4, 0, 0)),
                pl.BlockSpec((1, 1, N, GC), lambda s, core: (s // 4, s % 4, 0, 0)),
            ],
        ),
        out_shape=[state, state],
        compiler_params=pltpu.CompilerParams(vmem_limit_bytes=40 << 20),
        name="local_states",
    )(core, x, dy, cum, bt, ct)


def within_kernel(
    x_ref, dy_ref, cum_ref, cumt_ref, b_ref, c_ref, y_ref, dx_ref, db_ref, dc_ref, score_ref, acc_ref
):
    step = pl.program_id(0)
    causal = lax.broadcasted_iota(jnp.int32, (ROWS, ROWS), 0) >= lax.broadcasted_iota(
        jnp.int32, (ROWS, ROWS), 1
    )

    @pl.when(step == 0)
    def _():
        score_ref[...] = jnp.where(causal, dot(c_ref[...], b_ref[...], NT), 0.0)
        acc_ref[...] = jnp.zeros_like(acc_ref)

    first = lax.broadcasted_iota(jnp.int32, (ROWS, 128), 1) < HEAD
    zero = jnp.zeros((ROWS, 128), BF16)
    for p in range(PAIRS):
        columns = slice(128 * p, 128 * p + 128)
        x = x_ref[:, columns]
        dy = dy_ref[:, columns]
        y = dx = None
        for side in range(2):
            h = 2 * p + side
            keep = first if side == 0 else jnp.logical_not(first)
            xs = jnp.where(keep, x, zero)
            dys = jnp.where(keep, dy, zero)
            decay = jnp.exp(
                jnp.minimum(cum_ref[0, :, h : h + 1] - cumt_ref[0, h : h + 1, :], 0.0)
            )
            weights = (score_ref[...] * decay).astype(BF16)
            part = dot(weights, xs)
            y = part if y is None else y + part
            dweights = dot(dys, x, NT).astype(BF16).astype(F32)
            acc_ref[...] += dweights * decay
            part = dot(weights, dys, TN)
            dx = part if dx is None else dx + part
        y_ref[:, columns] = y
        dx_ref[:, columns] = dx

    @pl.when(step == GROUPS - 1)
    def _():
        high, low = halves(jnp.where(causal, acc_ref[...], 0.0))
        b, c = b_ref[...], c_ref[...]
        dc_ref[...] = dot(high, b) + dot(low, b)
        db_ref[...] = dot(high, c, TN) + dot(low, c, TN)


def within(x, dy, cum, cumt, b, c):
    by_column = pl.BlockSpec((ROWS, GC), lambda s: (0, s))
    whole = pl.BlockSpec((ROWS, N), lambda s: (0, 0))
    wide = jax.ShapeDtypeStruct((ROWS, GC * GROUPS), F32)
    small = jax.ShapeDtypeStruct((ROWS, N), F32)
    return pl.pallas_call(
        within_kernel,
        grid=(GROUPS,),
        in_specs=[
            by_column,
            by_column,
            pl.BlockSpec((1, ROWS, 16), lambda s: (s, 0, 0)),
            pl.BlockSpec((1, 16, ROWS), lambda s: (s, 0, 0)),
            whole,
            whole,
        ],
        out_specs=[by_column, by_column, whole, whole],
        out_shape=[wide, wide, small, small],
        scratch_shapes=[pltpu.VMEM((ROWS, ROWS), F32), pltpu.VMEM((ROWS, ROWS), F32)],
        compiler_params=pltpu.CompilerParams(vmem_limit_bytes=40 << 20),
        cost_estimate=pl.CostEstimate(
            flops=20_000_000_000, bytes_accessed=12_000_000, transcendentals=3_000_000
        ),
        name="within_chunk",
    )(x, dy, cum, cumt, b, c)


def finish_kernel(
    core, x_ref, dy_ref, cum_ref, cumt_ref, y_ref, dx_ref, ekeep_ref, ecome_ref, gkeep_ref, gcome_ref,
    gain_ref, b_ref, c_ref, db0_ref, dc0_ref, out_ref, gs_ref, db_ref, dc_ref, gd_ref,
):
    step = pl.program_id(0)

    @pl.when(step == 0)
    def _():
        db_ref[...] = db0_ref[...]
        dc_ref[...] = dc0_ref[...]

    kept = step < 4
    entering = jnp.where(kept, ekeep_ref[0], ecome_ref[0])
    leaving = jnp.where(kept, gkeep_ref[0], gcome_ref[0])
    cum = cum_ref[0]
    from_start = spread(jnp.exp(cum))
    to_end = spread(jnp.exp(cum[ROWS - 1 : ROWS, :] - cum))
    x = x_ref[...].astype(F32)
    dy = dy_ref[...].astype(F32)
    gain = gain_ref[0]
    b, c = b_ref[...], c_ref[...]
    e_high, e_low = halves(entering)
    y = y_ref[...] + from_start * (dot(c, e_high) + dot(c, e_low))
    out_ref[...] = (y + gain * x).astype(BF16)
    g_high, g_low = halves(leaving)
    dx_in = dx_ref[...]
    dx_carried = to_end * (dot(b, g_high) + dot(b, g_low))
    gs_ref[...] = (dx_in + dx_carried + gain * dy).astype(BF16)
    high, low = halves(from_start * dy)
    dc_ref[...] += dot(high, e_high, NT) + dot(high, e_low, NT) + dot(low, e_high, NT)
    high, low = halves(to_end * x)
    db_ref[...] += dot(high, g_high, NT) + dot(high, g_low, NT) + dot(low, g_high, NT)
    of_head = (
        lax.broadcasted_iota(jnp.int32, (16, GC), 1) // HEAD
        == lax.broadcasted_iota(jnp.int32, (16, GC), 0)
    ).astype(BF16)

    def by_head(v):
        high, low = halves(v)
        return dot(of_head, high, NT) + dot(of_head, low, NT)

    here = by_head(dy * y - x * dx_in)
    carried = by_head(x * dx_carried)
    across = by_head(
        jnp.broadcast_to(jnp.sum(entering * leaving, axis=0, keepdims=True), (ROWS, GC))
    )
    t = lax.broadcasted_iota(jnp.int32, (ROWS, ROWS), 0)
    s = lax.broadcasted_iota(jnp.int32, (ROWS, ROWS), 1)
    after = (t >= s).astype(BF16)
    before = (t < s).astype(BF16)
    gd = across * jnp.exp(cumt_ref[0, :, ROWS - 1 : ROWS])
    for part in thirds(here):
        gd += dot(part, after)
    for part in thirds(carried):
        gd += dot(part, before)
    gd_ref[0] = gd


def finish(core, x, dy, cum, cumt, y, dx, ekeep, ecome, gkeep, gcome, gain, b, c, db, dc):
    def group(s, core):
        return 2 * (s % 4) + (core[0] + s // 4) % 2

    by_column = pl.BlockSpec((ROWS, GC), lambda s, core: (0, group(s, core)))
    by_group = lambda *shape: pl.BlockSpec(
        (1, *shape), lambda s, core: (group(s, core), *(0 for _ in shape))
    )
    kept = pl.BlockSpec((1, N, GC), lambda s, core: (jnp.minimum(s, 3), 0, 0))
    come = pl.BlockSpec((1, N, GC), lambda s, core: (jnp.maximum(s - 4, 0), 0, 0))
    whole = pl.BlockSpec((ROWS, N), lambda s, core: (0, 0))
    narrow = jax.ShapeDtypeStruct((ROWS, GC * GROUPS), BF16)
    small = jax.ShapeDtypeStruct((ROWS, N), F32)
    return pl.pallas_call(
        finish_kernel,
        grid_spec=pltpu.PrefetchScalarGridSpec(
            num_scalar_prefetch=1,
            grid=(GROUPS,),
            in_specs=[
                by_column, by_column, by_group(ROWS, 16), by_group(16, ROWS), by_column, by_column,
                kept, come, kept, come, by_group(1, GC), whole, whole, whole, whole,
            ],
            out_specs=[by_column, by_column, whole, whole, by_group(16, ROWS)],
        ),
        out_shape=[narrow, narrow, small, small, jax.ShapeDtypeStruct((GROUPS, 16, ROWS), F32)],
        compiler_params=pltpu.CompilerParams(vmem_limit_bytes=48 << 20),
        name="finish",
    )(core, x, dy, cum, cumt, y, dx, ekeep, ecome, gkeep, gcome, gain, b, c, db, dc)


def totals_kernel(s_ref, g_ref, d_ref, tile_ref, out_ref):
    d = [d_ref[i : i + 1, :] for i in range(4)]
    f = ((s_ref[0] * d[1] + s_ref[1]) * d[2] + s_ref[2]) * d[3] + s_ref[3]
    g = ((g_ref[3] * d[2] + g_ref[2]) * d[1] + g_ref[1]) * d[0] + g_ref[0]
    out_ref[0:16, :, 0:GC] = f.reshape(16, 8, GC)
    out_ref[16:32, :, 0:GC] = g.reshape(16, 8, GC)
    out_ref[:, :, GC:] = jnp.broadcast_to(tile_ref[...][None], (32, 8, 128))


def chain_kernel(flag_ref, p_ref, out_ref):
    backward = flag_ref[0]
    state = [jnp.zeros((8, 128), F32) for _ in range(PAIRS)]
    for s in range(32):
        k = jnp.where(backward == 1, 31 - s, s)
        for t in range(PAIRS):
            columns = slice(128 * t, 128 * t + 128)
            out_ref[k, :, columns] = state[t]
            state[t] = state[t] * p_ref[k, t : t + 1, GC:] + p_ref[k, :, columns]


def entering_kernel(s_ref, g_ref, d_ref, edge_ref, e_ref, l_ref):
    d = [d_ref[i : i + 1, :] for i in range(4)]
    e = edge_ref[0:16].reshape(N, GC)
    for i in range(4):
        e_ref[i] = e
        if i < 3:
            e = e * d[i] + s_ref[i]
    g = edge_ref[16:32].reshape(N, GC)
    for i in (3, 2, 1, 0):
        l_ref[i] = g
        if i > 0:
            g = g * d[i] + g_ref[i]


VMEM = pl.BlockSpec(memory_space=pltpu.VMEM)
SMEM = pl.BlockSpec(memory_space=pltpu.SMEM)
ROOM = pltpu.CompilerParams(vmem_limit_bytes=40 << 20)


def shards(x, dy, b_all, c_all, log_decay, skip_gain):
    ix, iz = lax.axis_index("x"), lax.axis_index("z")
    iy, core = lax.axis_index("y"), lax.axis_index("core")
    core_arr = core.reshape(1).astype(jnp.int32)
    row0 = (2 * iy + core) * ROWS
    b = lax.dynamic_slice_in_dim(b_all, row0, ROWS, 0)
    c = lax.dynamic_slice_in_dim(c_all, row0, ROWS, 0)

    by_row = log_decay.T.reshape(HG, 4, 2, ROWS).transpose(1, 2, 0, 3)
    by_row = jnp.concatenate(
        [
            by_row,
            jnp.broadcast_to(jnp.pad(skip_gain, (0, ROWS - HG)), (4, 2, 1, ROWS)),
            jnp.zeros((4, 2, 5, ROWS), F32),
        ],
        axis=2,
    )
    send = jnp.broadcast_to(by_row[:, None], (4, 2, 2, 16, ROWS)).reshape(GROUPS, 2, 16, ROWS)
    got = lax.all_to_all(send, ("y", "core"), split_axis=0, concat_axis=0, tiled=True)
    gain = jnp.repeat(got[:, 0, HG, :HG], HEAD, axis=1).reshape(GROUPS, 1, GC)
    decays = jnp.where(lax.broadcasted_iota(jnp.int32, got.shape, 2) < HG, got, 0.0)
    own = lax.dynamic_index_in_dim(decays, core, 1, keepdims=False)
    upper = jnp.triu(jnp.ones((ROWS, ROWS), F32))
    cumt = lax.dot_general(
        own, upper, (((2,), (0,)), ((), ())), precision=lax.Precision.HIGHEST
    )
    cum = jnp.swapaxes(cumt, 1, 2)
    both = jnp.sum(decays[:, :, :HG], axis=3).reshape(4, 2, 2, HG)
    both = lax.dynamic_index_in_dim(both, core, 1, keepdims=False)
    kept = jnp.repeat(jnp.exp(both), HEAD, axis=2)[:, :, None, :]
    of_chip = jnp.sum(log_decay.reshape(4, 2 * ROWS, HG), axis=1)
    chip_keep = jnp.repeat(jnp.exp(of_chip), HEAD, axis=1)
    tile = jnp.repeat(jnp.exp(jnp.sum(of_chip, axis=0)), HEAD).reshape(PAIRS, 128)
    tile = jnp.pad(tile, ((0, 8 - PAIRS), (0, 0)))

    s_local, g_local = local_states(core_arr, x, dy, cum, b.T, c.T)
    s_come = lax.ppermute(s_local[0], "core", SWAP)
    g_come = lax.ppermute(g_local[0], "core", SWAP)
    s_mine, g_mine = s_local[1], g_local[1]
    low = core == 0
    s0, s1 = jnp.where(low, s_mine, s_come), jnp.where(low, s_come, s_mine)
    g0, g1 = jnp.where(low, g_mine, g_come), jnp.where(low, g_come, g_mine)
    s_chip = kept[:, 1] * s0 + s1
    g_chip = g0 + kept[:, 0] * g1
    exchange = lambda v: lax.all_to_all(v, "y", split_axis=0, concat_axis=0, tiled=True)
    s_all, g_all = exchange(s_chip), exchange(g_chip)
    y_in, dx_in, db_in, dc_in = within(x, dy, cum, cumt, b, c)

    payload = pl.pallas_call(
        totals_kernel,
        in_specs=[VMEM] * 4,
        out_specs=VMEM,
        out_shape=jax.ShapeDtypeStruct((32, 8, GC + 128), F32),
        compiler_params=ROOM,
        name="group_totals",
    )(s_all, g_all, chip_keep, tile)
    payload = lax.all_to_all(payload, ("x", "z"), split_axis=0, concat_axis=0, tiled=True)
    edges = pl.pallas_call(
        chain_kernel,
        in_specs=[SMEM, VMEM],
        out_specs=VMEM,
        out_shape=jax.ShapeDtypeStruct((32, 8, GC), F32),
        compiler_params=ROOM,
        name="chain",
    )((ix >= 2).reshape(1).astype(jnp.int32), payload)
    edges = lax.all_to_all(edges, ("x", "z"), split_axis=0, concat_axis=0, tiled=True)
    e_all, l_all = pl.pallas_call(
        entering_kernel,
        in_specs=[VMEM] * 4,
        out_specs=[VMEM] * 2,
        out_shape=[jax.ShapeDtypeStruct((4, N, GC), F32)] * 2,
        compiler_params=ROOM,
        name="entering",
    )(s_all, g_all, chip_keep, edges)
    e_chip, l_chip = exchange(e_all), exchange(l_all)
    e_late = kept[:, 0] * e_chip + s0
    l_early = kept[:, 1] * l_chip + g1
    e_keep, e_send = jnp.where(low, e_chip, e_late), jnp.where(low, e_late, e_chip)
    l_keep, l_send = jnp.where(low, l_early, l_chip), jnp.where(low, l_chip, l_early)
    e_come = lax.ppermute(e_send, "core", SWAP)
    l_come = lax.ppermute(l_send, "core", SWAP)
    out, grad_x, db, dc, gd = finish(
        core_arr, x, dy, cum, cumt, y_in, dx_in, e_keep, e_come, l_keep, l_come, gain, b, c, db_in, dc_in
    )

    gd = lax.all_to_all(gd, ("y", "core"), split_axis=0, concat_axis=0, tiled=True)
    grad_decay = gd[:, :HG].transpose(0, 2, 1).reshape(GROUPS * ROWS, HG)
    maps = jnp.concatenate([db, dc], axis=1)
    turns = [maps] + [
        lax.ppermute(maps, "y", [(i, (i - s) % 4) for i in range(4)]) for s in (1, 2, 3)
    ]
    chips = jnp.roll(jnp.stack(turns), iy, axis=0)
    other = lax.ppermute(chips, "core", SWAP)
    whole = jnp.stack(
        [jnp.where(low, chips, other), jnp.where(low, other, chips)], axis=1
    ).reshape(GROUPS * ROWS, 2 * N)
    return out, grad_x, whole[:, :N], whole[:, N:], grad_decay


def solution(mesh):
    grid = Mesh(mesh.devices.reshape(4, 8, 4, 2), ("x", "z", "y", "core"))
    ctx, head = ("x", "z"), ("y", "core")
    rows = P((*ctx, *head), None)
    return jax.shard_map(
        shards,
        mesh=grid,
        in_specs=(rows, rows, P(ctx, None), P(ctx, None), P(ctx, head), P(head)),
        out_specs=(rows, rows, P(ctx, None), P(ctx, None), P(ctx, head)),
        check_vma=False,
    )
```

profile of v0, /device:TPU:33, one launch (start us, length us, event | category | flops | bytes accessed | tf_op | source)
XLA Modules:
  0.0 235.0 jit_solution(3868149472287006339)
XLA Ops:
  0.6 1.0 reshape.46
  1.7 0.7 pad.8
  2.6 0.7 broadcast_in_dim.39
  3.3 5.3 %all-to-all-start = ((f32[8,2,16,192]{3,2,1,0:T(8,128)}), f32[8,2,16,192]{3,2,1,0:T(8,128)S(1)}, u32[]{:S(2)}, u32[]{:S(2)}) async-start(f32[8,2,16,192]{3,2,1,0:T(8,128)} %bitcast.3), calls=%async_computation | async-start | bytes 524288 | tf_op jit(solution)/shard_map/all_to_all | solution.py:313
  8.6 0.8 constant_dynamic-slice_fusion.2
  9.4 0.1 copy.44.bt_ref
  9.5 0.1 copy.45.ct_ref
  9.7 5.4 %all-to-all-done = f32[8,2,16,192]{3,2,1,0:T(8,128)S(1)} async-done(((f32[8,2,16,192]{3,2,1,0:T(8,128)}), f32[8,2,16,192]{3,2,1,0:T(8,128)S(1)}, u32[]{:S(2)}, u32[]{:S(2)}) %all-to-all-start) | async-done | bytes 196640 | tf_op jit(solution)/shard_map/all_to_all | solution.py:313
  15.2 0.6 copy-done.18
  15.8 0.4 fusion.6.cumt_ref
  16.1 0.3 copy.39
  16.4 1.5 copy-done.2
  18.0 8.0 %local_states.1 = (f32[2,4,128,640]{3,2,1,0:T(8,128)S(1)}, f32[2,4,128,640]{3,2,1,0:T(8,128)S(1)}) custom-call(s32[1]{0:T(128)} %bitcast.core, bf16[192,5120]{1,0:T(8,128)(2,1)S(1)} %copy-done, bf16[192,5120]{1,0:T(8,128)(2,1)S(1)} %copy-done.2, f32[8,192,16]{2,1,0:T(8,128)S(1)} %bitcast.77, bf16[128,192]{1,0:T(8,128)(2,1)S(1)} %copy.44.bt_ref, ...), custom_call_target="tpu_custom_call" | custom-call | tf_op jit(solution)/shard_map/local_states/pallas_call | solution.py:72
  26.0 1.5 copy-done.5
  27.6 1.3 slice_bitcast_fusion
  28.8 1.0 collective-permute-start.1
  29.9 0.1 slice_reduce_fusion
  30.0 2.6 %slice_bitcast_fusion.1 = f32[4,128,640]{2,1,0:T(8,128)} fusion(f32[2,4,128,640]{3,2,1,0:T(8,128)} %copy-done.4), kind=kLoop, calls=%fused_computation.14 | loop fusion | bytes 2621440 | tf_op jit(solution)/shard_map/squeeze | solution.py:331
  32.7 0.7 broadcast_in_dim.43
  33.4 1.5 broadcast_in_dim_reshape.3
  34.9 0.8 fusion.18
  35.8 0.6 copy-done.19
  36.3 2.5 %fusion = f32[4,128,640]{2,1,0:T(8,128)} fusion(f32[4,128,640]{2,1,0:T(8,128)} %collective-permute-done.1, f32[2,4,128,640]{3,2,1,0:T(8,128)S(1)} %copy-done.6, f32[4,640]{1,0:T(4,128)S(1)} %bitcast.85, pred[]{:T(512)S(6)} %eq.6), kind=kLoop, calls=%fused_computation.3 | loop fusion | flops 1310720 | bytes 3942401 | tf_op jit(solution)/shard_map/add | solution.py:338
  38.9 3.5 %all-to-all-start.2 = ((f32[4,128,640]{2,1,0:T(8,128)}), f32[4,128,640]{2,1,0:T(8,128)S(1)}, u32[]{:S(2)}, u32[]{:S(2)}) async-start(f32[4,128,640]{2,1,0:T(8,128)} %fusion), calls=%async_computation.2 | async-start | bytes 2621440 | tf_op jit(solution)/shard_map/all_to_all | solution.py:339
  42.5 0.6 copy-done.21
  43.0 2.9 %fusion.1 = f32[4,128,640]{2,1,0:T(8,128)} fusion(f32[4,128,640]{2,1,0:T(8,128)} %collective-permute-done, f32[2,4,128,640]{3,2,1,0:T(8,128)} %copy-done.4, f32[4,640]{1,0:T(4,128)S(1)} %bitcast.87, pred[]{:T(512)S(6)} %eq.6), kind=kLoop, calls=%fused_computation.6 | loop fusion | flops 1310720 | bytes 3942401 | tf_op jit(solution)/shard_map/add | solution.py:337
  46.0 13.9 %all-to-all-done.2.g_ref = f32[4,128,640]{2,1,0:T(8,128)S(1)} async-done(((f32[4,128,640]{2,1,0:T(8,128)}), f32[4,128,640]{2,1,0:T(8,128)S(1)}, u32[]{:S(2)}, u32[]{:S(2)}) %all-to-all-start.2) | async-done | bytes 1310752 | tf_op jit(solution)/shard_map/all_to_all | solution.py:339
  59.9 3.5 %all-to-all-start.1 = ((f32[4,128,640]{2,1,0:T(8,128)}), f32[4,128,640]{2,1,0:T(8,128)S(1)}, u32[]{:S(2)}, u32[]{:S(2)}) async-start(f32[4,128,640]{2,1,0:T(8,128)} %fusion.1), calls=%async_computation.1 | async-start | bytes 2621440 | tf_op jit(solution)/shard_map/all_to_all | solution.py:339
  63.4 1.0 reduce_sum.29
  64.5 1.5 reshape.49
  66.2 0.9 reduce_sum.28
  67.3 0.7 broadcast_in_dim.44
  68.0 0.8 reshape.50.d_ref
  68.8 11.2 %all-to-all-done.1.s_ref = f32[4,128,640]{2,1,0:T(8,128)S(1)} async-done(((f32[4,128,640]{2,1,0:T(8,128)}), f32[4,128,640]{2,1,0:T(8,128)S(1)}, u32[]{:S(2)}, u32[]{:S(2)}) %all-to-all-start.1) | async-done | bytes 1310752 | tf_op jit(solution)/shard_map/all_to_all | solution.py:339
  80.0 0.1 group_totals.1
  80.1 0.9 copy-done.11
  81.0 10.7 %all-to-all-start.3 = ((f32[32,8,768]{2,1,0:T(8,128)}), f32[32,8,768]{2,1,0:T(8,128)}, u32[]{:S(2)}, u32[]{:S(2)}) async-start(f32[32,8,768]{2,1,0:T(8,128)} %copy-done.11), calls=%async_computation.3 | async-start | bytes 1572864 | tf_op jit(solution)/shard_map/all_to_all | solution.py:351
  91.7 19.6 %all-to-all-done.3.p_ref = f32[32,8,768]{2,1,0:T(8,128)} async-done(((f32[32,8,768]{2,1,0:T(8,128)}), f32[32,8,768]{2,1,0:T(8,128)}, u32[]{:S(2)}, u32[]{:S(2)}) %all-to-all-start.3) | async-done | bytes 786464 | tf_op jit(solution)/shard_map/all_to_all | solution.py:351
  111.3 1.2 chain.1
  112.5 22.9 %all_to_all.40.edge_ref = f32[32,8,640]{2,1,0:T(8,128)S(1)} all-to-all(f32[32,8,640]{2,1,0:T(8,128)S(1)} %chain.1), channel_id=1, replica_groups=mesh['x'=4,'z'=8,'y'=4,'core'=2] {'x','z'}, dimensions={0} | all-to-all | bytes 1310720 | tf_op jit(solution)/shard_map/all_to_all | solution.py:360
  135.4 0.3 entering.1
  135.7 16.5 %all_to_all.41 = f32[4,128,640]{2,1,0:T(8,128)} all-to-all(f32[4,128,640]{2,1,0:T(8,128)S(1)} %get-tuple-element.23), channel_id=1, replica_groups=mesh['x'=4,'z'=8,'y'=4,'core'=2] {'y'}, dimensions={0} | all-to-all | bytes 2621440 | tf_op jit(solution)/shard_map/all_to_all | solution.py:339
  152.2 4.6 %all-to-all-start.5 = ((f32[4,128,640]{2,1,0:T(8,128)}), f32[4,128,640]{2,1,0:T(8,128)}, u32[]{:S(2)}, u32[]{:S(2)}) async-start(f32[4,128,640]{2,1,0:T(8,128)} %copy-done.12), calls=%async_computation.5 | async-start | bytes 2621440 | tf_op jit(solution)/shard_map/all_to_all | solution.py:339
  156.8 0.8 slice.49
  157.6 0.7 broadcast_in_dim.47
  158.3 1.5 reshape_reshape.5.gain_ref
  159.8 3.1 %fusion.2 = (f32[4,128,640]{2,1,0:T(8,128)}, f32[4,128,640]{2,1,0:T(8,128)}) fusion(f32[4,128,640]{2,1,0:T(8,128)} %all_to_all.41, f32[4,640]{1,0:T(4,128)} %bitcast.88, pred[]{:T(512)S(6)} %eq.6, f32[4,128,640]{2,1,0:T(8,128)} %collective-permute-done.1, f32[2,4,128,640]{3,2,1,0:T(8,128)S(1)} %copy-done.7), kind=kLoop, calls=%fused_computation.8 | loop fusion | flops 1638400 | bytes 6563841 | tf_op jit(solution)/shard_map/jit(_where)/select_n | solution.py:373
  162.9 6.0 %collective-permute-start.3 = (f32[4,128,640]{2,1,0:T(8,128)}, f32[4,128,640]{2,1,0:T(8,128)}, u32[]{:S(2)}, u32[]{:S(2)}) collective-permute-start(f32[4,128,640]{2,1,0:T(8,128)} %get-tuple-element.31), channel_id=1, source_target_pairs={{0,1},{1,0},{2,3},{3,2},{4,5},{5,4},{6,7},{7,6},{8,9},{9,8},{10,11... | collective-permute-start | bytes 3932168 | tf_op jit(solution)/shard_map/ppermute | solution.py:375
  169.0 2.5 %fusion.4 = (f32[4,128,640]{2,1,0:T(8,128)S(1)}, f32[4,128,640]{2,1,0:T(8,128)S(1)}) fusion(f32[4,128,640]{2,1,0:T(8,128)} %all-to-all-done.5, f32[4,640]{1,0:T(4,128)S(1)} %bitcast.86, pred[]{:T(512)S(6)} %eq.6, f32[4,128,640]{2,1,0:T(8,128)} %collective-permute-done, f32[2,4,128,640]{3,2,1,0:T(8,128)} %copy-done.4), kind=kLoop, calls=%fused_computation.11 | loop fusion | flops 1638400 | bytes 6563841 | tf_op jit(solution)/shard_map/jit(_where)/select_n | solution.py:372
  171.5 6.4 %collective-permute-start.2 = (f32[4,128,640]{2,1,0:T(8,128)S(1)}, f32[4,128,640]{2,1,0:T(8,128)S(1)}, u32[]{:S(2)}, u32[]{:S(2)}) collective-permute-start(f32[4,128,640]{2,1,0:T(8,128)S(1)} %get-tuple-element.33), channel_id=1, source_target_pairs={{0,1},{1,0},{2,3},{3,2},{4,5},{5,4},{6,7},{7,6},{8,9},{9,8},{10,11... | collective-permute-start | bytes 3932168 | tf_op jit(solution)/shard_map/ppermute | solution.py:374
  178.0 11.0 %within_chunk.1 = (f32[192,5120]{1,0:T(8,128)S(1)}, f32[192,5120]{1,0:T(8,128)S(1)}, f32[192,128]{1,0:T(8,128)S(1)}, f32[192,128]{1,0:T(8,128)S(1)}) custom-call(bf16[192,5120]{1,0:T(8,128)(2,1)S(1)} %copy-done.1, bf16[192,5120]{1,0:T(8,128)(2,1)S(1)} %copy-done.3, f32[8,192,16]{2,1,0:T(8,128)S(1)} %bitcast.78, f32[8,16,192]{2,1,0:T(8,128)S(1)} %fusion.6.cumt_ref, ...), custom_call_target="tpu_custom_call" | custom-call | flops 20000000000 | bytes 12000000 | tf_op jit(solution)/shard_map/within_chunk/pallas_call | solution.py:146
  189.0 1.9 copy-done.9
  190.9 1.9 copy-done.10
  192.8 16.9 %finish.1 = (bf16[192,5120]{1,0:T(8,128)(2,1)}, bf16[192,5120]{1,0:T(8,128)(2,1)}, f32[192,128]{1,0:T(8,128)S(1)}, f32[192,128]{1,0:T(8,128)S(1)}, f32[8,16,192]{2,1,0:T(8,128)S(1)}) custom-call(s32[1]{0:T(128)} %bitcast.core, bf16[192,5120]{1,0:T(8,128)(2,1)} %x_ref.5, bf16[192,5120]{1,0:T(8,128)(2,1)} %dy_ref.5, f32[8,192,16]{2,1,0:T(8,128)S(1)} %bitcast.79, ...), custom_call_target="tpu_custom_call" | custom-call | tf_op jit(solution)/shard_map/finish/pallas_call | solution.py:239
  209.7 0.4 collective-permute-start.6
  210.1 1.8 collective-permute-start.5
  211.9 0.9 collective-permute-start.4
  212.8 9.2 %collective-permute-done.4 = f32[192,256]{1,0:T(8,128)S(1)} collective-permute-done((f32[192,256]{1,0:T(8,128)S(1)}, f32[192,256]{1,0:T(8,128)S(1)}, u32[]{:S(2)}, u32[]{:S(2)}) %collective-permute-start.4) | collective-permute-done | bytes 196640 | tf_op jit(solution)/shard_map/ppermute | solution.py:384
  222.2 1.2 collective-permute-start.7
  223.5 9.1 %all_to_all.42 = f32[8,16,192]{2,1,0:T(8,128)S(1)} all-to-all(f32[8,16,192]{2,1,0:T(8,128)S(1)} %get-tuple-element.30), channel_id=1, replica_groups=mesh['x'=4,'z'=8,'y'=4,'core'=2] {'y','core'}, dimensions={0} | all-to-all | bytes 196608 | tf_op jit(solution)/shard_map/all_to_all | solution.py:380
  232.6 0.7 reshape.52
  233.4 0.1 select_bitcast_fusion.1
  233.5 0.1 pad_maximum_fusion
  233.8 1.2 fusion.17
  (80 shorter events, 1.2 us)
Async XLA Ops:
  3.3 13.1 %copy-start = (bf16[192,5120]{1,0:T(8,128)(2,1)S(1)}, bf16[192,5120]{1,0:T(8,128)(2,1)}, u32[]{:S(2)}) copy-start(bf16[192,5120]{1,0:T(8,128)(2,1)} %x_ref.5) | copy-start | bytes 5898244
  3.3 11.8 %all-to-all-start = ((f32[8,2,16,192]{3,2,1,0:T(8,128)}), f32[8,2,16,192]{3,2,1,0:T(8,128)S(1)}, u32[]{:S(2)}, u32[]{:S(2)}) async-start(f32[8,2,16,192]{3,2,1,0:T(8,128)} %bitcast.3), calls=%async_computation | async-start | bytes 524288 | tf_op jit(solution)/shard_map/all_to_all | solution.py:313
  9.4 5.8 %copy-start.13 = (bf16[192,128]{1,0:T(8,128)(2,1)}, bf16[192,128]{1,0:T(8,128)(2,1)S(1)}, u32[]{:S(2)}) copy-start(bf16[192,128]{1,0:T(8,128)(2,1)S(1)} %get-tuple-element.41.c_ref) | copy-start | bytes 147460
  9.4 5.8 %copy-start.15 = (bf16[192,128]{1,0:T(8,128)(2,1)}, bf16[192,128]{1,0:T(8,128)(2,1)S(1)}, u32[]{:S(2)}) copy-start(bf16[192,128]{1,0:T(8,128)(2,1)S(1)} %get-tuple-element.42.b_ref) | copy-start | bytes 147460
  15.1 0.7 copy-start.18
  16.4 1.5 copy-start.2
  26.0 1.5 copy-start.5
  26.0 2.8 %copy-start.4 = (f32[2,4,128,640]{3,2,1,0:T(8,128)}, f32[2,4,128,640]{3,2,1,0:T(8,128)S(1)}, u32[]{:S(2)}) copy-start(f32[2,4,128,640]{3,2,1,0:T(8,128)S(1)} %get-tuple-element.20) | copy-start | bytes 7864324
  28.8 6.9 %collective-permute-start.1 = (f32[4,128,640]{2,1,0:T(8,128)}, f32[4,128,640]{2,1,0:T(8,128)}, u32[]{:S(2)}, u32[]{:S(2)}) collective-permute-start(f32[4,128,640]{2,1,0:T(8,128)} %slice_bitcast_fusion), channel_id=1, source_target_pairs={{0,1},{1,0},{2,3},{3,2},{4,5},{5,4},{6,7},{7,6},{8,9},{9,8},{10,11... | collective-permute-start | bytes 3932168 | tf_op jit(solution)/shard_map/ppermute | solution.py:332
  30.0 6.3 %copy-start.6 = (f32[2,4,128,640]{3,2,1,0:T(8,128)S(1)}, f32[2,4,128,640]{3,2,1,0:T(8,128)}, u32[]{:S(2)}) copy-start(f32[2,4,128,640]{3,2,1,0:T(8,128)} %copy-done.5) | copy-start | bytes 7864324
  32.6 9.8 %collective-permute-start = (f32[4,128,640]{2,1,0:T(8,128)}, f32[4,128,640]{2,1,0:T(8,128)}, u32[]{:S(2)}, u32[]{:S(2)}) collective-permute-start(f32[4,128,640]{2,1,0:T(8,128)} %slice_bitcast_fusion.1), channel_id=1, source_target_pairs={{0,1},{1,0},{2,3},{3,2},{4,5},{5,4},{6,7},{7,6},{8,9},{9,8},{10,11... | collective-permute-start | bytes 3932168 | tf_op jit(solution)/shard_map/ppermute | solution.py:331
  35.7 0.6 copy-start.19
  38.9 21.0 %all-to-all-start.2 = ((f32[4,128,640]{2,1,0:T(8,128)}), f32[4,128,640]{2,1,0:T(8,128)S(1)}, u32[]{:S(2)}, u32[]{:S(2)}) async-start(f32[4,128,640]{2,1,0:T(8,128)} %fusion), calls=%async_computation.2 | async-start | bytes 2621440 | tf_op jit(solution)/shard_map/all_to_all | solution.py:339
  42.4 0.6 copy-start.21
  59.9 20.1 %all-to-all-start.1 = ((f32[4,128,640]{2,1,0:T(8,128)}), f32[4,128,640]{2,1,0:T(8,128)S(1)}, u32[]{:S(2)}, u32[]{:S(2)}) async-start(f32[4,128,640]{2,1,0:T(8,128)} %fusion.1), calls=%async_computation.1 | async-start | bytes 2621440 | tf_op jit(solution)/shard_map/all_to_all | solution.py:339
  80.1 0.9 copy-start.11
  81.0 30.3 %all-to-all-start.3 = ((f32[32,8,768]{2,1,0:T(8,128)}), f32[32,8,768]{2,1,0:T(8,128)}, u32[]{:S(2)}, u32[]{:S(2)}) async-start(f32[32,8,768]{2,1,0:T(8,128)} %copy-done.11), calls=%async_computation.3 | async-start | bytes 1572864 | tf_op jit(solution)/shard_map/all_to_all | solution.py:351
  135.7 16.5 %copy-start.12 = (f32[4,128,640]{2,1,0:T(8,128)}, f32[4,128,640]{2,1,0:T(8,128)S(1)}, u32[]{:S(2)}) copy-start(f32[4,128,640]{2,1,0:T(8,128)S(1)} %get-tuple-element.22) | copy-start | bytes 3932164
  152.2 7.6 %copy-start.7 = (f32[2,4,128,640]{3,2,1,0:T(8,128)S(1)}, f32[2,4,128,640]{3,2,1,0:T(8,128)}, u32[]{:S(2)}) copy-start(f32[2,4,128,640]{3,2,1,0:T(8,128)} %copy-done.5) | copy-start | bytes 7864324
  152.2 16.7 %all-to-all-start.5 = ((f32[4,128,640]{2,1,0:T(8,128)}), f32[4,128,640]{2,1,0:T(8,128)}, u32[]{:S(2)}, u32[]{:S(2)}) async-start(f32[4,128,640]{2,1,0:T(8,128)} %copy-done.12), calls=%async_computation.5 | async-start | bytes 2621440 | tf_op jit(solution)/shard_map/all_to_all | solution.py:339
  159.8 9.1 %copy-start.20 = (f32[4,1,1,640]{3,0,1,2:T(4,128)S(1)}, f32[4,1,1,640]{3,0,1,2:T(4,128)}, u32[]{:S(2)}) copy-start(f32[4,1,1,640]{3,0,1,2:T(4,128)} %copy-done.19) | copy-start | bytes 30724
  162.9 15.1 %copy-start.1 = (bf16[192,5120]{1,0:T(8,128)(2,1)S(1)}, bf16[192,5120]{1,0:T(8,128)(2,1)}, u32[]{:S(2)}) copy-start(bf16[192,5120]{1,0:T(8,128)(2,1)} %x_ref.5) | copy-start | bytes 5898244
  162.9 15.1 %copy-start.14 = (bf16[192,128]{1,0:T(8,128)(2,1)S(1)}, bf16[192,128]{1,0:T(8,128)(2,1)}, u32[]{:S(2)}) copy-start(bf16[192,128]{1,0:T(8,128)(2,1)} %copy-done.13) | copy-start | bytes 147460
  162.9 15.1 %copy-start.16 = (bf16[192,128]{1,0:T(8,128)(2,1)S(1)}, bf16[192,128]{1,0:T(8,128)(2,1)}, u32[]{:S(2)}) copy-start(bf16[192,128]{1,0:T(8,128)(2,1)} %copy-done.15) | copy-start | bytes 147460
  162.9 29.9 %collective-permute-start.3 = (f32[4,128,640]{2,1,0:T(8,128)}, f32[4,128,640]{2,1,0:T(8,128)}, u32[]{:S(2)}, u32[]{:S(2)}) collective-permute-start(f32[4,128,640]{2,1,0:T(8,128)} %get-tuple-element.31), channel_id=1, source_target_pairs={{0,1},{1,0},{2,3},{3,2},{4,5},{5,4},{6,7},{7,6},{8,9},{9,8},{10,11... | collective-permute-start | bytes 3932168 | tf_op jit(solution)/shard_map/ppermute | solution.py:375
  169.0 9.0 %copy-start.3 = (bf16[192,5120]{1,0:T(8,128)(2,1)S(1)}, bf16[192,5120]{1,0:T(8,128)(2,1)}, u32[]{:S(2)}) copy-start(bf16[192,5120]{1,0:T(8,128)(2,1)} %dy_ref.5) | copy-start | bytes 5898244
  171.5 21.3 %copy-start.8 = (f32[4,128,640]{2,1,0:T(8,128)S(1)}, f32[4,128,640]{2,1,0:T(8,128)}, u32[]{:S(2)}) copy-start(f32[4,128,640]{2,1,0:T(8,128)} %get-tuple-element.32.gkeep_ref) | copy-start | bytes 3932164
  171.5 21.3 %copy-start.17 = (f32[8,1,640]{2,1,0:T(1,128)S(1)}, f32[8,1,640]{2,1,0:T(1,128)}, u32[]{:S(2)}) copy-start(f32[8,1,640]{2,1,0:T(1,128)} %reshape_reshape.5.gain_ref) | copy-start | bytes 61444
  171.5 21.3 %collective-permute-start.2 = (f32[4,128,640]{2,1,0:T(8,128)S(1)}, f32[4,128,640]{2,1,0:T(8,128)S(1)}, u32[]{:S(2)}, u32[]{:S(2)}) collective-permute-start(f32[4,128,640]{2,1,0:T(8,128)S(1)} %get-tuple-element.33), channel_id=1, source_target_pairs={{0,1},{1,0},{2,3},{3,2},{4,5},{5,4},{6,7},{7,6},{8,9},{9,8},{10,11... | collective-permute-start | bytes 3932168 | tf_op jit(solution)/shard_map/ppermute | solution.py:374
  189.0 1.9 copy-start.9
  190.9 1.9 copy-start.10
  209.7 12.3 %collective-permute-start.6 = (f32[192,256]{1,0:T(8,128)S(1)}, f32[192,256]{1,0:T(8,128)S(1)}, u32[]{:S(2)}, u32[]{:S(2)}) collective-permute-start(f32[192,256]{1,0:T(8,128)S(1)} %constant_dynamic-update-slice_fusion), channel_id=1, source_target_pairs={{0,2},{2,4},{4,6},{6,0},{1,3},{3,5},{5,7},{7,1},{8,10},{10,12},{12... | collective-permute-start | bytes 589832 | tf_op jit(solution)/shard_map/ppermute | solution.py:384
  210.1 11.9 %collective-permute-start.5 = (f32[192,256]{1,0:T(8,128)S(1)}, f32[192,256]{1,0:T(8,128)S(1)}, u32[]{:S(2)}, u32[]{:S(2)}) collective-permute-start(f32[192,256]{1,0:T(8,128)S(1)} %constant_dynamic-update-slice_fusion), channel_id=1, source_target_pairs={{0,4},{2,6},{4,0},{6,2},{1,5},{3,7},{5,1},{7,3},{8,12},{10,14},{12... | collective-permute-start | bytes 589832 | tf_op jit(solution)/shard_map/ppermute | solution.py:384
  211.9 10.1 %collective-permute-start.4 = (f32[192,256]{1,0:T(8,128)S(1)}, f32[192,256]{1,0:T(8,128)S(1)}, u32[]{:S(2)}, u32[]{:S(2)}) collective-permute-start(f32[192,256]{1,0:T(8,128)S(1)} %constant_dynamic-update-slice_fusion), channel_id=1, source_target_pairs={{0,6},{2,0},{4,2},{6,4},{1,7},{3,1},{5,3},{7,5},{8,14},{10,8},{12,... | collective-permute-start | bytes 589832 | tf_op jit(solution)/shard_map/ppermute | solution.py:384
  222.2 11.1 %collective-permute-start.7 = (f32[4,192,256]{2,1,0:T(8,128)S(1)}, f32[4,192,256]{2,1,0:T(8,128)S(1)}, u32[]{:S(2)}, u32[]{:S(2)}) collective-permute-start(f32[4,192,256]{2,1,0:T(8,128)S(1)} %constant_dynamic-slice_fusion), channel_id=1, source_target_pairs={{0,1},{1,0},{2,3},{3,2},{4,5},{5,4},{6,7},{7,6},{8,9},{9,8},{10,11... | collective-permute-start | bytes 2359304 | tf_op jit(solution)/shard_map/ppermute | solution.py:387
where the time goes:
time: 237 us; the launch traced here: 235 us
  waiting for transfers between devices  59.4 us (25%)
  blocking collectives  48.5 us (20%)
  starting transfers between devices  45.4 us (19%)
  Pallas kernels  37.6 us (16%)
  local copies, waits for them, and re-layouts  29 us (12%)
  other arithmetic  13.6 us (6%)
    all_to_all x3, waiting for transfers between devices, shards(): lax.all_to_all(v, 'y', split_axis=0, concat_axis=0, tiled=True)  25.1 us
    all_to_all x1, blocking collectives, shards(): lax.all_to_all(edges, ('x', 'z'), split_axis=0, concat_axis=0, tiled=True)  22.9 us
    all_to_all x1, waiting for transfers between devices, shards(): lax.all_to_all(payload, ('x', 'z'), split_axis=0, concat_axis=0, tiled=True)  19.6 us
    pallas_call x1, Pallas kernels, finish(): pl.pallas_call(finish_kernel, grid_spec=pltpu.PrefetchScalarGridSpec(num_...  16.9 us
    all_to_all x1, blocking collectives, shards(): lax.all_to_all(v, 'y', split_axis=0, concat_axis=0, tiled=True)  16.5 us
    all_to_all x3, starting transfers between devices, shards(): lax.all_to_all(v, 'y', split_axis=0, concat_axis=0, tiled=True)  11.7 us
    pallas_call x1, Pallas kernels, within(): pl.pallas_call(within_kernel, grid=(GROUPS,), in_specs=[by_column, by_col...  11 us
    all_to_all x1, starting transfers between devices, shards(): lax.all_to_all(payload, ('x', 'z'), split_axis=0, concat_axis=0, tiled=True)  10.7 us
  transfers between devices with their start and end apart: 13, of which 5 were waited for; matrix products, arithmetic and copies ran while one was open for 12% of the time, Pallas kernels for 5%

commit v1 on v0

v1 whole, which is shorter than its diff:
```python
import functools

import jax
import jax.numpy as jnp
from jax import lax
from jax.experimental import pallas as pl
from jax.experimental.pallas import tpu as pltpu
from jax.sharding import Mesh
from jax.sharding import PartitionSpec as P

ROWS = 192
N = 128
HEAD = 64
HG = 10
GC = HG * HEAD
GROUPS = 8
PAIRS = GC // 128
F32, BF16 = jnp.float32, jnp.bfloat16
SWAP = [(0, 1), (1, 0)]
NN = (((1,), (0,)), ((), ()))
NT = (((1,), (1,)), ((), ()))
TN = (((0,), (0,)), ((), ()))


def dot(a, b, dims=NN):
    return lax.dot_general(a, b, dims, preferred_element_type=F32)


def halves(v):
    high = v.astype(BF16)
    return high, (v - high.astype(F32)).astype(BF16)


def thirds(v):
    high = v.astype(BF16)
    rest = v - high.astype(F32)
    middle = rest.astype(BF16)
    return high, middle, (rest - middle.astype(F32)).astype(BF16)


def spread(columns):
    rows = columns.shape[0]
    first = lax.broadcasted_iota(jnp.int32, (rows, 128), 1) < HEAD
    return jnp.concatenate(
        [
            jnp.where(
                first,
                jnp.broadcast_to(columns[:, 2 * p : 2 * p + 1], (rows, 128)),
                jnp.broadcast_to(columns[:, 2 * p + 1 : 2 * p + 2], (rows, 128)),
            )
            for p in range(PAIRS)
        ],
        axis=1,
    )


def within_kernel(
    x_ref, dy_ref, cum_ref, cumt_ref, b_ref, c_ref, y_ref, dx_ref, db_ref, dc_ref, score_ref, acc_ref
):
    step = pl.program_id(0)
    causal = lax.broadcasted_iota(jnp.int32, (ROWS, ROWS), 0) >= lax.broadcasted_iota(
        jnp.int32, (ROWS, ROWS), 1
    )

    @pl.when(step == 0)
    def _():
        score_ref[...] = jnp.where(causal, dot(c_ref[...], b_ref[...], NT), 0.0)
        acc_ref[...] = jnp.zeros_like(acc_ref)

    first = lax.broadcasted_iota(jnp.int32, (ROWS, 128), 1) < HEAD
    zero = jnp.zeros((ROWS, 128), BF16)
    for p in range(PAIRS):
        columns = slice(128 * p, 128 * p + 128)
        x = x_ref[:, columns]
        dy = dy_ref[:, columns]
        y = dx = None
        for side in range(2):
            h = 2 * p + side
            keep = first if side == 0 else jnp.logical_not(first)
            xs = jnp.where(keep, x, zero)
            dys = jnp.where(keep, dy, zero)
            decay = jnp.exp(
                jnp.minimum(cum_ref[0, :, h : h + 1] - cumt_ref[0, h : h + 1, :], 0.0)
            )
            weights = (score_ref[...] * decay).astype(BF16)
            part = dot(weights, xs)
            y = part if y is None else y + part
            dweights = dot(dys, x, NT).astype(BF16).astype(F32)
            acc_ref[...] += dweights * decay
            part = dot(weights, dys, TN)
            dx = part if dx is None else dx + part
        y_ref[:, columns] = y
        dx_ref[:, columns] = dx

    @pl.when(step == GROUPS - 1)
    def _():
        high, low = halves(jnp.where(causal, acc_ref[...], 0.0))
        b, c = b_ref[...], c_ref[...]
        dc_ref[...] = dot(high, b) + dot(low, b)
        db_ref[...] = dot(high, c, TN) + dot(low, c, TN)


def within(x, dy, cum, cumt, b, c):
    by_column = pl.BlockSpec((ROWS, GC), lambda s: (0, s))
    whole = pl.BlockSpec((ROWS, N), lambda s: (0, 0))
    wide = jax.ShapeDtypeStruct((ROWS, GC * GROUPS), F32)
    small = jax.ShapeDtypeStruct((ROWS, N), F32)
    return pl.pallas_call(
        within_kernel,
        grid=(GROUPS,),
        in_specs=[
            by_column,
            by_column,
            pl.BlockSpec((1, ROWS, 16), lambda s: (s, 0, 0)),
            pl.BlockSpec((1, 16, ROWS), lambda s: (s, 0, 0)),
            whole,
            whole,
        ],
        out_specs=[by_column, by_column, whole, whole],
        out_shape=[wide, wide, small, small],
        scratch_shapes=[pltpu.VMEM((ROWS, ROWS), F32), pltpu.VMEM((ROWS, ROWS), F32)],
        compiler_params=pltpu.CompilerParams(vmem_limit_bytes=40 << 20),
        cost_estimate=pl.CostEstimate(
            flops=20_000_000_000, bytes_accessed=12_000_000, transcendentals=3_000_000
        ),
        name="within_chunk",
    )(x, dy, cum, cumt, b, c)


CHIPS = 4
VMEM = pl.BlockSpec(memory_space=pltpu.VMEM)
SMEM = pl.BlockSpec(memory_space=pltpu.SMEM)
PAIR = (2, N, GC)
RETURN = F32


def on_chip(kernel, name, outs, *args, scratch=(), scalars=1):
    return pl.pallas_call(
        kernel,
        in_specs=[SMEM] * scalars + [VMEM] * (len(args) - scalars),
        out_specs=[VMEM] * len(outs),
        out_shape=outs,
        scratch_shapes=list(scratch),
        compiler_params=pltpu.CompilerParams(vmem_limit_bytes=44 << 20),
        name=name,
    )(*args)


def pack_kernel(ld_ref, gain_ref, out_ref):
    out_ref[...] = jnp.zeros_like(out_ref)
    for chunk in range(GROUPS):
        rows = ld_ref[:, chunk * ROWS : (chunk + 1) * ROWS]
        for core in range(2):
            at = 2 * (chunk // 2) + core
            out_ref[at, chunk % 2, 0:HG, :] = rows
            out_ref[at, chunk % 2, HG : HG + 1, 0:HG] = gain_ref[...]


def owner_kernel(ld_ref, out_ref):
    width = 2 * ROWS
    of = lax.broadcasted_iota(jnp.int32, (8, 8 * ROWS), 1) // width
    row = lax.broadcasted_iota(jnp.int32, (8, 8 * ROWS), 0)
    pick = jnp.logical_or(of == row, row == CHIPS).astype(BF16)
    totals = sum(dot(pick, part, NT) for part in thirds(ld_ref[...]))
    out_ref[...] = spread(jnp.exp(totals))


def decays_kernel(core_ref, got_ref, cumt_ref, cum_ref, gain_ref, kept_ref):
    low = core_ref[0] == 0
    t = lax.broadcasted_iota(jnp.int32, (ROWS, ROWS), 0)
    s = lax.broadcasted_iota(jnp.int32, (ROWS, ROWS), 1)
    upper = (t <= s).astype(BF16)
    lower = (t >= s).astype(BF16)
    is_head = lax.broadcasted_iota(jnp.int32, (GROUPS, 16, ROWS), 1) < HG
    flat, tall = [], []
    for half in range(2):
        ld = jnp.where(is_head, got_ref[:, half], 0.0).reshape(GROUPS * 16, ROWS)
        parts = thirds(ld)
        flat.append(sum(dot(part, upper) for part in parts))
        tall.append(sum(dot(lower, part, NT) for part in parts))
    cumt_ref[...] = jnp.where(low, flat[0], flat[1]).reshape(GROUPS, 16, ROWS)
    own = jnp.where(low, tall[0], tall[1])
    for g in range(GROUPS):
        cum_ref[g] = own[:, 16 * g : 16 * g + 16]
        gain_ref[g] = spread(got_ref[g, 0, HG : HG + 1, :])
    for half in range(2):
        ends = jnp.exp(tall[half][ROWS - 1 : ROWS, :])
        for j in range(CHIPS):
            a = ends[:, 32 * j : 32 * j + 16]
            b = ends[:, 32 * j + 16 : 32 * j + 32]
            kept_ref[half, j] = spread(jnp.where(low, a, b))


def states_kernel(place, x_ref, dy_ref, cum_ref, bt_ref, ct_ref, send_ref, keep_ref):
    low = place[0] == 0
    for way, (v_ref, m_ref) in enumerate(((x_ref, bt_ref), (dy_ref, ct_ref))):
        m = m_ref[...]
        states = []
        for k in range(2):
            cum = cum_ref[k]
            scale = jnp.exp(cum[ROWS - 1 : ROWS, :] - cum if way == 0 else cum)
            high, low_part = halves(v_ref[:, k * GC : (k + 1) * GC].astype(F32) * spread(scale))
            states.append(dot(m, high) + dot(m, low_part))
        keep_ref[0, way] = jnp.where(low, states[0], states[1])
        send_ref[0, way] = jnp.where(low, states[1], states[0])


def chunk_states(place, x, dy, cum, bt, ct):
    columns = pl.BlockSpec((ROWS, 2 * GC), lambda s, place: (0, s))
    whole = pl.BlockSpec((N, ROWS), lambda s, place: (0, 0))
    quad = pl.BlockSpec((1, *PAIR), lambda s, place: (s, 0, 0, 0))
    return pl.pallas_call(
        states_kernel,
        grid_spec=pltpu.PrefetchScalarGridSpec(
            num_scalar_prefetch=1,
            grid=(CHIPS,),
            in_specs=[
                columns,
                columns,
                pl.BlockSpec((2, ROWS, 16), lambda s, place: (s, 0, 0)),
                whole,
                whole,
            ],
            out_specs=[quad, quad],
        ),
        out_shape=[jax.ShapeDtypeStruct((CHIPS, *PAIR), F32)] * 2,
        compiler_params=pltpu.CompilerParams(vmem_limit_bytes=60 << 20),
        name="chunk_states",
    )(place, x, dy, cum, bt, ct)


def join_kernel(place_ref, keep_ref, come_ref, kept_ref, *outs):
    low = place_ref[0] == 0
    for turn, out in enumerate(outs):
        j = lax.rem(place_ref[1] + turn, CHIPS)
        for way in range(2):
            scaled = low if way == 0 else jnp.logical_not(low)
            keep, come = keep_ref[j, way], come_ref[j, way]
            out[way] = jnp.where(scaled, keep, come) * kept_ref[1 - way, j] + jnp.where(
                scaled, come, keep
            )


ORDERS = ((0, 1, 2, 3), (3, 2, 1, 0))


def totals_kernel(place_ref, r0, r1, r2, r3, d_ref, out_ref, sorted_ref):
    for turn, ref in enumerate((r0, r1, r2, r3)):
        sorted_ref[lax.rem(place_ref[1] - turn + CHIPS, CHIPS)] = ref[...]
    for way, order in enumerate(ORDERS):
        total = sorted_ref[order[0], way]
        for c in order[1:]:
            total = total * d_ref[c : c + 1, :] + sorted_ref[c, way]
        out_ref[16 * way : 16 * way + 16, :, :GC] = total.reshape(16, 8, GC)
    for tile in range(PAIRS):
        row = d_ref[CHIPS : CHIPS + 1, 128 * tile : 128 * tile + 128]
        out_ref[:, tile : tile + 1, GC:] = jnp.broadcast_to(row[None], (32, 1, 128))
    out_ref[:, PAIRS:, GC:] = jnp.zeros((32, 8 - PAIRS, 128), F32)


def chain_kernel(flag_ref, p_ref, out_ref):
    backward = flag_ref[0] == 1
    state = [jnp.zeros((8, 128), F32) for _ in range(PAIRS)]
    for s in range(32):
        k = jnp.where(backward, 31 - s, s)
        for t in range(PAIRS):
            columns = slice(128 * t, 128 * t + 128)
            out_ref[k, :, columns] = state[t]
            state[t] = state[t] * p_ref[k, t : t + 1, GC:] + p_ref[k, :, columns]


def entering_kernel(place_ref, sorted_ref, d_ref, edge_ref, o0, o1, o2, o3, all_ref):
    for way, order in enumerate(ORDERS):
        e = edge_ref[16 * way : 16 * way + 16].reshape(N, GC)
        for c in order:
            all_ref[c, way] = e
            if c != order[-1]:
                e = e * d_ref[c : c + 1, :] + sorted_ref[c, way]
    for turn, out in enumerate((o0, o1, o2, o3)):
        out[...] = all_ref[lax.rem(place_ref[1] + turn, CHIPS)].astype(RETURN)


def fork_kernel(place_ref, r0, r1, r2, r3, keep_ref, come_ref, kept_ref, mine_ref, send_ref):
    low = place_ref[0] == 0
    for turn, ref in enumerate((r0, r1, r2, r3)):
        j = lax.rem(place_ref[1] - turn + CHIPS, CHIPS)
        for way in range(2):
            direct_is_mine = low if way == 0 else jnp.logical_not(low)
            direct = ref[way].astype(F32)
            passed = jnp.where(direct_is_mine, keep_ref[j, way], come_ref[j, way])
            through = kept_ref[way, j] * direct + passed
            mine_ref[j, way] = jnp.where(direct_is_mine, direct, through)
            send_ref[j, way] = jnp.where(direct_is_mine, through, direct)


def finish_kernel(
    place, x_ref, dy_ref, cum_ref, cumt_ref, y_ref, dx_ref, mine_ref, come_ref, gain_ref, b_ref, c_ref,
    db0_ref, dc0_ref, out_ref, gs_ref, o0, o1, o2, o3, db_ref, dc_ref, gd_ref,
):
    step = pl.program_id(0)
    low_core = place[0] == 0

    @pl.when(step == 0)
    def _():
        db_ref[...] = db0_ref[...]
        dc_ref[...] = dc0_ref[...]

    def both(way):
        mine, come = mine_ref[0, way], come_ref[0, way]
        return jnp.concatenate([jnp.where(low_core, mine, come), jnp.where(low_core, come, mine)], axis=1)

    cums = cum_ref[0], cum_ref[1]
    from_start = jnp.concatenate([spread(jnp.exp(v)) for v in cums], axis=1)
    to_end = jnp.concatenate([spread(jnp.exp(v[ROWS - 1 : ROWS, :] - v)) for v in cums], axis=1)
    gain = jnp.concatenate([gain_ref[0], gain_ref[1]], axis=1)
    x = x_ref[...].astype(F32)
    dy = dy_ref[...].astype(F32)
    entering, leaving = both(0), both(1)
    b, c = b_ref[...], c_ref[...]

    def carried(matrix, state, scale, v):
        parts = jnp.concatenate(halves(state), axis=0)
        product = scale * dot(jnp.concatenate([matrix, matrix], axis=1), parts)
        high, low = halves(scale * v)
        wide = dot(high, parts, NT)
        return product, wide[:, :N] + wide[:, N:] + dot(low, parts[:N], NT)

    y_carried, dc = carried(c, entering, from_start, dy)
    dx_carried, db = carried(b, leaving, to_end, x)
    y = y_ref[...] + y_carried
    dx_in = dx_ref[...]
    out_ref[...] = (y + gain * x).astype(BF16)
    gs_ref[...] = (dx_in + dx_carried + gain * dy).astype(BF16)
    dc_ref[...] += dc
    db_ref[...] += db
    of_head = (
        lax.broadcasted_iota(jnp.int32, (32, 2 * GC), 1) // GC * 16
        + lax.broadcasted_iota(jnp.int32, (32, 2 * GC), 1) % GC // HEAD
        == lax.broadcasted_iota(jnp.int32, (32, 2 * GC), 0)
    ).astype(BF16)

    def by_head(v):
        high, low = halves(v)
        return dot(of_head, high, NT) + dot(of_head, low, NT)

    product = jnp.sum(entering * leaving, axis=0, keepdims=True)
    across = by_head(jnp.broadcast_to(product, (8, 2 * GC)))[:, 0:1]
    t = lax.broadcasted_iota(jnp.int32, (ROWS, ROWS), 0)
    s = lax.broadcasted_iota(jnp.int32, (ROWS, ROWS), 1)
    after = (t >= s).astype(BF16)
    before = (t < s).astype(BF16)
    gd = across * jnp.exp(cumt_ref[...].reshape(32, ROWS)[:, ROWS - 1 : ROWS])
    for part in thirds(by_head(dy * y - x * dx_in)):
        gd += dot(part, after)
    for part in thirds(by_head(x * dx_carried)):
        gd += dot(part, before)
    gd_ref[step] = gd

    @pl.when(step == CHIPS - 1)
    def _():
        for turn, out in enumerate((o0, o1, o2, o3)):
            out[0:ROWS, :] = db_ref[...]
            out[ROWS : 2 * ROWS, :] = dc_ref[...]
            mine = gd_ref[lax.rem(place[1] + turn, CHIPS)]
            out[384:416, :] = mine[:, 0:128]
            out[416:448, 0:64] = mine[:, 128:192]
            out[416:448, 64:128] = jnp.zeros((32, 64), F32)


def finish(place, x, dy, cum, cumt, y, dx, mine, come, gain, b, c, db, dc):
    columns = pl.BlockSpec((ROWS, 2 * GC), lambda s, place: (0, s))
    by_chip = lambda *shape: pl.BlockSpec((2, *shape), lambda s, place: (s, 0, 0))
    quad = pl.BlockSpec((1, *PAIR), lambda s, place: (s, 0, 0, 0))
    whole = lambda *shape: pl.BlockSpec(shape, lambda s, place: (0, 0))
    wide = jax.ShapeDtypeStruct((ROWS, GC * GROUPS), BF16)
    return pl.pallas_call(
        finish_kernel,
        grid_spec=pltpu.PrefetchScalarGridSpec(
            num_scalar_prefetch=1,
            grid=(CHIPS,),
            in_specs=[
                columns, columns, by_chip(ROWS, 16), by_chip(16, ROWS), columns, columns, quad, quad,
                by_chip(1, GC), *[whole(ROWS, N)] * 4,
            ],
            out_specs=[columns, columns] + [whole(448, 128)] * 4,
            scratch_shapes=[
                pltpu.VMEM((ROWS, N), F32), pltpu.VMEM((ROWS, N), F32), pltpu.VMEM((CHIPS, 32, ROWS), F32),
            ],
        ),
        out_shape=[wide, wide] + [jax.ShapeDtypeStruct((448, 128), F32)] * 4,
        compiler_params=pltpu.CompilerParams(vmem_limit_bytes=60 << 20),
        name="finish",
    )(place, x, dy, cum, cumt, y, dx, mine, come, gain, b, c, db, dc)


def tie(*values):
    return lax.optimization_barrier(values)


def turned(v):
    r = {
        turn: lax.ppermute(v[turn], "y", [(i, (i + turn) % CHIPS) for i in range(CHIPS)])
        for turn in (2, 1, 3)
    }
    return [v[0], r[1], r[2], r[3]]


def gathered(parts, iy, low):
    by_chip = jnp.roll(jnp.stack([parts[0], parts[3], parts[2], parts[1]]), iy, axis=0)
    other = lax.ppermute(by_chip, "core", SWAP)
    return jnp.stack(
        [jnp.where(low, by_chip, other), jnp.where(low, other, by_chip)], axis=1
    ).reshape(GROUPS, *by_chip.shape[1:])


def shards(x, dy, b_all, c_all, log_decay, skip_gain):
    ix = lax.axis_index("x")
    iy, core = lax.axis_index("y"), lax.axis_index("core")
    place = jnp.stack([core, iy]).astype(jnp.int32)
    row0 = (2 * iy + core) * ROWS
    b = lax.dynamic_slice_in_dim(b_all, row0, ROWS, 0)
    c = lax.dynamic_slice_in_dim(c_all, row0, ROWS, 0)
    swap = lambda v: lax.ppermute(v, "core", SWAP)
    over_ctx = lambda v: lax.all_to_all(v, ("x", "z"), split_axis=0, concat_axis=0, tiled=True)
    pair = lambda dtype: jax.ShapeDtypeStruct(PAIR, dtype)
    quad = jax.ShapeDtypeStruct((CHIPS, *PAIR), F32)

    ldt = log_decay.T
    [packed] = on_chip(
        pack_kernel, "pack", [jax.ShapeDtypeStruct((GROUPS, 2, 16, ROWS), F32)],
        ldt, skip_gain.reshape(1, HG), scalars=0,
    )
    got = lax.all_to_all(packed, ("y", "core"), split_axis=0, concat_axis=0, tiled=True)
    cumt, cum, gain, kept = on_chip(
        decays_kernel, "decays",
        [
            jax.ShapeDtypeStruct((GROUPS, 16, ROWS), F32),
            jax.ShapeDtypeStruct((GROUPS, ROWS, 16), F32),
            jax.ShapeDtypeStruct((GROUPS, 1, GC), F32),
            jax.ShapeDtypeStruct((2, CHIPS, 1, GC), F32),
        ],
        place, got,
    )
    send, keep = chunk_states(place, x, dy, cum, b.T, c.T)
    come = swap(send)
    out = on_chip(join_kernel, "join", [pair(F32)] * 4, place, keep, come, kept)
    parts = turned(out)
    x_w, dy_w, ldt_w, _ = tie(x, dy, ldt, out[0])
    [own] = on_chip(owner_kernel, "owner_decays", [jax.ShapeDtypeStruct((8, GC), F32)], ldt_w, scalars=0)
    inside = within(x_w, dy_w, cum, cumt, b, c)
    y_in, dx_in, db_in, dc_in, *parts = tie(*inside, *parts)
    total, by_chip = on_chip(
        totals_kernel, "totals", [jax.ShapeDtypeStruct((32, 8, GC + 128), F32), quad], place, *parts, own
    )
    total = over_ctx(total)
    flag = (ix >= 2).reshape(1).astype(jnp.int32)
    [edge] = on_chip(
        chain_kernel, "chain", [jax.ShapeDtypeStruct((32, 8, GC), F32)], flag, total
    )
    edge = over_ctx(edge)
    out = on_chip(
        entering_kernel, "entering", [pair(RETURN)] * 4, place, by_chip, own, edge,
        scratch=[pltpu.VMEM((CHIPS, *PAIR), F32)],
    )
    mine, send = on_chip(fork_kernel, "fork", [quad] * 2, place, *turned(out), keep, come, kept)
    scan_out, grad_x, *ends = finish(
        place, x, dy, cum, cumt, y_in, dx_in, mine, swap(send), gain, b, c, db_in, dc_in
    )
    ends = gathered(turned(ends), iy, core == 0)
    grad_b = ends[:, :ROWS].reshape(GROUPS * ROWS, N)
    grad_c = ends[:, ROWS : 2 * ROWS].reshape(GROUPS * ROWS, N)
    rest = ends[:, 2 * ROWS :].reshape(GROUPS, 2, 2, 16, 128)
    rest = lax.dynamic_index_in_dim(rest, core, 2, keepdims=False)
    rest = jnp.concatenate([rest[:, 0, :HG], rest[:, 1, :HG, :64]], axis=2)
    grad_decay = rest.transpose(0, 2, 1).reshape(GROUPS * ROWS, HG)
    return scan_out, grad_x, grad_b, grad_c, grad_decay


def solution(mesh):
    grid = Mesh(mesh.devices.reshape(4, 8, 4, 2), ("x", "z", "y", "core"))
    ctx, head = ("x", "z"), ("y", "core")
    rows = P((*ctx, *head), None)
    return jax.shard_map(
        shards,
        mesh=grid,
        in_specs=(rows, rows, P(ctx, None), P(ctx, None), P(ctx, head), P(head)),
        out_specs=(rows, rows, P(ctx, None), P(ctx, None), P(ctx, head)),
        check_vma=False,
    )
```

time: 237 us -> 212 us (0.89)
  waiting for transfers between devices: 59.4 us -> 89 us
  blocking collectives: 48.5 us -> 24.3 us
  starting transfers between devices: 45.4 us -> 30.3 us
  other arithmetic: 13.6 us -> 1.51 us
  local copies, waits for them, and re-layouts: 29 us -> 18.3 us
  Pallas kernels: 37.6 us -> 47.4 us
    ppermute x8 -> x12, waiting for transfers between devices: 9.24 us -> 64.2 us  [the longest x9 52.6 us: turned(): lax.ppermute(v[turn], 'y', [(i, (i + turn) % CHIPS) for i in range(CHIPS)])]
    all_to_all x5 -> x2, waiting for transfers between devices: 50.1 us -> 24.8 us  [the longest x1 20.7 us: shards(): lax.all_to_all(v, ('x', 'z'), split_axis=0, concat_axis=0, tiled=True)]
    all_to_all x3 -> x1, blocking collectives: 48.5 us -> 24.3 us  [shards(): lax.all_to_all(v, ('x', 'z'), split_axis=0, concat_axis=0, tiled=True)]
    all_to_all x5 -> x2, starting transfers between devices: 27.6 us -> 15.9 us  [the longest x1 10.8 us: shards(): lax.all_to_all(v, ('x', 'z'), split_axis=0, concat_axis=0, tiled=True)]
    pallas_call x4 -> x9, Pallas kernels: 9.65 us -> 18.1 us  [the longest x1 9.42 us: chunk_states(): pl.pallas_call(states_kernel, grid_spec=pltpu.PrefetchScalarGridSpec(num_...]
    select_n x3 -> x0, other arithmetic: 5.66 us -> none  [the longest x1 3.07 us: shards(): jnp.where(low, l_chip, l_early)]
    add x3 -> x0, other arithmetic: 5.49 us -> none  [the longest x1 2.94 us: shards(): s_chip = kept[:, 1] * s0 + s1]
    unnamed x54 -> x53, local copies, waits for them, and re-layouts: 9.59 us -> 13.7 us
  transfers between devices with their start and end apart: 13 -> 14, of which waited for: 5 -> 13; matrix products, arithmetic and copies ran while one was open for 12% -> 2% of each run, Pallas kernels for 5% -> 5%
where the time goes in v1:
time: 212 us
  waiting for transfers between devices  89 us (42%)
  Pallas kernels  47.4 us (22%)
  starting transfers between devices  30.3 us (14%)
  blocking collectives  24.3 us (11%)
  local copies, waits for them, and re-layouts  18.3 us (9%)
    ppermute x9, waiting for transfers between devices, turned(): lax.ppermute(v[turn], 'y', [(i, (i + turn) % CHIPS) for i in range(CHIPS)])  52.6 us
    all_to_all x1, blocking collectives, shards(): lax.all_to_all(v, ('x', 'z'), split_axis=0, concat_axis=0, tiled=True)  24.3 us
    all_to_all x1, waiting for transfers between devices, shards(): lax.all_to_all(v, ('x', 'z'), split_axis=0, concat_axis=0, tiled=True)  20.7 us
    pallas_call x1, Pallas kernels, finish(): pl.pallas_call(finish_kernel, grid_spec=pltpu.PrefetchScalarGridSpec(num_...  18.2 us
    unnamed x53, local copies, waits for them, and re-layouts  13.7 us
    pallas_call x1, Pallas kernels, within(): pl.pallas_call(within_kernel, grid=(GROUPS,), in_specs=[by_column, by_col...  11.1 us
    all_to_all x1, starting transfers between devices, shards(): lax.all_to_all(v, ('x', 'z'), split_axis=0, concat_axis=0, tiled=True)  10.8 us
    ppermute x9, starting transfers between devices, turned(): lax.ppermute(v[turn], 'y', [(i, (i + turn) % CHIPS) for i in range(CHIPS)])  10.4 us
  transfers between devices with their start and end apart: 14, of which 13 were waited for; matrix products, arithmetic and copies ran while one was open for 2% of the time, Pallas kernels for 5%

profile of v1, /device:TPU:33, one launch (start us, length us, event | category | flops | bytes accessed | tf_op | source)
XLA Modules:
  0.0 211.7 jit_solution(1309143656090935167)
XLA Ops:
  0.6 0.0 copy-start.12
  0.6 0.9 copy-done.12
  1.5 0.7 copy-done.21
  2.2 0.8 pack.1
  3.0 5.1 %all-to-all-start = ((f32[8,2,16,192]{3,2,1,0:T(8,128)}), f32[8,2,16,192]{3,2,1,0:T(8,128)S(1)}, u32[]{:S(2)}, u32[]{:S(2)}) async-start(f32[8,2,16,192]{3,2,1,0:T(8,128)} %pack.1), calls=%async_computation | async-start | bytes 524288 | tf_op jit(solution)/shard_map/all_to_all | solution.py:433
  8.1 0.8 constant_dynamic-slice_fusion.1
  9.0 0.7 copy.21.bt_ref
  9.7 0.7 copy.22.ct_ref
  10.5 0.1 pad_add_fusion.core_ref.place.place_ref
  10.5 4.1 %all-to-all-done.got_ref = f32[8,2,16,192]{3,2,1,0:T(8,128)S(1)} async-done(((f32[8,2,16,192]{3,2,1,0:T(8,128)}), f32[8,2,16,192]{3,2,1,0:T(8,128)S(1)}, u32[]{:S(2)}, u32[]{:S(2)}) %all-to-all-start) | async-done | bytes 196640 | tf_op jit(solution)/shard_map/all_to_all | solution.py:433
  14.6 1.3 decays.1
  16.0 0.0 copy-start.6
  16.0 0.9 copy-done.6
  16.9 9.4 %chunk_states.1 = (f32[4,2,128,640]{3,2,1,0:T(8,128)}, f32[4,2,128,640]{3,2,1,0:T(8,128)}) custom-call(s32[2]{0:T(128)} %copy-done.17, bf16[192,5120]{1,0:T(8,128)(2,1)} %x_ref.4, bf16[192,5120]{1,0:T(8,128)(2,1)} %dy_ref.4, f32[8,192,16]{2,1,0:T(8,128)} %copy-done.6, bf16[128,192]{1,0:T(8,128)(2,1)} %copy.21.bt_ref, bf16[128,192]{1,0:T(8,128)(2,1)} %copy.22.ct_ref), custom_call_target="tpu_custom_call" | custom-call | tf_op jit(solution)/shard_map/chunk_states/pallas_call | solution.py:212
  26.3 1.1 collective-permute-start
  27.3 4.7 %collective-permute-done.come_ref = f32[4,2,128,640]{3,2,1,0:T(8,128)S(1)} collective-permute-done((f32[4,2,128,640]{3,2,1,0:T(8,128)}, f32[4,2,128,640]{3,2,1,0:T(8,128)S(1)}, u32[]{:S(2)}, u32[]{:S(2)}) %collective-permute-start) | collective-permute-done | bytes 2621472 | tf_op jit(solution)/shard_map/ppermute | solution.py:423
  32.1 2.7 %copy-done = f32[4,2,128,640]{3,2,1,0:T(8,128)S(1)} copy-done((f32[4,2,128,640]{3,2,1,0:T(8,128)S(1)}, f32[4,2,128,640]{3,2,1,0:T(8,128)}, u32[]{:S(2)}) %copy-start) | copy-done | bytes 2621464
  34.8 0.7 copy-done.18
  35.5 0.9 join.1
  36.4 0.4 collective-permute-start.1
  36.7 1.8 collective-permute-start.2
  38.5 0.7 collective-permute-start.3
  39.3 0.0 copy-start.13
  39.3 11.1 %within_chunk.1 = (f32[192,5120]{1,0:T(8,128)S(1)}, f32[192,5120]{1,0:T(8,128)S(1)}, f32[192,128]{1,0:T(8,128)S(1)}, f32[192,128]{1,0:T(8,128)S(1)}) custom-call(bf16[192,5120]{1,0:T(8,128)(2,1)S(1)} %copy-done.2, bf16[192,5120]{1,0:T(8,128)(2,1)S(1)} %copy-done.3, f32[8,192,16]{2,1,0:T(8,128)S(1)} %copy-done.7, ...), custom_call_target="tpu_custom_call" | custom-call | flops 20000000000 | bytes 12000000 | tf_op jit(solution)/shard_map/within_chunk/pallas_call | solution.py:108
  50.3 1.9 copy-done.4
  52.2 1.9 copy-done.5
  54.1 0.6 copy-done.15
  54.7 0.3 owner_decays.1.d_ref
  55.0 0.0 collective-permute-done.1.r1
  55.0 12.1 %collective-permute-done.2.r2 = f32[2,128,640]{2,1,0:T(8,128)S(1)} collective-permute-done((f32[2,128,640]{2,1,0:T(8,128)S(1)}, f32[2,128,640]{2,1,0:T(8,128)S(1)}, u32[]{:S(2)}, u32[]{:S(2)}) %collective-permute-start.2) | collective-permute-done | bytes 655392 | tf_op jit(solution)/shard_map/ppermute | solution.py:402
  67.1 0.9 collective-permute-done.3.r3
  68.0 1.0 totals.1
  69.0 0.9 copy-done.9
  69.9 10.8 %all-to-all-start.1 = ((f32[32,8,768]{2,1,0:T(8,128)}), f32[32,8,768]{2,1,0:T(8,128)S(1)}, u32[]{:S(2)}, u32[]{:S(2)}) async-start(f32[32,8,768]{2,1,0:T(8,128)} %copy-done.9), calls=%async_computation.1 | async-start | bytes 1572864 | tf_op jit(solution)/shard_map/all_to_all | solution.py:424
  80.7 20.7 %all-to-all-done.1.p_ref = f32[32,8,768]{2,1,0:T(8,128)S(1)} async-done(((f32[32,8,768]{2,1,0:T(8,128)}), f32[32,8,768]{2,1,0:T(8,128)S(1)}, u32[]{:S(2)}, u32[]{:S(2)}) %all-to-all-start.1) | async-done | bytes 786464 | tf_op jit(solution)/shard_map/all_to_all | solution.py:424
  101.4 0.1 chain.1
  101.5 24.3 %all_to_all.15.edge_ref = f32[32,8,640]{2,1,0:T(8,128)S(1)} all-to-all(f32[32,8,640]{2,1,0:T(8,128)S(1)} %chain.1), channel_id=1, replica_groups=mesh['x'=4,'z'=8,'y'=4,'core'=2] {'x','z'}, dimensions={0} | all-to-all | bytes 1310720 | tf_op jit(solution)/shard_map/all_to_all | solution.py:424
  125.8 1.1 entering.1
  126.9 1.8 collective-permute-start.4
  128.7 3.1 %collective-permute-start.5 = (f32[2,128,640]{2,1,0:T(8,128)S(1)}, f32[2,128,640]{2,1,0:T(8,128)S(1)}, u32[]{:S(2)}, u32[]{:S(2)}) collective-permute-start(f32[2,128,640]{2,1,0:T(8,128)S(1)} %get-tuple-element.70), channel_id=1, source_target_pairs={{0,4},{2,6},{4,0},{6,2},{1,5},{3,7},{5,1},{7,3},{8,12},{10,14},{12... | collective-permute-start | bytes 1966088 | tf_op jit(solution)/shard_map/ppermute | solution.py:402
  131.7 10.6 %collective-permute-done.4.r1 = f32[2,128,640]{2,1,0:T(8,128)S(1)} collective-permute-done((f32[2,128,640]{2,1,0:T(8,128)S(1)}, f32[2,128,640]{2,1,0:T(8,128)S(1)}, u32[]{:S(2)}, u32[]{:S(2)}) %collective-permute-start.4) | collective-permute-done | bytes 655392 | tf_op jit(solution)/shard_map/ppermute | solution.py:402
  142.3 14.9 %collective-permute-done.5.r2 = f32[2,128,640]{2,1,0:T(8,128)S(1)} collective-permute-done((f32[2,128,640]{2,1,0:T(8,128)S(1)}, f32[2,128,640]{2,1,0:T(8,128)S(1)}, u32[]{:S(2)}, u32[]{:S(2)}) %collective-permute-start.5) | collective-permute-done | bytes 655392 | tf_op jit(solution)/shard_map/ppermute | solution.py:402
  157.3 2.2 %collective-permute-done.6.r3 = f32[2,128,640]{2,1,0:T(8,128)S(1)} collective-permute-done((f32[2,128,640]{2,1,0:T(8,128)S(1)}, f32[2,128,640]{2,1,0:T(8,128)S(1)}, u32[]{:S(2)}, u32[]{:S(2)}) %collective-permute-start.6) | collective-permute-done | bytes 655392 | tf_op jit(solution)/shard_map/ppermute | solution.py:402
  159.5 3.2 %fork.1 = (f32[4,2,128,640]{3,2,1,0:T(8,128)S(1)}, f32[4,2,128,640]{3,2,1,0:T(8,128)S(1)}) custom-call(s32[2]{0:T(128)S(1)} %copy-done.19, f32[2,128,640]{2,1,0:T(8,128)S(1)} %get-tuple-element.68.r0, f32[2,128,640]{2,1,0:T(8,128)S(1)} %collective-permute-done.4.r1, f32[2,128,640]{2,1,0:T(8,128)S(1)} %collective-permute-done.5.r2, ...), custom_call_target="tpu_custom_call" | custom-call | tf_op jit(solution)/shard_map/fork/pallas_call | solution.py:138
  162.7 1.6 copy-done.8
  164.2 2.0 collective-permute-start.7
  166.3 4.7 %collective-permute-done.7.come_ref = f32[4,2,128,640]{3,2,1,0:T(8,128)} collective-permute-done((f32[4,2,128,640]{3,2,1,0:T(8,128)S(1)}, f32[4,2,128,640]{3,2,1,0:T(8,128)}, u32[]{:S(2)}, u32[]{:S(2)}) %collective-permute-start.7) | collective-permute-done | bytes 2621472 | tf_op jit(solution)/shard_map/ppermute | solution.py:423
  170.9 18.2 %finish.1 = (bf16[192,5120]{1,0:T(8,128)(2,1)}, bf16[192,5120]{1,0:T(8,128)(2,1)}, f32[448,128]{1,0:T(8,128)}, f32[448,128]{1,0:T(8,128)}, f32[448,128]{1,0:T(8,128)}, /*index=5*/f32[448,128]{1,0:T(8,128)}) custom-call(s32[2]{0:T(128)} %copy-done.17, bf16[192,5120]{1,0:T(8,128)(2,1)} %x_ref.4, bf16[192,5120]{1,0:T(8,128)(2,1)} %dy_ref.4, ...), custom_call_target="tpu_custom_call" | custom-call | tf_op jit(solution)/shard_map/finish/pallas_call | solution.py:376
  189.1 0.0 copy-start.22
  189.1 2.0 collective-permute-start.8
  191.1 0.7 collective-permute-start.10
  191.8 1.0 bitcast_dynamic-update-slice_fusion.6
  192.7 3.5 %collective-permute-done.8 = f32[448,128]{1,0:T(8,128)S(1)} collective-permute-done((f32[448,128]{1,0:T(8,128)}, f32[448,128]{1,0:T(8,128)S(1)}, u32[]{:S(2)}, u32[]{:S(2)}) %collective-permute-start.8) | collective-permute-done | bytes 229408 | tf_op jit(solution)/shard_map/ppermute | solution.py:402
  196.3 3.1 %collective-permute-done.9 = f32[448,128]{1,0:T(8,128)S(1)} collective-permute-done((f32[448,128]{1,0:T(8,128)}, f32[448,128]{1,0:T(8,128)S(1)}, u32[]{:S(2)}, u32[]{:S(2)}) %collective-permute-start.9) | collective-permute-done | bytes 229408 | tf_op jit(solution)/shard_map/ppermute | solution.py:402
  199.4 5.2 %collective-permute-done.10 = f32[448,128]{1,0:T(8,128)S(1)} collective-permute-done((f32[448,128]{1,0:T(8,128)}, f32[448,128]{1,0:T(8,128)S(1)}, u32[]{:S(2)}, u32[]{:S(2)}) %collective-permute-start.10) | collective-permute-done | bytes 229408 | tf_op jit(solution)/shard_map/ppermute | solution.py:402
  204.8 0.1 constant_dynamic-slice_fusion
  204.8 0.9 collective-permute-start.11
  205.7 2.2 %collective-permute-done.11 = f32[4,448,128]{2,1,0:T(8,128)} collective-permute-done((f32[4,448,128]{2,1,0:T(8,128)S(1)}, f32[4,448,128]{2,1,0:T(8,128)}, u32[]{:S(2)}, u32[]{:S(2)}) %collective-permute-start.11) | collective-permute-done | bytes 917536 | tf_op jit(solution)/shard_map/ppermute | solution.py:410
  208.0 1.3 select_bitcast_fusion.1
  209.3 0.1 pad_maximum_fusion
  209.4 0.1 copy.23
  209.6 1.3 fusion
  210.9 0.1 copy.25
  211.0 0.7 reshape.36
  (46 shorter events, 0.2 us)
Async XLA Ops:
  0.6 0.9 copy-start.12
  1.5 0.7 copy-start.21
  3.0 11.6 %all-to-all-start = ((f32[8,2,16,192]{3,2,1,0:T(8,128)}), f32[8,2,16,192]{3,2,1,0:T(8,128)S(1)}, u32[]{:S(2)}, u32[]{:S(2)}) async-start(f32[8,2,16,192]{3,2,1,0:T(8,128)} %pack.1), calls=%async_computation | async-start | bytes 524288 | tf_op jit(solution)/shard_map/all_to_all | solution.py:433
  9.0 30.3 %copy-start.10 = (bf16[192,128]{1,0:T(8,128)(2,1)}, bf16[192,128]{1,0:T(8,128)(2,1)S(1)}, u32[]{:S(2)}) copy-start(bf16[192,128]{1,0:T(8,128)(2,1)S(1)} %get-tuple-element.87.c_ref) | copy-start | bytes 147460
  9.0 30.3 %copy-start.11 = (bf16[192,128]{1,0:T(8,128)(2,1)}, bf16[192,128]{1,0:T(8,128)(2,1)S(1)}, u32[]{:S(2)}) copy-start(bf16[192,128]{1,0:T(8,128)(2,1)S(1)} %get-tuple-element.88.b_ref) | copy-start | bytes 147460
  10.5 6.3 %copy-start.17 = (s32[2]{0:T(128)}, s32[2]{0:T(128)S(1)}, u32[]{:S(2)}) copy-start(s32[2]{0:T(128)S(1)} %pad_add_fusion.core_ref.place.place_ref) | copy-start | bytes 28
  16.0 0.9 copy-start.6
  16.9 9.4 %copy-start.20 = (f32[8,1,640]{2,1,0:T(1,128)}, f32[8,1,640]{2,1,0:T(1,128)S(1)}, u32[]{:S(2)}) copy-start(f32[8,1,640]{2,1,0:T(1,128)S(1)} %get-tuple-element.74.gain_ref) | copy-start | bytes 61444
  16.9 22.4 %copy-start.14 = (f32[8,16,192]{2,1,0:T(8,128)}, f32[8,16,192]{2,1,0:T(8,128)S(1)}, u32[]{:S(2)}) copy-start(f32[8,16,192]{2,1,0:T(8,128)S(1)} %get-tuple-element.45.cumt_ref) | copy-start | bytes 294916
  26.3 5.8 %collective-permute-start = (f32[4,2,128,640]{3,2,1,0:T(8,128)}, f32[4,2,128,640]{3,2,1,0:T(8,128)S(1)}, u32[]{:S(2)}, u32[]{:S(2)}) collective-permute-start(f32[4,2,128,640]{3,2,1,0:T(8,128)} %get-tuple-element.47), channel_id=1, source_target_pairs={{0,1},{1,0},{2,3},{3,2},{4,5},{5,4},{6,7},{7,6},{8,9},{9,8},{10,11... | collective-permute-start | bytes 7864328 | tf_op jit(solution)/shard_map/ppermute | solution.py:423
  32.1 4.3 %copy-start.1 = (f32[4,2,128,640]{3,2,1,0:T(8,128)}, f32[4,2,128,640]{3,2,1,0:T(8,128)S(1)}, u32[]{:S(2)}) copy-start(f32[4,2,128,640]{3,2,1,0:T(8,128)S(1)} %collective-permute-done.come_ref) | copy-start | bytes 7864324
  32.1 2.7 %copy-start = (f32[4,2,128,640]{3,2,1,0:T(8,128)S(1)}, f32[4,2,128,640]{3,2,1,0:T(8,128)}, u32[]{:S(2)}) copy-start(f32[4,2,128,640]{3,2,1,0:T(8,128)} %get-tuple-element.46.keep_ref) | copy-start | bytes 7864324
  34.8 0.7 copy-start.18
  35.5 3.8 %copy-start.2 = (bf16[192,5120]{1,0:T(8,128)(2,1)S(1)}, bf16[192,5120]{1,0:T(8,128)(2,1)}, u32[]{:S(2)}) copy-start(bf16[192,5120]{1,0:T(8,128)(2,1)} %x_ref.4) | copy-start | bytes 5898244
  35.5 3.8 %copy-start.3 = (bf16[192,5120]{1,0:T(8,128)(2,1)S(1)}, bf16[192,5120]{1,0:T(8,128)(2,1)}, u32[]{:S(2)}) copy-start(bf16[192,5120]{1,0:T(8,128)(2,1)} %dy_ref.4) | copy-start | bytes 5898244
  35.5 3.8 %copy-start.7 = (f32[8,192,16]{2,1,0:T(8,128)S(1)}, f32[8,192,16]{2,1,0:T(8,128)}, u32[]{:S(2)}) copy-start(f32[8,192,16]{2,1,0:T(8,128)} %copy-done.6) | copy-start | bytes 294916
  36.4 18.6 %collective-permute-start.1 = (f32[2,128,640]{2,1,0:T(8,128)S(1)}, f32[2,128,640]{2,1,0:T(8,128)S(1)}, u32[]{:S(2)}, u32[]{:S(2)}) collective-permute-start(f32[2,128,640]{2,1,0:T(8,128)S(1)} %get-tuple-element.56), channel_id=1, source_target_pairs={{0,2},{2,4},{4,6},{6,0},{1,3},{3,5},{5,7},{7,1},{8,10},{10,12},{12... | collective-permute-start | bytes 1966088 | tf_op jit(solution)/shard_map/ppermute | solution.py:402
  36.7 30.4 %collective-permute-start.2 = (f32[2,128,640]{2,1,0:T(8,128)S(1)}, f32[2,128,640]{2,1,0:T(8,128)S(1)}, u32[]{:S(2)}, u32[]{:S(2)}) collective-permute-start(f32[2,128,640]{2,1,0:T(8,128)S(1)} %get-tuple-element.57), channel_id=1, source_target_pairs={{0,4},{2,6},{4,0},{6,2},{1,5},{3,7},{5,1},{7,3},{8,12},{10,14},{12... | collective-permute-start | bytes 1966088 | tf_op jit(solution)/shard_map/ppermute | solution.py:402
  38.5 29.5 %collective-permute-start.3 = (f32[2,128,640]{2,1,0:T(8,128)S(1)}, f32[2,128,640]{2,1,0:T(8,128)S(1)}, u32[]{:S(2)}, u32[]{:S(2)}) collective-permute-start(f32[2,128,640]{2,1,0:T(8,128)S(1)} %get-tuple-element.58), channel_id=1, source_target_pairs={{0,6},{2,0},{4,2},{6,4},{1,7},{3,1},{5,3},{7,5},{8,14},{10,8},{12,... | collective-permute-start | bytes 1966088 | tf_op jit(solution)/shard_map/ppermute | solution.py:402
  39.3 15.5 %copy-start.13 = (f32[1536,10]{0,1:T(8,128)S(1)}, f32[1536,10]{0,1:T(8,128)}, u32[]{:S(2)}) copy-start(f32[1536,10]{0,1:T(8,128)} %param.10) | copy-start | bytes 184324
  50.3 1.9 copy-start.4
  52.2 1.9 copy-start.5
  54.1 0.6 copy-start.15
  54.7 14.3 %copy-start.16 = (f32[192,128]{1,0:T(8,128)}, f32[192,128]{1,0:T(8,128)S(1)}, u32[]{:S(2)}) copy-start(f32[192,128]{1,0:T(8,128)S(1)} %get-tuple-element.76.dc0_ref) | copy-start | bytes 294916
  69.0 0.9 copy-start.9
  69.9 55.8 %copy-start.19 = (s32[2]{0:T(128)S(1)}, s32[2]{0:T(128)}, u32[]{:S(2)}) copy-start(s32[2]{0:T(128)} %copy-done.17) | copy-start | bytes 28
  69.9 31.4 %all-to-all-start.1 = ((f32[32,8,768]{2,1,0:T(8,128)}), f32[32,8,768]{2,1,0:T(8,128)S(1)}, u32[]{:S(2)}, u32[]{:S(2)}) async-start(f32[32,8,768]{2,1,0:T(8,128)} %copy-done.9), calls=%async_computation.1 | async-start | bytes 1572864 | tf_op jit(solution)/shard_map/all_to_all | solution.py:424
  126.9 15.5 %collective-permute-start.4 = (f32[2,128,640]{2,1,0:T(8,128)S(1)}, f32[2,128,640]{2,1,0:T(8,128)S(1)}, u32[]{:S(2)}, u32[]{:S(2)}) collective-permute-start(f32[2,128,640]{2,1,0:T(8,128)S(1)} %get-tuple-element.69), channel_id=1, source_target_pairs={{0,2},{2,4},{4,6},{6,0},{1,3},{3,5},{5,7},{7,1},{8,10},{10,12},{12... | collective-permute-start | bytes 1966088 | tf_op jit(solution)/shard_map/ppermute | solution.py:402
  128.7 28.6 %collective-permute-start.5 = (f32[2,128,640]{2,1,0:T(8,128)S(1)}, f32[2,128,640]{2,1,0:T(8,128)S(1)}, u32[]{:S(2)}, u32[]{:S(2)}) collective-permute-start(f32[2,128,640]{2,1,0:T(8,128)S(1)} %get-tuple-element.70), channel_id=1, source_target_pairs={{0,4},{2,6},{4,0},{6,2},{1,5},{3,7},{5,1},{7,3},{8,12},{10,14},{12... | collective-permute-start | bytes 1966088 | tf_op jit(solution)/shard_map/ppermute | solution.py:402
  131.7 27.7 %collective-permute-start.6 = (f32[2,128,640]{2,1,0:T(8,128)S(1)}, f32[2,128,640]{2,1,0:T(8,128)S(1)}, u32[]{:S(2)}, u32[]{:S(2)}) collective-permute-start(f32[2,128,640]{2,1,0:T(8,128)S(1)} %get-tuple-element.71), channel_id=1, source_target_pairs={{0,6},{2,0},{4,2},{6,4},{1,7},{3,1},{5,3},{7,5},{8,14},{10,8},{12,... | collective-permute-start | bytes 1966088 | tf_op jit(solution)/shard_map/ppermute | solution.py:402
  162.7 1.6 copy-start.8
  164.2 6.7 %collective-permute-start.7 = (f32[4,2,128,640]{3,2,1,0:T(8,128)S(1)}, f32[4,2,128,640]{3,2,1,0:T(8,128)}, u32[]{:S(2)}, u32[]{:S(2)}) collective-permute-start(f32[4,2,128,640]{3,2,1,0:T(8,128)S(1)} %get-tuple-element.73), channel_id=1, source_target_pairs={{0,1},{1,0},{2,3},{3,2},{4,5},{5,4},{6,7},{7,6},{8,9},{9,8},{10,11... | collective-permute-start | bytes 7864328 | tf_op jit(solution)/shard_map/ppermute | solution.py:423
  189.1 15.5 %copy-start.22 = (f32[448,128]{1,0:T(8,128)S(1)}, f32[448,128]{1,0:T(8,128)}, u32[]{:S(2)}) copy-start(f32[448,128]{1,0:T(8,128)} %get-tuple-element.79) | copy-start | bytes 688132
  189.1 7.1 %collective-permute-start.8 = (f32[448,128]{1,0:T(8,128)}, f32[448,128]{1,0:T(8,128)S(1)}, u32[]{:S(2)}, u32[]{:S(2)}) collective-permute-start(f32[448,128]{1,0:T(8,128)} %get-tuple-element.80), channel_id=1, source_target_pairs={{0,6},{2,0},{4,2},{6,4},{1,7},{3,1},{5,3},{7,5},{8,14},{10,8},{12,... | collective-permute-start | bytes 688136 | tf_op jit(solution)/shard_map/ppermute | solution.py:402
  191.1 8.3 %collective-permute-start.9 = (f32[448,128]{1,0:T(8,128)}, f32[448,128]{1,0:T(8,128)S(1)}, u32[]{:S(2)}, u32[]{:S(2)}) collective-permute-start(f32[448,128]{1,0:T(8,128)} %get-tuple-element.81), channel_id=1, source_target_pairs={{0,4},{2,6},{4,0},{6,2},{1,5},{3,7},{5,1},{7,3},{8,12},{10,14},{12... | collective-permute-start | bytes 688136 | tf_op jit(solution)/shard_map/ppermute | solution.py:402
  191.1 13.5 %collective-permute-start.10 = (f32[448,128]{1,0:T(8,128)}, f32[448,128]{1,0:T(8,128)S(1)}, u32[]{:S(2)}, u32[]{:S(2)}) collective-permute-start(f32[448,128]{1,0:T(8,128)} %get-tuple-element.82), channel_id=1, source_target_pairs={{0,2},{2,4},{4,6},{6,0},{1,3},{3,5},{5,7},{7,1},{8,10},{10,12},{12... | collective-permute-start | bytes 688136 | tf_op jit(solution)/shard_map/ppermute | solution.py:402
  204.8 3.1 %collective-permute-start.11 = (f32[4,448,128]{2,1,0:T(8,128)S(1)}, f32[4,448,128]{2,1,0:T(8,128)}, u32[]{:S(2)}, u32[]{:S(2)}) collective-permute-start(f32[4,448,128]{2,1,0:T(8,128)S(1)} %constant_dynamic-slice_fusion), channel_id=1, source_target_pairs={{0,1},{1,0},{2,3},{3,2},{4,5},{5,4},{6,7},{7,6},{8,9},{9,8},{10,11... | collective-permute-start | bytes 2752520 | tf_op jit(solution)/shard_map/ppermute | solution.py:410

commit v2 on v1

--- a/solution.py
+++ b/solution.py
@@ -131,7 +131,7 @@
 VMEM = pl.BlockSpec(memory_space=pltpu.VMEM)
 SMEM = pl.BlockSpec(memory_space=pltpu.SMEM)
 PAIR = (2, N, GC)
-RETURN = F32
+LOWS = 64
 
 
 def on_chip(kernel, name, outs, *args, scratch=(), scalars=1):
@@ -277,7 +277,11 @@
             if c != order[-1]:
                 e = e * d_ref[c : c + 1, :] + sorted_ref[c, way]
     for turn, out in enumerate((o0, o1, o2, o3)):
-        out[...] = all_ref[lax.rem(place_ref[1] + turn, CHIPS)].astype(RETURN)
+        at = lax.rem(place_ref[1] + turn, CHIPS)
+        for way in range(2):
+            high, low = halves(all_ref[at, way])
+            out[way, :N] = high
+            out[way, N:] = low[:LOWS]
 
 
 def fork_kernel(place_ref, r0, r1, r2, r3, keep_ref, come_ref, kept_ref, mine_ref, send_ref):
@@ -286,7 +290,10 @@
         j = lax.rem(place_ref[1] - turn + CHIPS, CHIPS)
         for way in range(2):
             direct_is_mine = low if way == 0 else jnp.logical_not(low)
-            direct = ref[way].astype(F32)
+            low_rows = jnp.concatenate(
+                [ref[way, N:].astype(F32), jnp.zeros((N - LOWS, GC), F32)], axis=0
+            )
+            direct = ref[way, :N].astype(F32) + low_rows
             passed = jnp.where(direct_is_mine, keep_ref[j, way], come_ref[j, way])
             through = kept_ref[way, j] * direct + passed
             mine_ref[j, way] = jnp.where(direct_is_mine, direct, through)
@@ -343,17 +350,15 @@
         high, low = halves(v)
         return dot(of_head, high, NT) + dot(of_head, low, NT)
 
-    product = jnp.sum(entering * leaving, axis=0, keepdims=True)
-    across = by_head(jnp.broadcast_to(product, (8, 2 * GC)))[:, 0:1]
+    x_dx = x * dx_carried
+    row = from_start[ROWS - 1 : ROWS, :] * jnp.sum(entering * leaving, axis=0, keepdims=True)
+    row += jnp.sum(x_dx, axis=0, keepdims=True)
     t = lax.broadcasted_iota(jnp.int32, (ROWS, ROWS), 0)
     s = lax.broadcasted_iota(jnp.int32, (ROWS, ROWS), 1)
     after = (t >= s).astype(BF16)
-    before = (t < s).astype(BF16)
-    gd = across * jnp.exp(cumt_ref[...].reshape(32, ROWS)[:, ROWS - 1 : ROWS])
-    for part in thirds(by_head(dy * y - x * dx_in)):
+    gd = jnp.broadcast_to(by_head(jnp.broadcast_to(row, (8, 2 * GC)))[:, 0:1], (32, ROWS))
+    for part in thirds(by_head(dy * y - (x * dx_in + x_dx))):
         gd += dot(part, after)
-    for part in thirds(by_head(x * dx_carried)):
-        gd += dot(part, before)
     gd_ref[step] = gd
 
     @pl.when(step == CHIPS - 1)
@@ -459,7 +464,7 @@
     )
     edge = over_ctx(edge)
     out = on_chip(
-        entering_kernel, "entering", [pair(RETURN)] * 4, place, by_chip, own, edge,
+        entering_kernel, "entering", [jax.ShapeDtypeStruct((2, N + LOWS, GC), BF16)] * 4, place, by_chip, own, edge,
         scratch=[pltpu.VMEM((CHIPS, *PAIR), F32)],
     )
     mine, send = on_chip(fork_kernel, "fork", [quad] * 2, place, *turned(out), keep, come, kept)

time: 212 us -> 202 us (0.953)
  waiting for transfers between devices: 89 us -> 81.9 us
  Pallas kernels: 47.4 us -> 44 us
    ppermute x9, waiting for transfers between devices: 52.6 us -> 45.5 us  [turned(): lax.ppermute(v[turn], 'y', [(i, (i + turn) % CHIPS) for i in range(CHIPS)])]
    pallas_call x1, Pallas kernels: 18.2 us -> 15.4 us  [finish(): pl.pallas_call(finish_kernel, grid_spec=pltpu.PrefetchScalarGridSpec(num_...]
    unnamed x53 -> x55, local copies, waits for them, and re-layouts: 13.7 us -> 13.7 us
  transfers between devices with their start and end apart: 14 -> 14, of which waited for: 13 -> 13; matrix products, arithmetic and copies ran while one was open for 2% -> 2% of each run, Pallas kernels for 5% -> 6%
where the time goes in v2:
time: 202 us; the launch traced here: 201 us
  waiting for transfers between devices  81.9 us (41%)
  Pallas kernels  44 us (22%)
  starting transfers between devices  30.3 us (15%)
  blocking collectives  24.3 us (12%)
  local copies, waits for them, and re-layouts  18.4 us (9%)
    ppermute x9, waiting for transfers between devices, turned(): lax.ppermute(v[turn], 'y', [(i, (i + turn) % CHIPS) for i in range(CHIPS)])  45.5 us
    all_to_all x1, blocking collectives, shards(): lax.all_to_all(v, ('x', 'z'), split_axis=0, concat_axis=0, tiled=True)  24.3 us
    all_to_all x1, waiting for transfers between devices, shards(): lax.all_to_all(v, ('x', 'z'), split_axis=0, concat_axis=0, tiled=True)  20.7 us
    pallas_call x1, Pallas kernels, finish(): pl.pallas_call(finish_kernel, grid_spec=pltpu.PrefetchScalarGridSpec(num_...  15.4 us
    unnamed x55, local copies, waits for them, and re-layouts  13.7 us
    pallas_call x1, Pallas kernels, within(): pl.pallas_call(within_kernel, grid=(GROUPS,), in_specs=[by_column, by_col...  11.1 us
    all_to_all x1, starting transfers between devices, shards(): lax.all_to_all(v, ('x', 'z'), split_axis=0, concat_axis=0, tiled=True)  10.8 us
    ppermute x9, starting transfers between devices, turned(): lax.ppermute(v[turn], 'y', [(i, (i + turn) % CHIPS) for i in range(CHIPS)])  10.4 us
  transfers between devices with their start and end apart: 14, of which 13 were waited for; matrix products, arithmetic and copies ran while one was open for 2% of the time, Pallas kernels for 6%

profile of v2, /device:TPU:33, one launch (start us, length us, event | category | flops | bytes accessed | tf_op | source)
XLA Modules:
  0.0 201.3 jit_solution(13265199735923685430)
XLA Ops:
  0.6 0.0 copy-start.13
  0.6 0.9 copy-done.13
  1.5 0.7 copy-done.22
  2.2 0.8 pack.1
  3.0 5.1 %all-to-all-start = ((f32[8,2,16,192]{3,2,1,0:T(8,128)}), f32[8,2,16,192]{3,2,1,0:T(8,128)S(1)}, u32[]{:S(2)}, u32[]{:S(2)}) async-start(f32[8,2,16,192]{3,2,1,0:T(8,128)} %pack.1), calls=%async_computation | async-start | bytes 524288 | tf_op jit(solution)/shard_map/all_to_all | solution.py:438
  8.1 0.8 constant_dynamic-slice_fusion.1
  9.0 0.7 copy.21.bt_ref
  9.7 0.7 copy.22.ct_ref
  10.5 0.1 pad_add_fusion.core_ref.place.place_ref
  10.5 4.1 %all-to-all-done.got_ref = f32[8,2,16,192]{3,2,1,0:T(8,128)S(1)} async-done(((f32[8,2,16,192]{3,2,1,0:T(8,128)}), f32[8,2,16,192]{3,2,1,0:T(8,128)S(1)}, u32[]{:S(2)}, u32[]{:S(2)}) %all-to-all-start) | async-done | bytes 196640 | tf_op jit(solution)/shard_map/all_to_all | solution.py:438
  14.6 1.3 decays.1
  16.0 0.0 copy-start.7
  16.0 0.9 copy-done.7
  16.9 9.4 %chunk_states.1 = (f32[4,2,128,640]{3,2,1,0:T(8,128)}, f32[4,2,128,640]{3,2,1,0:T(8,128)}) custom-call(s32[2]{0:T(128)} %copy-done.18, bf16[192,5120]{1,0:T(8,128)(2,1)} %x_ref.4, bf16[192,5120]{1,0:T(8,128)(2,1)} %dy_ref.4, f32[8,192,16]{2,1,0:T(8,128)} %copy-done.7, bf16[128,192]{1,0:T(8,128)(2,1)} %copy.21.bt_ref, bf16[128,192]{1,0:T(8,128)(2,1)} %copy.22.ct_ref), custom_call_target="tpu_custom_call" | custom-call | tf_op jit(solution)/shard_map/chunk_states/pallas_call | solution.py:212
  26.3 1.1 collective-permute-start
  27.4 4.7 %collective-permute-done.come_ref = f32[4,2,128,640]{3,2,1,0:T(8,128)S(1)} collective-permute-done((f32[4,2,128,640]{3,2,1,0:T(8,128)}, f32[4,2,128,640]{3,2,1,0:T(8,128)S(1)}, u32[]{:S(2)}, u32[]{:S(2)}) %collective-permute-start) | collective-permute-done | bytes 2621472 | tf_op jit(solution)/shard_map/ppermute | solution.py:428
  32.1 2.7 %copy-done = f32[4,2,128,640]{3,2,1,0:T(8,128)S(1)} copy-done((f32[4,2,128,640]{3,2,1,0:T(8,128)S(1)}, f32[4,2,128,640]{3,2,1,0:T(8,128)}, u32[]{:S(2)}) %copy-start) | copy-done | bytes 2621464
  34.8 0.7 copy-done.19
  35.5 0.9 join.1
  36.4 0.4 collective-permute-start.1
  36.7 1.8 collective-permute-start.2
  38.5 0.7 collective-permute-start.3
  39.3 11.1 %within_chunk.1 = (f32[192,5120]{1,0:T(8,128)S(1)}, f32[192,5120]{1,0:T(8,128)S(1)}, f32[192,128]{1,0:T(8,128)S(1)}, f32[192,128]{1,0:T(8,128)S(1)}) custom-call(bf16[192,5120]{1,0:T(8,128)(2,1)S(1)} %copy-done.3, bf16[192,5120]{1,0:T(8,128)(2,1)S(1)} %copy-done.4, f32[8,192,16]{2,1,0:T(8,128)S(1)} %copy-done.8, ...), custom_call_target="tpu_custom_call" | custom-call | flops 20000000000 | bytes 12000000 | tf_op jit(solution)/shard_map/within_chunk/pallas_call | solution.py:108
  50.3 1.9 copy-done.5
  52.2 1.9 copy-done.6
  54.1 0.6 copy-done.16
  54.8 0.3 owner_decays.1.d_ref
  55.0 0.0 collective-permute-done.1.r1
  55.0 12.0 %collective-permute-done.2.r2 = f32[2,128,640]{2,1,0:T(8,128)S(1)} collective-permute-done((f32[2,128,640]{2,1,0:T(8,128)S(1)}, f32[2,128,640]{2,1,0:T(8,128)S(1)}, u32[]{:S(2)}, u32[]{:S(2)}) %collective-permute-start.2) | collective-permute-done | bytes 655392 | tf_op jit(solution)/shard_map/ppermute | solution.py:407
  67.1 0.9 collective-permute-done.3.r3
  68.0 1.0 totals.1
  69.0 0.0 copy-start.10
  69.0 0.9 copy-done.10
  69.9 10.8 %all-to-all-start.1 = ((f32[32,8,768]{2,1,0:T(8,128)}), f32[32,8,768]{2,1,0:T(8,128)S(1)}, u32[]{:S(2)}, u32[]{:S(2)}) async-start(f32[32,8,768]{2,1,0:T(8,128)} %copy-done.10), calls=%async_computation.1 | async-start | bytes 1572864 | tf_op jit(solution)/shard_map/all_to_all | solution.py:429
  80.7 20.7 %all-to-all-done.1.p_ref = f32[32,8,768]{2,1,0:T(8,128)S(1)} async-done(((f32[32,8,768]{2,1,0:T(8,128)}), f32[32,8,768]{2,1,0:T(8,128)S(1)}, u32[]{:S(2)}, u32[]{:S(2)}) %all-to-all-start.1) | async-done | bytes 786464 | tf_op jit(solution)/shard_map/all_to_all | solution.py:429
  101.4 0.1 chain.1
  101.5 24.3 %all_to_all.15.edge_ref = f32[32,8,640]{2,1,0:T(8,128)S(1)} all-to-all(f32[32,8,640]{2,1,0:T(8,128)S(1)} %chain.1), channel_id=1, replica_groups=mesh['x'=4,'z'=8,'y'=4,'core'=2] {'x','z'}, dimensions={0} | all-to-all | bytes 1310720 | tf_op jit(solution)/shard_map/all_to_all | solution.py:429
  125.8 1.2 entering.1
  127.0 1.8 collective-permute-start.4
  128.8 3.1 %collective-permute-start.5 = (bf16[2,192,640]{2,1,0:T(8,128)(2,1)S(1)}, bf16[2,192,640]{2,1,0:T(8,128)(2,1)S(1)}, u32[]{:S(2)}, u32[]{:S(2)}) collective-permute-start(bf16[2,192,640]{2,1,0:T(8,128)(2,1)S(1)} %get-tuple-element.70), channel_id=1, source_target_pairs={{0,4},{2,6},{4,0},{6,2},{1,5},{3,7},{5,1},{7,3},{8,12},{10,14},{12... | collective-permute-start | bytes 1474568 | tf_op jit(solution)/shard_map/ppermute | solution.py:407
  131.9 7.1 %collective-permute-done.4.r1 = bf16[2,192,640]{2,1,0:T(8,128)(2,1)S(1)} collective-permute-done((bf16[2,192,640]{2,1,0:T(8,128)(2,1)S(1)}, bf16[2,192,640]{2,1,0:T(8,128)(2,1)S(1)}, u32[]{:S(2)}, u32[]{:S(2)}) %collective-permute-start.4) | collective-permute-done | bytes 491552 | tf_op jit(solution)/shard_map/ppermute | solution.py:407
  138.9 11.4 %collective-permute-done.5.r2 = bf16[2,192,640]{2,1,0:T(8,128)(2,1)S(1)} collective-permute-done((bf16[2,192,640]{2,1,0:T(8,128)(2,1)S(1)}, bf16[2,192,640]{2,1,0:T(8,128)(2,1)S(1)}, u32[]{:S(2)}, u32[]{:S(2)}) %collective-permute-start.5) | collective-permute-done | bytes 491552 | tf_op jit(solution)/shard_map/ppermute | solution.py:407
  150.3 2.2 %collective-permute-done.6.r3 = bf16[2,192,640]{2,1,0:T(8,128)(2,1)S(1)} collective-permute-done((bf16[2,192,640]{2,1,0:T(8,128)(2,1)S(1)}, bf16[2,192,640]{2,1,0:T(8,128)(2,1)S(1)}, u32[]{:S(2)}, u32[]{:S(2)}) %collective-permute-start.6) | collective-permute-done | bytes 491552 | tf_op jit(solution)/shard_map/ppermute | solution.py:407
  152.5 2.5 %fork.1 = (f32[4,2,128,640]{3,2,1,0:T(8,128)S(1)}, f32[4,2,128,640]{3,2,1,0:T(8,128)S(1)}) custom-call(s32[2]{0:T(128)S(1)} %copy-done.20, bf16[2,192,640]{2,1,0:T(8,128)(2,1)S(1)} %get-tuple-element.68.r0, bf16[2,192,640]{2,1,0:T(8,128)(2,1)S(1)} %collective-permute-done.4.r1, bf16[2,192,640]{2,1,0:T(8,128)(2,1)S(1)} %collective-permute-done.5.r2, ...), custom_call_target="tpu_custom_call" | custom-call | tf_op jit(solution)/shard_map/fork/pallas_call | solution.py:138
  155.1 1.6 copy-done.9
  156.6 2.0 %collective-permute-start.7 = (f32[4,2,128,640]{3,2,1,0:T(8,128)S(1)}, f32[4,2,128,640]{3,2,1,0:T(8,128)}, u32[]{:S(2)}, u32[]{:S(2)}) collective-permute-start(f32[4,2,128,640]{3,2,1,0:T(8,128)S(1)} %get-tuple-element.73), channel_id=1, source_target_pairs={{0,1},{1,0},{2,3},{3,2},{4,5},{5,4},{6,7},{7,6},{8,9},{9,8},{10,11... | collective-permute-start | bytes 7864328 | tf_op jit(solution)/shard_map/ppermute | solution.py:428
  158.7 4.7 %collective-permute-done.7.come_ref = f32[4,2,128,640]{3,2,1,0:T(8,128)} collective-permute-done((f32[4,2,128,640]{3,2,1,0:T(8,128)S(1)}, f32[4,2,128,640]{3,2,1,0:T(8,128)}, u32[]{:S(2)}, u32[]{:S(2)}) %collective-permute-start.7) | collective-permute-done | bytes 2621472 | tf_op jit(solution)/shard_map/ppermute | solution.py:428
  163.3 15.4 %finish.1 = (bf16[192,5120]{1,0:T(8,128)(2,1)}, bf16[192,5120]{1,0:T(8,128)(2,1)}, f32[448,128]{1,0:T(8,128)}, f32[448,128]{1,0:T(8,128)}, f32[448,128]{1,0:T(8,128)}, /*index=5*/f32[448,128]{1,0:T(8,128)}) custom-call(s32[2]{0:T(128)} %copy-done.18, bf16[192,5120]{1,0:T(8,128)(2,1)} %x_ref.4, bf16[192,5120]{1,0:T(8,128)(2,1)} %dy_ref.4, ...), custom_call_target="tpu_custom_call" | custom-call | tf_op jit(solution)/shard_map/finish/pallas_call | solution.py:381
  178.7 0.0 copy-start.23
  178.7 2.0 collective-permute-start.8
  180.7 0.7 collective-permute-start.10
  181.4 1.0 bitcast_dynamic-update-slice_fusion.6
  182.3 3.5 %collective-permute-done.8 = f32[448,128]{1,0:T(8,128)S(1)} collective-permute-done((f32[448,128]{1,0:T(8,128)}, f32[448,128]{1,0:T(8,128)S(1)}, u32[]{:S(2)}, u32[]{:S(2)}) %collective-permute-start.8) | collective-permute-done | bytes 229408 | tf_op jit(solution)/shard_map/ppermute | solution.py:407
  185.9 3.1 %collective-permute-done.9 = f32[448,128]{1,0:T(8,128)S(1)} collective-permute-done((f32[448,128]{1,0:T(8,128)}, f32[448,128]{1,0:T(8,128)S(1)}, u32[]{:S(2)}, u32[]{:S(2)}) %collective-permute-start.9) | collective-permute-done | bytes 229408 | tf_op jit(solution)/shard_map/ppermute | solution.py:407
  189.0 5.2 %collective-permute-done.10 = f32[448,128]{1,0:T(8,128)S(1)} collective-permute-done((f32[448,128]{1,0:T(8,128)}, f32[448,128]{1,0:T(8,128)S(1)}, u32[]{:S(2)}, u32[]{:S(2)}) %collective-permute-start.10) | collective-permute-done | bytes 229408 | tf_op jit(solution)/shard_map/ppermute | solution.py:407
  194.4 0.1 constant_dynamic-slice_fusion
  194.4 0.9 collective-permute-start.11
  195.3 2.2 %collective-permute-done.11 = f32[4,448,128]{2,1,0:T(8,128)} collective-permute-done((f32[4,448,128]{2,1,0:T(8,128)S(1)}, f32[4,448,128]{2,1,0:T(8,128)}, u32[]{:S(2)}, u32[]{:S(2)}) %collective-permute-start.11) | collective-permute-done | bytes 917536 | tf_op jit(solution)/shard_map/ppermute | solution.py:415
  197.6 1.3 select_bitcast_fusion.1
  198.9 0.1 pad_maximum_fusion
  199.0 0.1 copy.23
  199.2 1.3 fusion
  200.5 0.1 copy.25
  200.6 0.7 reshape.36
  (48 shorter events, 0.3 us)
Async XLA Ops:
  0.6 0.9 copy-start.13
  1.5 0.7 copy-start.22
  3.0 11.6 %all-to-all-start = ((f32[8,2,16,192]{3,2,1,0:T(8,128)}), f32[8,2,16,192]{3,2,1,0:T(8,128)S(1)}, u32[]{:S(2)}, u32[]{:S(2)}) async-start(f32[8,2,16,192]{3,2,1,0:T(8,128)} %pack.1), calls=%async_computation | async-start | bytes 524288 | tf_op jit(solution)/shard_map/all_to_all | solution.py:438
  9.0 30.3 %copy-start.11 = (bf16[192,128]{1,0:T(8,128)(2,1)}, bf16[192,128]{1,0:T(8,128)(2,1)S(1)}, u32[]{:S(2)}) copy-start(bf16[192,128]{1,0:T(8,128)(2,1)S(1)} %get-tuple-element.87.c_ref) | copy-start | bytes 147460
  9.0 30.3 %copy-start.12 = (bf16[192,128]{1,0:T(8,128)(2,1)}, bf16[192,128]{1,0:T(8,128)(2,1)S(1)}, u32[]{:S(2)}) copy-start(bf16[192,128]{1,0:T(8,128)(2,1)S(1)} %get-tuple-element.88.b_ref) | copy-start | bytes 147460
  10.5 6.3 %copy-start.18 = (s32[2]{0:T(128)}, s32[2]{0:T(128)S(1)}, u32[]{:S(2)}) copy-start(s32[2]{0:T(128)S(1)} %pad_add_fusion.core_ref.place.place_ref) | copy-start | bytes 28
  16.0 0.9 copy-start.7
  16.9 9.5 %copy-start.21 = (f32[8,1,640]{2,1,0:T(1,128)}, f32[8,1,640]{2,1,0:T(1,128)S(1)}, u32[]{:S(2)}) copy-start(f32[8,1,640]{2,1,0:T(1,128)S(1)} %get-tuple-element.74.gain_ref) | copy-start | bytes 61444
  16.9 22.4 %copy-start.15 = (f32[8,16,192]{2,1,0:T(8,128)}, f32[8,16,192]{2,1,0:T(8,128)S(1)}, u32[]{:S(2)}) copy-start(f32[8,16,192]{2,1,0:T(8,128)S(1)} %get-tuple-element.45.cumt_ref) | copy-start | bytes 294916
  26.3 5.8 %collective-permute-start = (f32[4,2,128,640]{3,2,1,0:T(8,128)}, f32[4,2,128,640]{3,2,1,0:T(8,128)S(1)}, u32[]{:S(2)}, u32[]{:S(2)}) collective-permute-start(f32[4,2,128,640]{3,2,1,0:T(8,128)} %get-tuple-element.47), channel_id=1, source_target_pairs={{0,1},{1,0},{2,3},{3,2},{4,5},{5,4},{6,7},{7,6},{8,9},{9,8},{10,11... | collective-permute-start | bytes 7864328 | tf_op jit(solution)/shard_map/ppermute | solution.py:428
  32.1 4.3 %copy-start.2 = (f32[4,2,128,640]{3,2,1,0:T(8,128)}, f32[4,2,128,640]{3,2,1,0:T(8,128)S(1)}, u32[]{:S(2)}) copy-start(f32[4,2,128,640]{3,2,1,0:T(8,128)S(1)} %collective-permute-done.come_ref) | copy-start | bytes 7864324
  32.1 2.7 %copy-start = (f32[4,2,128,640]{3,2,1,0:T(8,128)S(1)}, f32[4,2,128,640]{3,2,1,0:T(8,128)}, u32[]{:S(2)}) copy-start(f32[4,2,128,640]{3,2,1,0:T(8,128)} %get-tuple-element.46.keep_ref) | copy-start | bytes 7864324
  34.8 0.7 copy-start.19
  35.5 3.8 %copy-start.3 = (bf16[192,5120]{1,0:T(8,128)(2,1)S(1)}, bf16[192,5120]{1,0:T(8,128)(2,1)}, u32[]{:S(2)}) copy-start(bf16[192,5120]{1,0:T(8,128)(2,1)} %x_ref.4) | copy-start | bytes 5898244
  35.5 3.8 %copy-start.4 = (bf16[192,5120]{1,0:T(8,128)(2,1)S(1)}, bf16[192,5120]{1,0:T(8,128)(2,1)}, u32[]{:S(2)}) copy-start(bf16[192,5120]{1,0:T(8,128)(2,1)} %dy_ref.4) | copy-start | bytes 5898244
  35.5 3.8 %copy-start.8 = (f32[8,192,16]{2,1,0:T(8,128)S(1)}, f32[8,192,16]{2,1,0:T(8,128)}, u32[]{:S(2)}) copy-start(f32[8,192,16]{2,1,0:T(8,128)} %copy-done.7) | copy-start | bytes 294916
  36.4 18.7 %collective-permute-start.1 = (f32[2,128,640]{2,1,0:T(8,128)S(1)}, f32[2,128,640]{2,1,0:T(8,128)S(1)}, u32[]{:S(2)}, u32[]{:S(2)}) collective-permute-start(f32[2,128,640]{2,1,0:T(8,128)S(1)} %get-tuple-element.56), channel_id=1, source_target_pairs={{0,2},{2,4},{4,6},{6,0},{1,3},{3,5},{5,7},{7,1},{8,10},{10,12},{12... | collective-permute-start | bytes 1966088 | tf_op jit(solution)/shard_map/ppermute | solution.py:407
  36.7 30.4 %collective-permute-start.2 = (f32[2,128,640]{2,1,0:T(8,128)S(1)}, f32[2,128,640]{2,1,0:T(8,128)S(1)}, u32[]{:S(2)}, u32[]{:S(2)}) collective-permute-start(f32[2,128,640]{2,1,0:T(8,128)S(1)} %get-tuple-element.57), channel_id=1, source_target_pairs={{0,4},{2,6},{4,0},{6,2},{1,5},{3,7},{5,1},{7,3},{8,12},{10,14},{12... | collective-permute-start | bytes 1966088 | tf_op jit(solution)/shard_map/ppermute | solution.py:407
  38.5 29.5 %collective-permute-start.3 = (f32[2,128,640]{2,1,0:T(8,128)S(1)}, f32[2,128,640]{2,1,0:T(8,128)S(1)}, u32[]{:S(2)}, u32[]{:S(2)}) collective-permute-start(f32[2,128,640]{2,1,0:T(8,128)S(1)} %get-tuple-element.58), channel_id=1, source_target_pairs={{0,6},{2,0},{4,2},{6,4},{1,7},{3,1},{5,3},{7,5},{8,14},{10,8},{12,... | collective-permute-start | bytes 1966088 | tf_op jit(solution)/shard_map/ppermute | solution.py:407
  39.3 15.5 %copy-start.14 = (f32[1536,10]{0,1:T(8,128)S(1)}, f32[1536,10]{0,1:T(8,128)}, u32[]{:S(2)}) copy-start(f32[1536,10]{0,1:T(8,128)} %param.10) | copy-start | bytes 184324
  50.3 1.9 copy-start.5
  52.2 1.9 copy-start.6
  54.1 0.6 copy-start.16
  54.8 14.3 %copy-start.17 = (f32[192,128]{1,0:T(8,128)}, f32[192,128]{1,0:T(8,128)S(1)}, u32[]{:S(2)}) copy-start(f32[192,128]{1,0:T(8,128)S(1)} %get-tuple-element.76.dc0_ref) | copy-start | bytes 294916
  69.0 0.9 copy-start.10
  69.9 55.8 %copy-start.20 = (s32[2]{0:T(128)S(1)}, s32[2]{0:T(128)}, u32[]{:S(2)}) copy-start(s32[2]{0:T(128)} %copy-done.18) | copy-start | bytes 28
  69.9 31.4 %all-to-all-start.1 = ((f32[32,8,768]{2,1,0:T(8,128)}), f32[32,8,768]{2,1,0:T(8,128)S(1)}, u32[]{:S(2)}, u32[]{:S(2)}) async-start(f32[32,8,768]{2,1,0:T(8,128)} %copy-done.10), calls=%async_computation.1 | async-start | bytes 1572864 | tf_op jit(solution)/shard_map/all_to_all | solution.py:429
  125.7 26.8 %copy-start.1 = (f32[4,2,128,640]{3,2,1,0:T(8,128)S(1)}, f32[4,2,128,640]{3,2,1,0:T(8,128)}, u32[]{:S(2)}) copy-start(f32[4,2,128,640]{3,2,1,0:T(8,128)} %get-tuple-element.46.keep_ref) | copy-start | bytes 7864324
  127.0 11.9 %collective-permute-start.4 = (bf16[2,192,640]{2,1,0:T(8,128)(2,1)S(1)}, bf16[2,192,640]{2,1,0:T(8,128)(2,1)S(1)}, u32[]{:S(2)}, u32[]{:S(2)}) collective-permute-start(bf16[2,192,640]{2,1,0:T(8,128)(2,1)S(1)} %get-tuple-element.69), channel_id=1, source_target_pairs={{0,2},{2,4},{4,6},{6,0},{1,3},{3,5},{5,7},{7,1},{8,10},{10,12},{12... | collective-permute-start | bytes 1474568 | tf_op jit(solution)/shard_map/ppermute | solution.py:407
  128.8 21.6 %collective-permute-start.5 = (bf16[2,192,640]{2,1,0:T(8,128)(2,1)S(1)}, bf16[2,192,640]{2,1,0:T(8,128)(2,1)S(1)}, u32[]{:S(2)}, u32[]{:S(2)}) collective-permute-start(bf16[2,192,640]{2,1,0:T(8,128)(2,1)S(1)} %get-tuple-element.70), channel_id=1, source_target_pairs={{0,4},{2,6},{4,0},{6,2},{1,5},{3,7},{5,1},{7,3},{8,12},{10,14},{12... | collective-permute-start | bytes 1474568 | tf_op jit(solution)/shard_map/ppermute | solution.py:407
  131.9 20.7 %collective-permute-start.6 = (bf16[2,192,640]{2,1,0:T(8,128)(2,1)S(1)}, bf16[2,192,640]{2,1,0:T(8,128)(2,1)S(1)}, u32[]{:S(2)}, u32[]{:S(2)}) collective-permute-start(bf16[2,192,640]{2,1,0:T(8,128)(2,1)S(1)} %get-tuple-element.71), channel_id=1, source_target_pairs={{0,6},{2,0},{4,2},{6,4},{1,7},{3,1},{5,3},{7,5},{8,14},{10,8},{12,... | collective-permute-start | bytes 1474568 | tf_op jit(solution)/shard_map/ppermute | solution.py:407
  155.1 1.6 copy-start.9
  156.6 6.7 %collective-permute-start.7 = (f32[4,2,128,640]{3,2,1,0:T(8,128)S(1)}, f32[4,2,128,640]{3,2,1,0:T(8,128)}, u32[]{:S(2)}, u32[]{:S(2)}) collective-permute-start(f32[4,2,128,640]{3,2,1,0:T(8,128)S(1)} %get-tuple-element.73), channel_id=1, source_target_pairs={{0,1},{1,0},{2,3},{3,2},{4,5},{5,4},{6,7},{7,6},{8,9},{9,8},{10,11... | collective-permute-start | bytes 7864328 | tf_op jit(solution)/shard_map/ppermute | solution.py:428
  178.7 15.5 %copy-start.23 = (f32[448,128]{1,0:T(8,128)S(1)}, f32[448,128]{1,0:T(8,128)}, u32[]{:S(2)}) copy-start(f32[448,128]{1,0:T(8,128)} %get-tuple-element.79) | copy-start | bytes 688132
  178.7 7.1 %collective-permute-start.8 = (f32[448,128]{1,0:T(8,128)}, f32[448,128]{1,0:T(8,128)S(1)}, u32[]{:S(2)}, u32[]{:S(2)}) collective-permute-start(f32[448,128]{1,0:T(8,128)} %get-tuple-element.80), channel_id=1, source_target_pairs={{0,6},{2,0},{4,2},{6,4},{1,7},{3,1},{5,3},{7,5},{8,14},{10,8},{12,... | collective-permute-start | bytes 688136 | tf_op jit(solution)/shard_map/ppermute | solution.py:407
  180.7 8.3 %collective-permute-start.9 = (f32[448,128]{1,0:T(8,128)}, f32[448,128]{1,0:T(8,128)S(1)}, u32[]{:S(2)}, u32[]{:S(2)}) collective-permute-start(f32[448,128]{1,0:T(8,128)} %get-tuple-element.81), channel_id=1, source_target_pairs={{0,4},{2,6},{4,0},{6,2},{1,5},{3,7},{5,1},{7,3},{8,12},{10,14},{12... | collective-permute-start | bytes 688136 | tf_op jit(solution)/shard_map/ppermute | solution.py:407
  180.7 13.5 %collective-permute-start.10 = (f32[448,128]{1,0:T(8,128)}, f32[448,128]{1,0:T(8,128)S(1)}, u32[]{:S(2)}, u32[]{:S(2)}) collective-permute-start(f32[448,128]{1,0:T(8,128)} %get-tuple-element.82), channel_id=1, source_target_pairs={{0,2},{2,4},{4,6},{6,0},{1,3},{3,5},{5,7},{7,1},{8,10},{10,12},{12... | collective-permute-start | bytes 688136 | tf_op jit(solution)/shard_map/ppermute | solution.py:407
  194.4 3.1 %collective-permute-start.11 = (f32[4,448,128]{2,1,0:T(8,128)S(1)}, f32[4,448,128]{2,1,0:T(8,128)}, u32[]{:S(2)}, u32[]{:S(2)}) collective-permute-start(f32[4,448,128]{2,1,0:T(8,128)S(1)} %constant_dynamic-slice_fusion), channel_id=1, source_target_pairs={{0,1},{1,0},{2,3},{3,2},{4,5},{5,4},{6,7},{7,6},{8,9},{9,8},{10,11... | collective-permute-start | bytes 2752520 | tf_op jit(solution)/shard_map/ppermute | solution.py:415

commit v3 on v2

--- a/solution.py
+++ b/solution.py
@@ -284,25 +284,46 @@
             out[way, N:] = low[:LOWS]
 
 
-def fork_kernel(place_ref, r0, r1, r2, r3, keep_ref, come_ref, kept_ref, mine_ref, send_ref):
-    low = place_ref[0] == 0
-    for turn, ref in enumerate((r0, r1, r2, r3)):
-        j = lax.rem(place_ref[1] - turn + CHIPS, CHIPS)
-        for way in range(2):
-            direct_is_mine = low if way == 0 else jnp.logical_not(low)
-            low_rows = jnp.concatenate(
-                [ref[way, N:].astype(F32), jnp.zeros((N - LOWS, GC), F32)], axis=0
-            )
-            direct = ref[way, :N].astype(F32) + low_rows
-            passed = jnp.where(direct_is_mine, keep_ref[j, way], come_ref[j, way])
-            through = kept_ref[way, j] * direct + passed
-            mine_ref[j, way] = jnp.where(direct_is_mine, direct, through)
-            send_ref[j, way] = jnp.where(direct_is_mine, through, direct)
+def fork_kernel(place, r_ref, keep_ref, come_ref, kept_ref, mine_ref, send_ref):
+    low = place[0] == 0
+    for way in range(2):
+        direct_is_mine = low if way == 0 else jnp.logical_not(low)
+        low_rows = jnp.concatenate(
+            [r_ref[way, N:].astype(F32), jnp.zeros((N - LOWS, GC), F32)], axis=0
+        )
+        direct = r_ref[way, :N].astype(F32) + low_rows
+        passed = jnp.where(direct_is_mine, keep_ref[0, way], come_ref[0, way])
+        through = kept_ref[way, 0] * direct + passed
+        mine_ref[way] = jnp.where(direct_is_mine, direct, through)
+        send_ref[way] = jnp.where(direct_is_mine, through, direct)
+
+
+def fork(turn, place, r, keep, come, kept):
+    source = lambda place: lax.rem(place[1] - turn + CHIPS, CHIPS)
+    quad = pl.BlockSpec((1, *PAIR), lambda s, place: (source(place), 0, 0, 0))
+    pair = pl.BlockSpec(PAIR, lambda s, place: (0, 0, 0))
+    return pl.pallas_call(
+        fork_kernel,
+        grid_spec=pltpu.PrefetchScalarGridSpec(
+            num_scalar_prefetch=1,
+            grid=(1,),
+            in_specs=[
+                pl.BlockSpec((2, N + LOWS, GC), lambda s, place: (0, 0, 0)),
+                quad,
+                quad,
+                pl.BlockSpec((2, 1, 1, GC), lambda s, place: (0, source(place), 0, 0)),
+            ],
+            out_specs=[pair, pair],
+        ),
+        out_shape=[jax.ShapeDtypeStruct(PAIR, F32)] * 2,
+        compiler_params=pltpu.CompilerParams(vmem_limit_bytes=40 << 20),
+        name="fork",
+    )(place, r, keep, come, kept)
 
 
 def finish_kernel(
-    place, x_ref, dy_ref, cum_ref, cumt_ref, y_ref, dx_ref, mine_ref, come_ref, gain_ref, b_ref, c_ref,
-    db0_ref, dc0_ref, out_ref, gs_ref, o0, o1, o2, o3, db_ref, dc_ref, gd_ref,
+    place, x_ref, dy_ref, cum_ref, y_ref, dx_ref, m0, m1, m2, m3, c0, c1, c2, c3, gain_ref, b_ref, c_ref,
+    db0_ref, dc0_ref, out_ref, gs_ref, o0, o1, o2, o3, db_ref, dc_ref, gd_ref, mine_ref, come_ref,
 ):
     step = pl.program_id(0)
     low_core = place[0] == 0
@@ -312,8 +333,15 @@
         db_ref[...] = db0_ref[...]
         dc_ref[...] = dc0_ref[...]
 
+    for turn, (mine_in, come_in) in enumerate(((m0, c0), (m1, c1), (m2, c2), (m3, c3))):
+
+        @pl.when(step == turn)
+        def _(mine_in=mine_in, come_in=come_in):
+            mine_ref[...] = mine_in[...]
+            come_ref[...] = come_in[...]
+
     def both(way):
-        mine, come = mine_ref[0, way], come_ref[0, way]
+        mine, come = mine_ref[way], come_ref[way]
         return jnp.concatenate([jnp.where(low_core, mine, come), jnp.where(low_core, come, mine)], axis=1)
 
     cums = cum_ref[0], cum_ref[1]
@@ -359,7 +387,7 @@
     gd = jnp.broadcast_to(by_head(jnp.broadcast_to(row, (8, 2 * GC)))[:, 0:1], (32, ROWS))
     for part in thirds(by_head(dy * y - (x * dx_in + x_dx))):
         gd += dot(part, after)
-    gd_ref[step] = gd
+    gd_ref[lax.rem(place[1] - step + CHIPS, CHIPS)] = gd
 
     @pl.when(step == CHIPS - 1)
     def _():
@@ -372,10 +400,11 @@
             out[416:448, 64:128] = jnp.zeros((32, 64), F32)
 
 
-def finish(place, x, dy, cum, cumt, y, dx, mine, come, gain, b, c, db, dc):
-    columns = pl.BlockSpec((ROWS, 2 * GC), lambda s, place: (0, s))
-    by_chip = lambda *shape: pl.BlockSpec((2, *shape), lambda s, place: (s, 0, 0))
-    quad = pl.BlockSpec((1, *PAIR), lambda s, place: (s, 0, 0, 0))
+def finish(place, x, dy, cum, y, dx, mine, come, gain, b, c, db, dc):
+    source = lambda s, place: lax.rem(place[1] - s + CHIPS, CHIPS)
+    columns = pl.BlockSpec((ROWS, 2 * GC), lambda s, place: (0, source(s, place)))
+    by_chip = lambda *shape: pl.BlockSpec((2, *shape), lambda s, place: (source(s, place), 0, 0))
+    pair = pl.BlockSpec(PAIR, lambda s, place: (0, 0, 0))
     whole = lambda *shape: pl.BlockSpec(shape, lambda s, place: (0, 0))
     wide = jax.ShapeDtypeStruct((ROWS, GC * GROUPS), BF16)
     return pl.pallas_call(
@@ -384,18 +413,19 @@
             num_scalar_prefetch=1,
             grid=(CHIPS,),
             in_specs=[
-                columns, columns, by_chip(ROWS, 16), by_chip(16, ROWS), columns, columns, quad, quad,
+                columns, columns, by_chip(ROWS, 16), columns, columns, *[pair] * 8,
                 by_chip(1, GC), *[whole(ROWS, N)] * 4,
             ],
             out_specs=[columns, columns] + [whole(448, 128)] * 4,
             scratch_shapes=[
                 pltpu.VMEM((ROWS, N), F32), pltpu.VMEM((ROWS, N), F32), pltpu.VMEM((CHIPS, 32, ROWS), F32),
+                pltpu.VMEM(PAIR, F32), pltpu.VMEM(PAIR, F32),
             ],
         ),
         out_shape=[wide, wide] + [jax.ShapeDtypeStruct((448, 128), F32)] * 4,
         compiler_params=pltpu.CompilerParams(vmem_limit_bytes=60 << 20),
         name="finish",
-    )(place, x, dy, cum, cumt, y, dx, mine, come, gain, b, c, db, dc)
+    )(place, x, dy, cum, y, dx, *mine, *come, gain, b, c, db, dc)
 
 
 def tie(*values):
@@ -467,9 +497,13 @@
         entering_kernel, "entering", [jax.ShapeDtypeStruct((2, N + LOWS, GC), BF16)] * 4, place, by_chip, own, edge,
         scratch=[pltpu.VMEM((CHIPS, *PAIR), F32)],
     )
-    mine, send = on_chip(fork_kernel, "fork", [quad] * 2, place, *turned(out), keep, come, kept)
+    mine, come_in = [], []
+    for turn, r in enumerate(turned(out)):
+        own_part, send = fork(turn, place, r, keep, come, kept)
+        mine.append(own_part)
+        come_in.append(swap(send))
     scan_out, grad_x, *ends = finish(
-        place, x, dy, cum, cumt, y_in, dx_in, mine, swap(send), gain, b, c, db_in, dc_in
+        place, x, dy, cum, y_in, dx_in, mine, come_in, gain, b, c, db_in, dc_in
     )
     ends = gathered(turned(ends), iy, core == 0)
     grad_b = ends[:, :ROWS].reshape(GROUPS * ROWS, N)

time: 202 us -> 206 us (1.020)
  waiting for transfers between devices: 81.9 us -> 60.2 us
  starting transfers between devices: 30.3 us -> 46.7 us
  Pallas kernels: 44 us -> 49.8 us
  local copies, waits for them, and re-layouts: 18.4 us -> 21.8 us
    ppermute x9, waiting for transfers between devices: 45.5 us -> 26.5 us  [turned(): lax.ppermute(v[turn], 'y', [(i, (i + turn) % CHIPS) for i in range(CHIPS)])]
    ppermute x2 -> x5, starting transfers between devices: 3.08 us -> 18.5 us  [shards(): swap = lambda v: lax.ppermute(v, 'core', SWAP)]
    pallas_call x0 -> x4, Pallas kernels: none -> 6.74 us  [fork(): pl.pallas_call(fork_kernel, grid_spec=pltpu.PrefetchScalarGridSpec(num_sc...]
    unnamed x55 -> x63, local copies, waits for them, and re-layouts: 13.7 us -> 17.1 us
    ppermute x2 -> x5, waiting for transfers between devices: 9.41 us -> 6.68 us  [shards(): swap = lambda v: lax.ppermute(v, 'core', SWAP)]
    pallas_call x8 -> x7, Pallas kernels: 8.12 us -> 5.62 us  [on_chip(): pl.pallas_call(kernel, in_specs=[SMEM] * scalars + [VMEM] * (len(args) -...]
  transfers between devices with their start and end apart: 14 -> 17, of which waited for: 13 -> 10; matrix products, arithmetic and copies ran while one was open for 2% -> 2% of each run, Pallas kernels for 6% -> 9%
where the time goes in v3:
time: 206 us; the launch traced here: 205 us
  waiting for transfers between devices  60.2 us (29%)
  Pallas kernels  49.8 us (24%)
  starting transfers between devices  46.7 us (23%)
  blocking collectives  24.4 us (12%)
  local copies, waits for them, and re-layouts  21.8 us (11%)
    ppermute x9, waiting for transfers between devices, turned(): lax.ppermute(v[turn], 'y', [(i, (i + turn) % CHIPS) for i in range(CHIPS)])  26.5 us
    all_to_all x1, blocking collectives, shards(): lax.all_to_all(v, ('x', 'z'), split_axis=0, concat_axis=0, tiled=True)  24.4 us
    all_to_all x1, waiting for transfers between devices, shards(): lax.all_to_all(v, ('x', 'z'), split_axis=0, concat_axis=0, tiled=True)  20.7 us
    ppermute x5, starting transfers between devices, shards(): swap = lambda v: lax.ppermute(v, 'core', SWAP)  18.5 us
    unnamed x63, local copies, waits for them, and re-layouts  17.1 us
    pallas_call x1, Pallas kernels, finish(): pl.pallas_call(finish_kernel, grid_spec=pltpu.PrefetchScalarGridSpec(num_...  16.9 us
    ppermute x9, starting transfers between devices, turned(): lax.ppermute(v[turn], 'y', [(i, (i + turn) % CHIPS) for i in range(CHIPS)])  11.4 us
    pallas_call x1, Pallas kernels, within(): pl.pallas_call(within_kernel, grid=(GROUPS,), in_specs=[by_column, by_col...  11.1 us
  transfers between devices with their start and end apart: 17, of which 10 were waited for; matrix products, arithmetic and copies ran while one was open for 2% of the time, Pallas kernels for 9%

profile of v3, /device:TPU:33, one launch (start us, length us, event | category | flops | bytes accessed | tf_op | source)
XLA Modules:
  0.0 205.3 jit_solution(2681435956221247126)
XLA Ops:
  0.6 0.9 copy-done.17
  1.5 0.7 copy-done.25
  2.2 0.8 pack.1
  3.0 5.1 %all-to-all-start = ((f32[8,2,16,192]{3,2,1,0:T(8,128)}), f32[8,2,16,192]{3,2,1,0:T(8,128)S(1)}, u32[]{:S(2)}, u32[]{:S(2)}) async-start(f32[8,2,16,192]{3,2,1,0:T(8,128)} %pack.1), calls=%async_computation | async-start | bytes 524288 | tf_op jit(solution)/shard_map/all_to_all | solution.py:468
  8.1 0.8 constant_dynamic-slice_fusion.1
  9.0 0.7 copy.21.bt_ref
  9.7 0.7 copy.22.ct_ref
  10.5 0.1 pad_add_fusion.core_ref.place.place_ref
  10.5 4.1 %all-to-all-done.got_ref = f32[8,2,16,192]{3,2,1,0:T(8,128)S(1)} async-done(((f32[8,2,16,192]{3,2,1,0:T(8,128)}), f32[8,2,16,192]{3,2,1,0:T(8,128)S(1)}, u32[]{:S(2)}, u32[]{:S(2)}) %all-to-all-start) | async-done | bytes 196640 | tf_op jit(solution)/shard_map/all_to_all | solution.py:468
  14.6 1.3 decays.1
  16.0 0.9 copy-done.6
  16.9 9.4 %chunk_states.1 = (f32[4,2,128,640]{3,2,1,0:T(8,128)}, f32[4,2,128,640]{3,2,1,0:T(8,128)}) custom-call(s32[2]{0:T(128)} %copy-done.21, bf16[192,5120]{1,0:T(8,128)(2,1)} %x_ref.4, bf16[192,5120]{1,0:T(8,128)(2,1)} %dy_ref.4, f32[8,192,16]{2,1,0:T(8,128)} %copy-done.6, bf16[128,192]{1,0:T(8,128)(2,1)} %copy.21.bt_ref, bf16[128,192]{1,0:T(8,128)(2,1)} %copy.22.ct_ref), custom_call_target="tpu_custom_call" | custom-call | tf_op jit(solution)/shard_map/chunk_states/pallas_call | solution.py:212
  26.3 1.1 collective-permute-start
  27.3 4.7 %collective-permute-done.come_ref = f32[4,2,128,640]{3,2,1,0:T(8,128)S(1)} collective-permute-done((f32[4,2,128,640]{3,2,1,0:T(8,128)}, f32[4,2,128,640]{3,2,1,0:T(8,128)S(1)}, u32[]{:S(2)}, u32[]{:S(2)}) %collective-permute-start) | collective-permute-done | bytes 2621472 | tf_op jit(solution)/shard_map/ppermute | solution.py:458
  32.1 1.7 copy-done
  33.8 0.6 copy-done.22
  34.5 0.9 join.1
  35.4 0.4 collective-permute-start.1
  35.7 1.8 collective-permute-start.2
  37.5 0.7 collective-permute-start.3
  38.3 11.1 %within_chunk.1 = (f32[192,5120]{1,0:T(8,128)S(1)}, f32[192,5120]{1,0:T(8,128)S(1)}, f32[192,128]{1,0:T(8,128)S(1)}, f32[192,128]{1,0:T(8,128)S(1)}) custom-call(bf16[192,5120]{1,0:T(8,128)(2,1)S(1)} %copy-done.2, bf16[192,5120]{1,0:T(8,128)(2,1)S(1)} %copy-done.3, f32[8,192,16]{2,1,0:T(8,128)S(1)} %copy-done.7, ...), custom_call_target="tpu_custom_call" | custom-call | flops 20000000000 | bytes 12000000 | tf_op jit(solution)/shard_map/within_chunk/pallas_call | solution.py:108
  49.4 1.9 copy-done.4
  51.3 2.0 copy-done.5
  53.2 0.6 copy-done.19
  53.8 0.3 owner_decays.1.d_ref
  54.1 12.0 %collective-permute-done.2.r2 = f32[2,128,640]{2,1,0:T(8,128)S(1)} collective-permute-done((f32[2,128,640]{2,1,0:T(8,128)S(1)}, f32[2,128,640]{2,1,0:T(8,128)S(1)}, u32[]{:S(2)}, u32[]{:S(2)}) %collective-permute-start.2) | collective-permute-done | bytes 655392 | tf_op jit(solution)/shard_map/ppermute | solution.py:437
  66.1 0.9 collective-permute-done.3.r3
  67.0 1.0 totals.1
  68.1 1.6 copy-done.8
  69.6 0.9 copy-done.10
  70.5 10.8 %all-to-all-start.1 = ((f32[32,8,768]{2,1,0:T(8,128)}), f32[32,8,768]{2,1,0:T(8,128)S(1)}, u32[]{:S(2)}, u32[]{:S(2)}) async-start(f32[32,8,768]{2,1,0:T(8,128)} %copy-done.10), calls=%async_computation.1 | async-start | bytes 1572864 | tf_op jit(solution)/shard_map/all_to_all | solution.py:459
  81.3 20.7 %all-to-all-done.1.p_ref = f32[32,8,768]{2,1,0:T(8,128)S(1)} async-done(((f32[32,8,768]{2,1,0:T(8,128)}), f32[32,8,768]{2,1,0:T(8,128)S(1)}, u32[]{:S(2)}, u32[]{:S(2)}) %all-to-all-start.1) | async-done | bytes 786464 | tf_op jit(solution)/shard_map/all_to_all | solution.py:459
  102.0 0.1 chain.1
  102.1 24.4 %all_to_all.15.edge_ref = f32[32,8,640]{2,1,0:T(8,128)S(1)} all-to-all(f32[32,8,640]{2,1,0:T(8,128)S(1)} %chain.1), channel_id=1, replica_groups=mesh['x'=4,'z'=8,'y'=4,'core'=2] {'x','z'}, dimensions={0} | all-to-all | bytes 1310720 | tf_op jit(solution)/shard_map/all_to_all | solution.py:459
  126.5 1.2 entering.1
  127.7 3.7 %collective-permute-start.6 = (bf16[2,192,640]{2,1,0:T(8,128)(2,1)S(1)}, bf16[2,192,640]{2,1,0:T(8,128)(2,1)S(1)}, u32[]{:S(2)}, u32[]{:S(2)}) collective-permute-start(bf16[2,192,640]{2,1,0:T(8,128)(2,1)S(1)} %get-tuple-element.80), channel_id=1, source_target_pairs={{0,6},{2,0},{4,2},{6,4},{1,7},{3,1},{5,3},{7,5},{8,14},{10,8},{12,... | collective-permute-start | bytes 1474568 | tf_op jit(solution)/shard_map/ppermute | solution.py:437
  131.4 0.7 collective-permute-start.4
  132.1 1.7 fork.4
  133.8 0.9 copy-done.11
  134.7 3.9 %collective-permute-start.7 = (f32[2,128,640]{2,1,0:T(8,128)}, f32[2,128,640]{2,1,0:T(8,128)}, u32[]{:S(2)}, u32[]{:S(2)}) collective-permute-start(f32[2,128,640]{2,1,0:T(8,128)} %get-tuple-element.82), channel_id=1, source_target_pairs={{0,1},{1,0},{2,3},{3,2},{4,5},{5,4},{6,7},{7,6},{8,9},{9,8},{10,11... | collective-permute-start | bytes 1966088 | tf_op jit(solution)/shard_map/ppermute | solution.py:458
  138.6 1.7 collective-permute-done.6.r_ref
  140.3 1.7 fork.7
  142.0 0.8 copy-done.12
  142.8 13.1 %collective-permute-start.10 = (f32[2,128,640]{2,1,0:T(8,128)}, f32[2,128,640]{2,1,0:T(8,128)}, u32[]{:S(2)}, u32[]{:S(2)}) collective-permute-start(f32[2,128,640]{2,1,0:T(8,128)} %get-tuple-element.85), channel_id=1, source_target_pairs={{0,1},{1,0},{2,3},{3,2},{4,5},{5,4},{6,7},{7,6},{8,9},{9,8},{10,11... | collective-permute-start | bytes 1966088 | tf_op jit(solution)/shard_map/ppermute | solution.py:458
  155.9 1.7 fork.6
  157.6 0.8 copy-done.13
  158.5 1.7 fork.5
  160.1 0.9 copy-done.14
  161.0 0.5 collective-permute-start.8
  161.5 1.9 collective-permute-done.8.c1
  163.5 0.8 copy-done.27
  164.3 16.9 %finish.1 = (bf16[192,5120]{1,0:T(8,128)(2,1)}, bf16[192,5120]{1,0:T(8,128)(2,1)}, f32[448,128]{1,0:T(8,128)}, f32[448,128]{1,0:T(8,128)}, f32[448,128]{1,0:T(8,128)}, /*index=5*/f32[448,128]{1,0:T(8,128)}) custom-call(s32[2]{0:T(128)} %copy-done.21, bf16[192,5120]{1,0:T(8,128)(2,1)} %x_ref.4, bf16[192,5120]{1,0:T(8,128)(2,1)} %dy_ref.4, ...), custom_call_target="tpu_custom_call" | custom-call | tf_op jit(solution)/shard_map/finish/pallas_call | solution.py:410
  181.2 3.5 %collective-permute-start.11 = (f32[448,128]{1,0:T(8,128)}, f32[448,128]{1,0:T(8,128)S(1)}, u32[]{:S(2)}, u32[]{:S(2)}) collective-permute-start(f32[448,128]{1,0:T(8,128)} %get-tuple-element.92), channel_id=1, source_target_pairs={{0,6},{2,0},{4,2},{6,4},{1,7},{3,1},{5,3},{7,5},{8,14},{10,8},{12,... | collective-permute-start | bytes 688136 | tf_op jit(solution)/shard_map/ppermute | solution.py:437
  184.7 0.7 collective-permute-start.13
  185.3 1.0 bitcast_dynamic-update-slice_fusion.6
  186.3 8.1 %collective-permute-done.11 = f32[448,128]{1,0:T(8,128)S(1)} collective-permute-done((f32[448,128]{1,0:T(8,128)}, f32[448,128]{1,0:T(8,128)S(1)}, u32[]{:S(2)}, u32[]{:S(2)}) %collective-permute-start.11) | collective-permute-done | bytes 229408 | tf_op jit(solution)/shard_map/ppermute | solution.py:437
  194.4 3.8 %collective-permute-done.13 = f32[448,128]{1,0:T(8,128)S(1)} collective-permute-done((f32[448,128]{1,0:T(8,128)}, f32[448,128]{1,0:T(8,128)S(1)}, u32[]{:S(2)}, u32[]{:S(2)}) %collective-permute-start.13) | collective-permute-done | bytes 229408 | tf_op jit(solution)/shard_map/ppermute | solution.py:437
  198.4 0.9 collective-permute-start.14
  199.3 2.2 %collective-permute-done.14 = f32[4,448,128]{2,1,0:T(8,128)} collective-permute-done((f32[4,448,128]{2,1,0:T(8,128)S(1)}, f32[4,448,128]{2,1,0:T(8,128)}, u32[]{:S(2)}, u32[]{:S(2)}) %collective-permute-start.14) | collective-permute-done | bytes 917536 | tf_op jit(solution)/shard_map/ppermute | solution.py:445
  201.6 1.3 select_bitcast_fusion.1
  202.9 0.1 pad_maximum_fusion
  203.0 0.1 copy.23
  203.2 1.3 fusion
  204.5 0.7 reshape.36
  (65 shorter events, 0.4 us)
Async XLA Ops:
  0.6 0.9 copy-start.17
  1.5 0.7 copy-start.25
  3.0 11.6 %all-to-all-start = ((f32[8,2,16,192]{3,2,1,0:T(8,128)}), f32[8,2,16,192]{3,2,1,0:T(8,128)S(1)}, u32[]{:S(2)}, u32[]{:S(2)}) async-start(f32[8,2,16,192]{3,2,1,0:T(8,128)} %pack.1), calls=%async_computation | async-start | bytes 524288 | tf_op jit(solution)/shard_map/all_to_all | solution.py:468
  9.0 29.3 %copy-start.15 = (bf16[192,128]{1,0:T(8,128)(2,1)}, bf16[192,128]{1,0:T(8,128)(2,1)S(1)}, u32[]{:S(2)}) copy-start(bf16[192,128]{1,0:T(8,128)(2,1)S(1)} %get-tuple-element.99.c_ref) | copy-start | bytes 147460
  9.0 29.3 %copy-start.16 = (bf16[192,128]{1,0:T(8,128)(2,1)}, bf16[192,128]{1,0:T(8,128)(2,1)S(1)}, u32[]{:S(2)}) copy-start(bf16[192,128]{1,0:T(8,128)(2,1)S(1)} %get-tuple-element.100.b_ref) | copy-start | bytes 147460
  10.5 6.3 %copy-start.21 = (s32[2]{0:T(128)}, s32[2]{0:T(128)S(1)}, u32[]{:S(2)}) copy-start(s32[2]{0:T(128)S(1)} %pad_add_fusion.core_ref.place.place_ref) | copy-start | bytes 28
  16.0 0.9 copy-start.6
  16.8 9.4 %copy-start.24 = (f32[8,1,640]{2,1,0:T(1,128)}, f32[8,1,640]{2,1,0:T(1,128)S(1)}, u32[]{:S(2)}) copy-start(f32[8,1,640]{2,1,0:T(1,128)S(1)} %get-tuple-element.86.gain_ref) | copy-start | bytes 61444
  26.3 5.8 %collective-permute-start = (f32[4,2,128,640]{3,2,1,0:T(8,128)}, f32[4,2,128,640]{3,2,1,0:T(8,128)S(1)}, u32[]{:S(2)}, u32[]{:S(2)}) collective-permute-start(f32[4,2,128,640]{3,2,1,0:T(8,128)} %get-tuple-element.52), channel_id=1, source_target_pairs={{0,1},{1,0},{2,3},{3,2},{4,5},{5,4},{6,7},{7,6},{8,9},{9,8},{10,11... | collective-permute-start | bytes 7864328 | tf_op jit(solution)/shard_map/ppermute | solution.py:458
  32.1 1.7 copy-start
  33.8 0.6 copy-start.22
  34.5 3.8 %copy-start.2 = (bf16[192,5120]{1,0:T(8,128)(2,1)S(1)}, bf16[192,5120]{1,0:T(8,128)(2,1)}, u32[]{:S(2)}) copy-start(bf16[192,5120]{1,0:T(8,128)(2,1)} %x_ref.4) | copy-start | bytes 5898244
  34.5 3.8 %copy-start.3 = (bf16[192,5120]{1,0:T(8,128)(2,1)S(1)}, bf16[192,5120]{1,0:T(8,128)(2,1)}, u32[]{:S(2)}) copy-start(bf16[192,5120]{1,0:T(8,128)(2,1)} %dy_ref.4) | copy-start | bytes 5898244
  34.5 3.8 %copy-start.7 = (f32[8,192,16]{2,1,0:T(8,128)S(1)}, f32[8,192,16]{2,1,0:T(8,128)}, u32[]{:S(2)}) copy-start(f32[8,192,16]{2,1,0:T(8,128)} %copy-done.6) | copy-start | bytes 294916
  35.4 18.8 %collective-permute-start.1 = (f32[2,128,640]{2,1,0:T(8,128)S(1)}, f32[2,128,640]{2,1,0:T(8,128)S(1)}, u32[]{:S(2)}, u32[]{:S(2)}) collective-permute-start(f32[2,128,640]{2,1,0:T(8,128)S(1)} %get-tuple-element.62), channel_id=1, source_target_pairs={{0,2},{2,4},{4,6},{6,0},{1,3},{3,5},{5,7},{7,1},{8,10},{10,12},{12... | collective-permute-start | bytes 1966088 | tf_op jit(solution)/shard_map/ppermute | solution.py:437
  35.7 30.4 %collective-permute-start.2 = (f32[2,128,640]{2,1,0:T(8,128)S(1)}, f32[2,128,640]{2,1,0:T(8,128)S(1)}, u32[]{:S(2)}, u32[]{:S(2)}) collective-permute-start(f32[2,128,640]{2,1,0:T(8,128)S(1)} %get-tuple-element.63), channel_id=1, source_target_pairs={{0,4},{2,6},{4,0},{6,2},{1,5},{3,7},{5,1},{7,3},{8,12},{10,14},{12... | collective-permute-start | bytes 1966088 | tf_op jit(solution)/shard_map/ppermute | solution.py:437
  37.5 29.5 %collective-permute-start.3 = (f32[2,128,640]{2,1,0:T(8,128)S(1)}, f32[2,128,640]{2,1,0:T(8,128)S(1)}, u32[]{:S(2)}, u32[]{:S(2)}) collective-permute-start(f32[2,128,640]{2,1,0:T(8,128)S(1)} %get-tuple-element.64), channel_id=1, source_target_pairs={{0,6},{2,0},{4,2},{6,4},{1,7},{3,1},{5,3},{7,5},{8,14},{10,8},{12,... | collective-permute-start | bytes 1966088 | tf_op jit(solution)/shard_map/ppermute | solution.py:437
  38.2 15.6 %copy-start.18 = (f32[1536,10]{0,1:T(8,128)S(1)}, f32[1536,10]{0,1:T(8,128)}, u32[]{:S(2)}) copy-start(f32[1536,10]{0,1:T(8,128)} %param.10) | copy-start | bytes 184324
  49.4 1.9 copy-start.4
  51.3 2.0 copy-start.5
  53.2 0.6 copy-start.19
  53.8 14.2 %copy-start.20 = (f32[192,128]{1,0:T(8,128)}, f32[192,128]{1,0:T(8,128)S(1)}, u32[]{:S(2)}) copy-start(f32[192,128]{1,0:T(8,128)S(1)} %get-tuple-element.88.dc0_ref) | copy-start | bytes 294916
  68.0 1.6 copy-start.8
  69.6 0.9 copy-start.10
  70.5 56.0 %copy-start.23 = (s32[2]{0:T(128)S(1)}, s32[2]{0:T(128)}, u32[]{:S(2)}) copy-start(s32[2]{0:T(128)} %copy-done.21) | copy-start | bytes 28
  70.5 31.4 %all-to-all-start.1 = ((f32[32,8,768]{2,1,0:T(8,128)}), f32[32,8,768]{2,1,0:T(8,128)S(1)}, u32[]{:S(2)}, u32[]{:S(2)}) async-start(f32[32,8,768]{2,1,0:T(8,128)} %copy-done.10), calls=%async_computation.1 | async-start | bytes 1572864 | tf_op jit(solution)/shard_map/all_to_all | solution.py:459
  102.0 24.5 %copy-start.9 = (f32[4,2,128,640]{3,2,1,0:T(8,128)S(1)}, f32[4,2,128,640]{3,2,1,0:T(8,128)}, u32[]{:S(2)}) copy-start(f32[4,2,128,640]{3,2,1,0:T(8,128)} %copy-done.8) | copy-start | bytes 7864324
  126.5 5.6 %copy-start.1 = (f32[4,2,128,640]{3,2,1,0:T(8,128)S(1)}, f32[4,2,128,640]{3,2,1,0:T(8,128)}, u32[]{:S(2)}) copy-start(f32[4,2,128,640]{3,2,1,0:T(8,128)} %get-tuple-element.51.keep_ref) | copy-start | bytes 7864324
  127.7 12.6 %collective-permute-start.6 = (bf16[2,192,640]{2,1,0:T(8,128)(2,1)S(1)}, bf16[2,192,640]{2,1,0:T(8,128)(2,1)S(1)}, u32[]{:S(2)}, u32[]{:S(2)}) collective-permute-start(bf16[2,192,640]{2,1,0:T(8,128)(2,1)S(1)} %get-tuple-element.80), channel_id=1, source_target_pairs={{0,6},{2,0},{4,2},{6,4},{1,7},{3,1},{5,3},{7,5},{8,14},{10,8},{12,... | collective-permute-start | bytes 1474568 | tf_op jit(solution)/shard_map/ppermute | solution.py:437
  131.4 24.5 %collective-permute-start.5 = (bf16[2,192,640]{2,1,0:T(8,128)(2,1)S(1)}, bf16[2,192,640]{2,1,0:T(8,128)(2,1)S(1)}, u32[]{:S(2)}, u32[]{:S(2)}) collective-permute-start(bf16[2,192,640]{2,1,0:T(8,128)(2,1)S(1)} %get-tuple-element.78), channel_id=1, source_target_pairs={{0,4},{2,6},{4,0},{6,2},{1,5},{3,7},{5,1},{7,3},{8,12},{10,14},{12... | collective-permute-start | bytes 1474568 | tf_op jit(solution)/shard_map/ppermute | solution.py:437
  131.4 27.0 %collective-permute-start.4 = (bf16[2,192,640]{2,1,0:T(8,128)(2,1)S(1)}, bf16[2,192,640]{2,1,0:T(8,128)(2,1)S(1)}, u32[]{:S(2)}, u32[]{:S(2)}) collective-permute-start(bf16[2,192,640]{2,1,0:T(8,128)(2,1)S(1)} %get-tuple-element.76), channel_id=1, source_target_pairs={{0,2},{2,4},{4,6},{6,0},{1,3},{3,5},{5,7},{7,1},{8,10},{10,12},{12... | collective-permute-start | bytes 1474568 | tf_op jit(solution)/shard_map/ppermute | solution.py:437
  133.8 0.9 copy-start.11
  134.7 26.8 %collective-permute-start.7 = (f32[2,128,640]{2,1,0:T(8,128)}, f32[2,128,640]{2,1,0:T(8,128)}, u32[]{:S(2)}, u32[]{:S(2)}) collective-permute-start(f32[2,128,640]{2,1,0:T(8,128)} %get-tuple-element.82), channel_id=1, source_target_pairs={{0,1},{1,0},{2,3},{3,2},{4,5},{5,4},{6,7},{7,6},{8,9},{9,8},{10,11... | collective-permute-start | bytes 1966088 | tf_op jit(solution)/shard_map/ppermute | solution.py:458
  142.0 0.8 copy-start.12
  142.8 18.7 %collective-permute-start.10 = (f32[2,128,640]{2,1,0:T(8,128)}, f32[2,128,640]{2,1,0:T(8,128)}, u32[]{:S(2)}, u32[]{:S(2)}) collective-permute-start(f32[2,128,640]{2,1,0:T(8,128)} %get-tuple-element.85), channel_id=1, source_target_pairs={{0,1},{1,0},{2,3},{3,2},{4,5},{5,4},{6,7},{7,6},{8,9},{9,8},{10,11... | collective-permute-start | bytes 1966088 | tf_op jit(solution)/shard_map/ppermute | solution.py:458
  157.6 0.8 copy-start.13
  158.5 3.1 %collective-permute-start.9 = (f32[2,128,640]{2,1,0:T(8,128)}, f32[2,128,640]{2,1,0:T(8,128)}, u32[]{:S(2)}, u32[]{:S(2)}) collective-permute-start(f32[2,128,640]{2,1,0:T(8,128)} %get-tuple-element.84), channel_id=1, source_target_pairs={{0,1},{1,0},{2,3},{3,2},{4,5},{5,4},{6,7},{7,6},{8,9},{9,8},{10,11... | collective-permute-start | bytes 1966088 | tf_op jit(solution)/shard_map/ppermute | solution.py:458
  160.1 0.9 copy-start.14
  161.0 2.4 %collective-permute-start.8 = (f32[2,128,640]{2,1,0:T(8,128)}, f32[2,128,640]{2,1,0:T(8,128)S(1)}, u32[]{:S(2)}, u32[]{:S(2)}) collective-permute-start(f32[2,128,640]{2,1,0:T(8,128)} %get-tuple-element.83), channel_id=1, source_target_pairs={{0,1},{1,0},{2,3},{3,2},{4,5},{5,4},{6,7},{7,6},{8,9},{9,8},{10,11... | collective-permute-start | bytes 1966088 | tf_op jit(solution)/shard_map/ppermute | solution.py:458
  163.4 0.8 copy-start.27
  181.2 17.1 %copy-start.26 = (f32[448,128]{1,0:T(8,128)S(1)}, f32[448,128]{1,0:T(8,128)}, u32[]{:S(2)}) copy-start(f32[448,128]{1,0:T(8,128)} %get-tuple-element.91) | copy-start | bytes 688132
  181.2 13.2 %collective-permute-start.11 = (f32[448,128]{1,0:T(8,128)}, f32[448,128]{1,0:T(8,128)S(1)}, u32[]{:S(2)}, u32[]{:S(2)}) collective-permute-start(f32[448,128]{1,0:T(8,128)} %get-tuple-element.92), channel_id=1, source_target_pairs={{0,6},{2,0},{4,2},{6,4},{1,7},{3,1},{5,3},{7,5},{8,14},{10,8},{12,... | collective-permute-start | bytes 688136 | tf_op jit(solution)/shard_map/ppermute | solution.py:437
  184.7 9.7 %collective-permute-start.12 = (f32[448,128]{1,0:T(8,128)}, f32[448,128]{1,0:T(8,128)S(1)}, u32[]{:S(2)}, u32[]{:S(2)}) collective-permute-start(f32[448,128]{1,0:T(8,128)} %get-tuple-element.93), channel_id=1, source_target_pairs={{0,4},{2,6},{4,0},{6,2},{1,5},{3,7},{5,1},{7,3},{8,12},{10,14},{12... | collective-permute-start | bytes 688136 | tf_op jit(solution)/shard_map/ppermute | solution.py:437
  184.7 13.6 %collective-permute-start.13 = (f32[448,128]{1,0:T(8,128)}, f32[448,128]{1,0:T(8,128)S(1)}, u32[]{:S(2)}, u32[]{:S(2)}) collective-permute-start(f32[448,128]{1,0:T(8,128)} %get-tuple-element.94), channel_id=1, source_target_pairs={{0,2},{2,4},{4,6},{6,0},{1,3},{3,5},{5,7},{7,1},{8,10},{10,12},{12... | collective-permute-start | bytes 688136 | tf_op jit(solution)/shard_map/ppermute | solution.py:437
  198.4 3.1 %collective-permute-start.14 = (f32[4,448,128]{2,1,0:T(8,128)S(1)}, f32[4,448,128]{2,1,0:T(8,128)}, u32[]{:S(2)}, u32[]{:S(2)}) collective-permute-start(f32[4,448,128]{2,1,0:T(8,128)S(1)} %constant_dynamic-slice_fusion), channel_id=1, source_target_pairs={{0,1},{1,0},{2,3},{3,2},{4,5},{5,4},{6,7},{7,6},{8,9},{9,8},{10,11... | collective-permute-start | bytes 2752520 | tf_op jit(solution)/shard_map/ppermute | solution.py:445

commit v4 on v2

--- a/solution.py
+++ b/solution.py
@@ -224,7 +224,7 @@
             out_specs=[quad, quad],
         ),
         out_shape=[jax.ShapeDtypeStruct((CHIPS, *PAIR), F32)] * 2,
-        compiler_params=pltpu.CompilerParams(vmem_limit_bytes=60 << 20),
+        compiler_params=pltpu.CompilerParams(vmem_limit_bytes=40 << 20),
         name="chunk_states",
     )(place, x, dy, cum, bt, ct)
 

time: 202 us -> 204 us (level)
    pallas_call x1, Pallas kernels: 9.44 us -> 6.82 us  [chunk_states(): pl.pallas_call(states_kernel, grid_spec=pltpu.PrefetchScalarGridSpec(num_...]
    unnamed x55, local copies, waits for them, and re-layouts: 13.7 us -> 16.2 us
  transfers between devices with their start and end apart: 14 -> 14, of which waited for: 13 -> 13; matrix products, arithmetic and copies ran while one was open for 2% -> 1% of each run, Pallas kernels for 6% -> 6%
where the time goes in v4:
time: 204 us; the launch traced here: 203 us
  waiting for transfers between devices  83.8 us (41%)
  Pallas kernels  42.9 us (21%)
  starting transfers between devices  29.8 us (15%)
  blocking collectives  24.4 us (12%)
  local copies, waits for them, and re-layouts  19.5 us (10%)
    ppermute x9, waiting for transfers between devices, turned(): lax.ppermute(v[turn], 'y', [(i, (i + turn) % CHIPS) for i in range(CHIPS)])  46.2 us
    all_to_all x1, blocking collectives, shards(): lax.all_to_all(v, ('x', 'z'), split_axis=0, concat_axis=0, tiled=True)  24.4 us
    all_to_all x1, waiting for transfers between devices, shards(): lax.all_to_all(v, ('x', 'z'), split_axis=0, concat_axis=0, tiled=True)  20.7 us
    unnamed x55, local copies, waits for them, and re-layouts  16.2 us
    pallas_call x1, Pallas kernels, finish(): pl.pallas_call(finish_kernel, grid_spec=pltpu.PrefetchScalarGridSpec(num_...  15.4 us
    pallas_call x1, Pallas kernels, within(): pl.pallas_call(within_kernel, grid=(GROUPS,), in_specs=[by_column, by_col...  11.1 us
    all_to_all x1, starting transfers between devices, shards(): lax.all_to_all(v, ('x', 'z'), split_axis=0, concat_axis=0, tiled=True)  10.6 us
    ppermute x9, starting transfers between devices, turned(): lax.ppermute(v[turn], 'y', [(i, (i + turn) % CHIPS) for i in range(CHIPS)])  10 us
  transfers between devices with their start and end apart: 14, of which 13 were waited for; matrix products, arithmetic and copies ran while one was open for 1% of the time, Pallas kernels for 6%

profile of v4, /device:TPU:33, one launch (start us, length us, event | category | flops | bytes accessed | tf_op | source)
XLA Modules:
  0.0 203.0 jit_solution(8029967879896557490)
XLA Ops:
  0.6 0.9 copy-done.14
  1.5 0.7 copy-done.21
  2.2 0.8 pack.1
  3.0 5.1 %all-to-all-start = ((f32[8,2,16,192]{3,2,1,0:T(8,128)}), f32[8,2,16,192]{3,2,1,0:T(8,128)S(1)}, u32[]{:S(2)}, u32[]{:S(2)}) async-start(f32[8,2,16,192]{3,2,1,0:T(8,128)} %pack.1), calls=%async_computation | async-start | bytes 524288 | tf_op jit(solution)/shard_map/all_to_all | solution.py:438
  8.1 0.8 constant_dynamic-slice_fusion.1
  9.0 0.1 copy.21.bt_ref
  9.1 0.1 copy.22.ct_ref
  9.2 0.1 pad_add_fusion.core_ref.place.place_ref
  9.3 5.4 %all-to-all-done.got_ref = f32[8,2,16,192]{3,2,1,0:T(8,128)S(1)} async-done(((f32[8,2,16,192]{3,2,1,0:T(8,128)}), f32[8,2,16,192]{3,2,1,0:T(8,128)S(1)}, u32[]{:S(2)}, u32[]{:S(2)}) %all-to-all-start) | async-done | bytes 196640 | tf_op jit(solution)/shard_map/all_to_all | solution.py:438
  14.6 1.3 decays.1
  16.0 0.0 copy-start.7
  16.0 0.0 copy-start.1
  16.0 1.9 copy-done.1
  17.9 1.5 copy-done.3
  19.4 6.8 %chunk_states.1 = (f32[4,2,128,640]{3,2,1,0:T(8,128)S(1)}, f32[4,2,128,640]{3,2,1,0:T(8,128)S(1)}) custom-call(s32[2]{0:T(128)S(1)} %pad_add_fusion.core_ref.place.place_ref, bf16[192,5120]{1,0:T(8,128)(2,1)S(1)} %copy-done.1, bf16[192,5120]{1,0:T(8,128)(2,1)S(1)} %copy-done.3, f32[8,192,16]{2,1,0:T(8,128)S(1)} %get-tuple-element.44.cum_ref, ...), custom_call_target="tpu_custom_call" | custom-call | tf_op jit(solution)/shard_map/chunk_states/pallas_call | solution.py:212
  26.2 1.1 collective-permute-start
  27.4 4.5 %collective-permute-done.come_ref = f32[4,2,128,640]{3,2,1,0:T(8,128)S(1)} collective-permute-done((f32[4,2,128,640]{3,2,1,0:T(8,128)S(1)}, f32[4,2,128,640]{3,2,1,0:T(8,128)S(1)}, u32[]{:S(2)}, u32[]{:S(2)}) %collective-permute-start) | collective-permute-done | bytes 2621472 | tf_op jit(solution)/shard_map/ppermute | solution.py:428
  31.9 0.9 join.1
  32.8 0.7 copy-done
  33.5 0.3 collective-permute-start.1
  33.8 1.8 collective-permute-start.2
  35.6 0.6 collective-permute-start.3
  36.2 0.0 copy-start.15
  36.2 11.1 %within_chunk.1 = (f32[192,5120]{1,0:T(8,128)S(1)}, f32[192,5120]{1,0:T(8,128)S(1)}, f32[192,128]{1,0:T(8,128)S(1)}, f32[192,128]{1,0:T(8,128)S(1)}) custom-call(bf16[192,5120]{1,0:T(8,128)(2,1)S(1)} %copy-done.2, bf16[192,5120]{1,0:T(8,128)(2,1)S(1)} %copy-done.4, f32[8,192,16]{2,1,0:T(8,128)S(1)} %get-tuple-element.44.cum_ref, ...), custom_call_target="tpu_custom_call" | custom-call | flops 20000000000 | bytes 12000000 | tf_op jit(solution)/shard_map/within_chunk/pallas_call | solution.py:108
  47.3 1.9 copy-done.5
  49.2 1.9 copy-done.6
  51.1 0.3 owner_decays.1.d_ref
  51.3 0.0 collective-permute-done.1.r1
  51.4 12.8 %collective-permute-done.2.r2 = f32[2,128,640]{2,1,0:T(8,128)S(1)} collective-permute-done((f32[2,128,640]{2,1,0:T(8,128)S(1)}, f32[2,128,640]{2,1,0:T(8,128)S(1)}, u32[]{:S(2)}, u32[]{:S(2)}) %collective-permute-start.2) | collective-permute-done | bytes 655392 | tf_op jit(solution)/shard_map/ppermute | solution.py:407
  64.1 0.9 collective-permute-done.3.r3
  65.0 1.0 totals.1
  66.1 1.6 copy-done.9
  67.7 0.9 copy-done.11
  68.6 10.6 %all-to-all-start.1 = ((f32[32,8,768]{2,1,0:T(8,128)}), f32[32,8,768]{2,1,0:T(8,128)S(1)}, u32[]{:S(2)}, u32[]{:S(2)}) async-start(f32[32,8,768]{2,1,0:T(8,128)} %copy-done.11), calls=%async_computation.1 | async-start | bytes 1572864 | tf_op jit(solution)/shard_map/all_to_all | solution.py:429
  79.2 20.7 %all-to-all-done.1.p_ref = f32[32,8,768]{2,1,0:T(8,128)S(1)} async-done(((f32[32,8,768]{2,1,0:T(8,128)}), f32[32,8,768]{2,1,0:T(8,128)S(1)}, u32[]{:S(2)}, u32[]{:S(2)}) %all-to-all-start.1) | async-done | bytes 786464 | tf_op jit(solution)/shard_map/all_to_all | solution.py:429
  99.9 0.1 chain.1
  100.0 24.4 %all_to_all.15.edge_ref = f32[32,8,640]{2,1,0:T(8,128)S(1)} all-to-all(f32[32,8,640]{2,1,0:T(8,128)S(1)} %chain.1), channel_id=1, replica_groups=mesh['x'=4,'z'=8,'y'=4,'core'=2] {'x','z'}, dimensions={0} | all-to-all | bytes 1310720 | tf_op jit(solution)/shard_map/all_to_all | solution.py:429
  124.4 1.2 entering.1
  125.6 1.7 collective-permute-start.4
  127.3 3.0 %collective-permute-start.5 = (bf16[2,192,640]{2,1,0:T(8,128)(2,1)S(1)}, bf16[2,192,640]{2,1,0:T(8,128)(2,1)S(1)}, u32[]{:S(2)}, u32[]{:S(2)}) collective-permute-start(bf16[2,192,640]{2,1,0:T(8,128)(2,1)S(1)} %get-tuple-element.70), channel_id=1, source_target_pairs={{0,4},{2,6},{4,0},{6,2},{1,5},{3,7},{5,1},{7,3},{8,12},{10,14},{12... | collective-permute-start | bytes 1474568 | tf_op jit(solution)/shard_map/ppermute | solution.py:407
  130.3 7.1 %collective-permute-done.4.r1 = bf16[2,192,640]{2,1,0:T(8,128)(2,1)S(1)} collective-permute-done((bf16[2,192,640]{2,1,0:T(8,128)(2,1)S(1)}, bf16[2,192,640]{2,1,0:T(8,128)(2,1)S(1)}, u32[]{:S(2)}, u32[]{:S(2)}) %collective-permute-start.4) | collective-permute-done | bytes 491552 | tf_op jit(solution)/shard_map/ppermute | solution.py:407
  137.4 11.4 %collective-permute-done.5.r2 = bf16[2,192,640]{2,1,0:T(8,128)(2,1)S(1)} collective-permute-done((bf16[2,192,640]{2,1,0:T(8,128)(2,1)S(1)}, bf16[2,192,640]{2,1,0:T(8,128)(2,1)S(1)}, u32[]{:S(2)}, u32[]{:S(2)}) %collective-permute-start.5) | collective-permute-done | bytes 491552 | tf_op jit(solution)/shard_map/ppermute | solution.py:407
  148.8 2.2 %collective-permute-done.6.r3 = bf16[2,192,640]{2,1,0:T(8,128)(2,1)S(1)} collective-permute-done((bf16[2,192,640]{2,1,0:T(8,128)(2,1)S(1)}, bf16[2,192,640]{2,1,0:T(8,128)(2,1)S(1)}, u32[]{:S(2)}, u32[]{:S(2)}) %collective-permute-start.6) | collective-permute-done | bytes 491552 | tf_op jit(solution)/shard_map/ppermute | solution.py:407
  151.0 4.1 %fork.1 = (f32[4,2,128,640]{3,2,1,0:T(8,128)S(1)}, f32[4,2,128,640]{3,2,1,0:T(8,128)}) custom-call(s32[2]{0:T(128)S(1)} %pad_add_fusion.core_ref.place.place_ref, bf16[2,192,640]{2,1,0:T(8,128)(2,1)S(1)} %get-tuple-element.68.r0, bf16[2,192,640]{2,1,0:T(8,128)(2,1)S(1)} %collective-permute-done.4.r1, bf16[2,192,640]{2,1,0:T(8,128)(2,1)S(1)} %collective-permute-done.5.r2, ...), custom_call_target="tpu_custom_call" | custom-call | tf_op jit(solution)/shard_map/fork/pallas_call | solution.py:138
  155.1 1.6 copy-done.8
  156.7 2.0 collective-permute-start.7
  158.7 4.7 %collective-permute-done.7.come_ref = f32[4,2,128,640]{3,2,1,0:T(8,128)S(1)} collective-permute-done((f32[4,2,128,640]{3,2,1,0:T(8,128)}, f32[4,2,128,640]{3,2,1,0:T(8,128)S(1)}, u32[]{:S(2)}, u32[]{:S(2)}) %collective-permute-start.7) | collective-permute-done | bytes 2621472 | tf_op jit(solution)/shard_map/ppermute | solution.py:428
  163.4 1.6 copy-done.22
  165.1 15.4 %finish.1 = (bf16[192,5120]{1,0:T(8,128)(2,1)}, bf16[192,5120]{1,0:T(8,128)(2,1)}, f32[448,128]{1,0:T(8,128)}, f32[448,128]{1,0:T(8,128)}, f32[448,128]{1,0:T(8,128)}, /*index=5*/f32[448,128]{1,0:T(8,128)}) custom-call(s32[2]{0:T(128)} %copy-done.19, bf16[192,5120]{1,0:T(8,128)(2,1)} %x_ref.4, bf16[192,5120]{1,0:T(8,128)(2,1)} %dy_ref.4, ...), custom_call_target="tpu_custom_call" | custom-call | tf_op jit(solution)/shard_map/finish/pallas_call | solution.py:381
  180.4 2.0 collective-permute-start.8
  182.4 0.7 collective-permute-start.10
  183.1 1.0 bitcast_dynamic-update-slice_fusion.6
  184.0 3.5 %collective-permute-done.8 = f32[448,128]{1,0:T(8,128)S(1)} collective-permute-done((f32[448,128]{1,0:T(8,128)}, f32[448,128]{1,0:T(8,128)S(1)}, u32[]{:S(2)}, u32[]{:S(2)}) %collective-permute-start.8) | collective-permute-done | bytes 229408 | tf_op jit(solution)/shard_map/ppermute | solution.py:407
  187.6 3.1 %collective-permute-done.9 = f32[448,128]{1,0:T(8,128)S(1)} collective-permute-done((f32[448,128]{1,0:T(8,128)}, f32[448,128]{1,0:T(8,128)S(1)}, u32[]{:S(2)}, u32[]{:S(2)}) %collective-permute-start.9) | collective-permute-done | bytes 229408 | tf_op jit(solution)/shard_map/ppermute | solution.py:407
  190.7 5.2 %collective-permute-done.10 = f32[448,128]{1,0:T(8,128)S(1)} collective-permute-done((f32[448,128]{1,0:T(8,128)}, f32[448,128]{1,0:T(8,128)S(1)}, u32[]{:S(2)}, u32[]{:S(2)}) %collective-permute-start.10) | collective-permute-done | bytes 229408 | tf_op jit(solution)/shard_map/ppermute | solution.py:407
  196.1 0.1 constant_dynamic-slice_fusion
  196.1 0.9 collective-permute-start.11
  197.1 2.2 %collective-permute-done.11 = f32[4,448,128]{2,1,0:T(8,128)} collective-permute-done((f32[4,448,128]{2,1,0:T(8,128)S(1)}, f32[4,448,128]{2,1,0:T(8,128)}, u32[]{:S(2)}, u32[]{:S(2)}) %collective-permute-start.11) | collective-permute-done | bytes 917536 | tf_op jit(solution)/shard_map/ppermute | solution.py:415
  199.3 1.3 select_bitcast_fusion.1
  200.6 0.1 pad_maximum_fusion
  200.7 0.1 copy.23
  200.9 1.3 fusion
  202.2 0.1 copy.25
  202.3 0.7 reshape.36
  (48 shorter events, 0.3 us)
Async XLA Ops:
  0.6 0.9 copy-start.14
  1.5 0.7 copy-start.21
  3.0 11.6 %all-to-all-start = ((f32[8,2,16,192]{3,2,1,0:T(8,128)}), f32[8,2,16,192]{3,2,1,0:T(8,128)S(1)}, u32[]{:S(2)}, u32[]{:S(2)}) async-start(f32[8,2,16,192]{3,2,1,0:T(8,128)} %pack.1), calls=%async_computation | async-start | bytes 524288 | tf_op jit(solution)/shard_map/all_to_all | solution.py:438
  9.0 27.2 %copy-start.12 = (bf16[192,128]{1,0:T(8,128)(2,1)}, bf16[192,128]{1,0:T(8,128)(2,1)S(1)}, u32[]{:S(2)}) copy-start(bf16[192,128]{1,0:T(8,128)(2,1)S(1)} %get-tuple-element.87.c_ref) | copy-start | bytes 147460
  9.0 27.2 %copy-start.13 = (bf16[192,128]{1,0:T(8,128)(2,1)}, bf16[192,128]{1,0:T(8,128)(2,1)S(1)}, u32[]{:S(2)}) copy-start(bf16[192,128]{1,0:T(8,128)(2,1)S(1)} %get-tuple-element.88.b_ref) | copy-start | bytes 147460
  9.3 141.7 %copy-start.19 = (s32[2]{0:T(128)}, s32[2]{0:T(128)S(1)}, u32[]{:S(2)}) copy-start(s32[2]{0:T(128)S(1)} %pad_add_fusion.core_ref.place.place_ref) | copy-start | bytes 28
  16.0 10.3 %copy-start.20 = (f32[8,1,640]{2,1,0:T(1,128)}, f32[8,1,640]{2,1,0:T(1,128)S(1)}, u32[]{:S(2)}) copy-start(f32[8,1,640]{2,1,0:T(1,128)S(1)} %get-tuple-element.74.gain_ref) | copy-start | bytes 61444
  16.0 20.2 %copy-start.7 = (f32[8,192,16]{2,1,0:T(8,128)}, f32[8,192,16]{2,1,0:T(8,128)S(1)}, u32[]{:S(2)}) copy-start(f32[8,192,16]{2,1,0:T(8,128)S(1)} %get-tuple-element.44.cum_ref) | copy-start | bytes 294916
  16.0 20.2 %copy-start.16 = (f32[8,16,192]{2,1,0:T(8,128)}, f32[8,16,192]{2,1,0:T(8,128)S(1)}, u32[]{:S(2)}) copy-start(f32[8,16,192]{2,1,0:T(8,128)S(1)} %get-tuple-element.45.cumt_ref) | copy-start | bytes 294916
  16.0 1.9 copy-start.1
  17.9 1.5 copy-start.3
  26.2 5.7 %collective-permute-start = (f32[4,2,128,640]{3,2,1,0:T(8,128)S(1)}, f32[4,2,128,640]{3,2,1,0:T(8,128)S(1)}, u32[]{:S(2)}, u32[]{:S(2)}) collective-permute-start(f32[4,2,128,640]{3,2,1,0:T(8,128)S(1)} %get-tuple-element.47), channel_id=1, source_target_pairs={{0,1},{1,0},{2,3},{3,2},{4,5},{5,4},{6,7},{7,6},{8,9},{9,8},{10,11... | collective-permute-start | bytes 7864328 | tf_op jit(solution)/shard_map/ppermute | solution.py:428
  31.9 1.6 copy-start
  31.9 4.3 %copy-start.2 = (bf16[192,5120]{1,0:T(8,128)(2,1)S(1)}, bf16[192,5120]{1,0:T(8,128)(2,1)}, u32[]{:S(2)}) copy-start(bf16[192,5120]{1,0:T(8,128)(2,1)} %x_ref.4) | copy-start | bytes 5898244
  31.9 4.3 %copy-start.4 = (bf16[192,5120]{1,0:T(8,128)(2,1)S(1)}, bf16[192,5120]{1,0:T(8,128)(2,1)}, u32[]{:S(2)}) copy-start(bf16[192,5120]{1,0:T(8,128)(2,1)} %dy_ref.4) | copy-start | bytes 5898244
  33.5 17.9 %collective-permute-start.1 = (f32[2,128,640]{2,1,0:T(8,128)S(1)}, f32[2,128,640]{2,1,0:T(8,128)S(1)}, u32[]{:S(2)}, u32[]{:S(2)}) collective-permute-start(f32[2,128,640]{2,1,0:T(8,128)S(1)} %get-tuple-element.56), channel_id=1, source_target_pairs={{0,2},{2,4},{4,6},{6,0},{1,3},{3,5},{5,7},{7,1},{8,10},{10,12},{12... | collective-permute-start | bytes 1966088 | tf_op jit(solution)/shard_map/ppermute | solution.py:407
  33.8 30.3 %collective-permute-start.2 = (f32[2,128,640]{2,1,0:T(8,128)S(1)}, f32[2,128,640]{2,1,0:T(8,128)S(1)}, u32[]{:S(2)}, u32[]{:S(2)}) collective-permute-start(f32[2,128,640]{2,1,0:T(8,128)S(1)} %get-tuple-element.57), channel_id=1, source_target_pairs={{0,4},{2,6},{4,0},{6,2},{1,5},{3,7},{5,1},{7,3},{8,12},{10,14},{12... | collective-permute-start | bytes 1966088 | tf_op jit(solution)/shard_map/ppermute | solution.py:407
  35.6 29.5 %collective-permute-start.3 = (f32[2,128,640]{2,1,0:T(8,128)S(1)}, f32[2,128,640]{2,1,0:T(8,128)S(1)}, u32[]{:S(2)}, u32[]{:S(2)}) collective-permute-start(f32[2,128,640]{2,1,0:T(8,128)S(1)} %get-tuple-element.58), channel_id=1, source_target_pairs={{0,6},{2,0},{4,2},{6,4},{1,7},{3,1},{5,3},{7,5},{8,14},{10,8},{12,... | collective-permute-start | bytes 1966088 | tf_op jit(solution)/shard_map/ppermute | solution.py:407
  36.2 14.9 %copy-start.15 = (f32[1536,10]{0,1:T(8,128)S(1)}, f32[1536,10]{0,1:T(8,128)}, u32[]{:S(2)}) copy-start(f32[1536,10]{0,1:T(8,128)} %param.10) | copy-start | bytes 184324
  47.3 1.9 copy-start.5
  49.2 1.9 copy-start.6
  51.1 15.0 %copy-start.18 = (f32[192,128]{1,0:T(8,128)}, f32[192,128]{1,0:T(8,128)S(1)}, u32[]{:S(2)}) copy-start(f32[192,128]{1,0:T(8,128)S(1)} %get-tuple-element.76.dc0_ref) | copy-start | bytes 294916
  51.1 17.5 %copy-start.17 = (f32[192,128]{1,0:T(8,128)}, f32[192,128]{1,0:T(8,128)S(1)}, u32[]{:S(2)}) copy-start(f32[192,128]{1,0:T(8,128)S(1)} %get-tuple-element.75.db0_ref) | copy-start | bytes 294916
  66.1 1.6 copy-start.9
  67.7 0.9 copy-start.11
  68.6 31.3 %all-to-all-start.1 = ((f32[32,8,768]{2,1,0:T(8,128)}), f32[32,8,768]{2,1,0:T(8,128)S(1)}, u32[]{:S(2)}, u32[]{:S(2)}) async-start(f32[32,8,768]{2,1,0:T(8,128)} %copy-done.11), calls=%async_computation.1 | async-start | bytes 1572864 | tf_op jit(solution)/shard_map/all_to_all | solution.py:429
  99.9 24.5 %copy-start.10 = (f32[4,2,128,640]{3,2,1,0:T(8,128)S(1)}, f32[4,2,128,640]{3,2,1,0:T(8,128)}, u32[]{:S(2)}) copy-start(f32[4,2,128,640]{3,2,1,0:T(8,128)} %copy-done.9) | copy-start | bytes 7864324
  125.6 11.7 %collective-permute-start.4 = (bf16[2,192,640]{2,1,0:T(8,128)(2,1)S(1)}, bf16[2,192,640]{2,1,0:T(8,128)(2,1)S(1)}, u32[]{:S(2)}, u32[]{:S(2)}) collective-permute-start(bf16[2,192,640]{2,1,0:T(8,128)(2,1)S(1)} %get-tuple-element.69), channel_id=1, source_target_pairs={{0,2},{2,4},{4,6},{6,0},{1,3},{3,5},{5,7},{7,1},{8,10},{10,12},{12... | collective-permute-start | bytes 1474568 | tf_op jit(solution)/shard_map/ppermute | solution.py:407
  127.3 21.5 %collective-permute-start.5 = (bf16[2,192,640]{2,1,0:T(8,128)(2,1)S(1)}, bf16[2,192,640]{2,1,0:T(8,128)(2,1)S(1)}, u32[]{:S(2)}, u32[]{:S(2)}) collective-permute-start(bf16[2,192,640]{2,1,0:T(8,128)(2,1)S(1)} %get-tuple-element.70), channel_id=1, source_target_pairs={{0,4},{2,6},{4,0},{6,2},{1,5},{3,7},{5,1},{7,3},{8,12},{10,14},{12... | collective-permute-start | bytes 1474568 | tf_op jit(solution)/shard_map/ppermute | solution.py:407
  130.3 20.7 %collective-permute-start.6 = (bf16[2,192,640]{2,1,0:T(8,128)(2,1)S(1)}, bf16[2,192,640]{2,1,0:T(8,128)(2,1)S(1)}, u32[]{:S(2)}, u32[]{:S(2)}) collective-permute-start(bf16[2,192,640]{2,1,0:T(8,128)(2,1)S(1)} %get-tuple-element.71), channel_id=1, source_target_pairs={{0,6},{2,0},{4,2},{6,4},{1,7},{3,1},{5,3},{7,5},{8,14},{10,8},{12,... | collective-permute-start | bytes 1474568 | tf_op jit(solution)/shard_map/ppermute | solution.py:407
  155.1 1.6 copy-start.8
  156.7 6.8 %collective-permute-start.7 = (f32[4,2,128,640]{3,2,1,0:T(8,128)}, f32[4,2,128,640]{3,2,1,0:T(8,128)S(1)}, u32[]{:S(2)}, u32[]{:S(2)}) collective-permute-start(f32[4,2,128,640]{3,2,1,0:T(8,128)} %get-tuple-element.73), channel_id=1, source_target_pairs={{0,1},{1,0},{2,3},{3,2},{4,5},{5,4},{6,7},{7,6},{8,9},{9,8},{10,11... | collective-permute-start | bytes 7864328 | tf_op jit(solution)/shard_map/ppermute | solution.py:428
  163.4 1.6 copy-start.22
  180.4 15.5 %copy-start.23 = (f32[448,128]{1,0:T(8,128)S(1)}, f32[448,128]{1,0:T(8,128)}, u32[]{:S(2)}) copy-start(f32[448,128]{1,0:T(8,128)} %get-tuple-element.79) | copy-start | bytes 688132
  180.4 7.1 %collective-permute-start.8 = (f32[448,128]{1,0:T(8,128)}, f32[448,128]{1,0:T(8,128)S(1)}, u32[]{:S(2)}, u32[]{:S(2)}) collective-permute-start(f32[448,128]{1,0:T(8,128)} %get-tuple-element.80), channel_id=1, source_target_pairs={{0,6},{2,0},{4,2},{6,4},{1,7},{3,1},{5,3},{7,5},{8,14},{10,8},{12,... | collective-permute-start | bytes 688136 | tf_op jit(solution)/shard_map/ppermute | solution.py:407
  182.4 8.3 %collective-permute-start.9 = (f32[448,128]{1,0:T(8,128)}, f32[448,128]{1,0:T(8,128)S(1)}, u32[]{:S(2)}, u32[]{:S(2)}) collective-permute-start(f32[448,128]{1,0:T(8,128)} %get-tuple-element.81), channel_id=1, source_target_pairs={{0,4},{2,6},{4,0},{6,2},{1,5},{3,7},{5,1},{7,3},{8,12},{10,14},{12... | collective-permute-start | bytes 688136 | tf_op jit(solution)/shard_map/ppermute | solution.py:407
  182.4 13.5 %collective-permute-start.10 = (f32[448,128]{1,0:T(8,128)}, f32[448,128]{1,0:T(8,128)S(1)}, u32[]{:S(2)}, u32[]{:S(2)}) collective-permute-start(f32[448,128]{1,0:T(8,128)} %get-tuple-element.82), channel_id=1, source_target_pairs={{0,2},{2,4},{4,6},{6,0},{1,3},{3,5},{5,7},{7,1},{8,10},{10,12},{12... | collective-permute-start | bytes 688136 | tf_op jit(solution)/shard_map/ppermute | solution.py:407
  196.1 3.2 %collective-permute-start.11 = (f32[4,448,128]{2,1,0:T(8,128)S(1)}, f32[4,448,128]{2,1,0:T(8,128)}, u32[]{:S(2)}, u32[]{:S(2)}) collective-permute-start(f32[4,448,128]{2,1,0:T(8,128)S(1)} %constant_dynamic-slice_fusion), channel_id=1, source_target_pairs={{0,1},{1,0},{2,3},{3,2},{4,5},{5,4},{6,7},{7,6},{8,9},{9,8},{10,11... | collective-permute-start | bytes 2752520 | tf_op jit(solution)/shard_map/ppermute | solution.py:415

commit v5 on v2

--- a/solution.py
+++ b/solution.py
@@ -301,7 +301,7 @@
 
 
 def finish_kernel(
-    place, x_ref, dy_ref, cum_ref, cumt_ref, y_ref, dx_ref, mine_ref, come_ref, gain_ref, b_ref, c_ref,
+    place, x_ref, dy_ref, cum_ref, y_ref, dx_ref, mine_ref, come_ref, gain_ref, b_ref, c_ref,
     db0_ref, dc0_ref, out_ref, gs_ref, o0, o1, o2, o3, db_ref, dc_ref, gd_ref,
 ):
     step = pl.program_id(0)
@@ -372,7 +372,7 @@
             out[416:448, 64:128] = jnp.zeros((32, 64), F32)
 
 
-def finish(place, x, dy, cum, cumt, y, dx, mine, come, gain, b, c, db, dc):
+def finish(place, x, dy, cum, y, dx, mine, come, gain, b, c, db, dc):
     columns = pl.BlockSpec((ROWS, 2 * GC), lambda s, place: (0, s))
     by_chip = lambda *shape: pl.BlockSpec((2, *shape), lambda s, place: (s, 0, 0))
     quad = pl.BlockSpec((1, *PAIR), lambda s, place: (s, 0, 0, 0))
@@ -384,7 +384,7 @@
             num_scalar_prefetch=1,
             grid=(CHIPS,),
             in_specs=[
-                columns, columns, by_chip(ROWS, 16), by_chip(16, ROWS), columns, columns, quad, quad,
+                columns, columns, by_chip(ROWS, 16), columns, columns, quad, quad,
                 by_chip(1, GC), *[whole(ROWS, N)] * 4,
             ],
             out_specs=[columns, columns] + [whole(448, 128)] * 4,
@@ -393,9 +393,9 @@
             ],
         ),
         out_shape=[wide, wide] + [jax.ShapeDtypeStruct((448, 128), F32)] * 4,
-        compiler_params=pltpu.CompilerParams(vmem_limit_bytes=60 << 20),
+        compiler_params=pltpu.CompilerParams(vmem_limit_bytes=57 << 20),
         name="finish",
-    )(place, x, dy, cum, cumt, y, dx, mine, come, gain, b, c, db, dc)
+    )(place, x, dy, cum, y, dx, mine, come, gain, b, c, db, dc)
 
 
 def tie(*values):
@@ -469,7 +469,7 @@
     )
     mine, send = on_chip(fork_kernel, "fork", [quad] * 2, place, *turned(out), keep, come, kept)
     scan_out, grad_x, *ends = finish(
-        place, x, dy, cum, cumt, y_in, dx_in, mine, swap(send), gain, b, c, db_in, dc_in
+        place, x, dy, cum, y_in, dx_in, mine, swap(send), gain, b, c, db_in, dc_in
     )
     ends = gathered(turned(ends), iy, core == 0)
     grad_b = ends[:, :ROWS].reshape(GROUPS * ROWS, N)

time: 202 us -> 202 us (level)
    unnamed x55 -> x53, local copies, waits for them, and re-layouts: 13.7 us -> 13.6 us
where the time goes in v5:
time: 202 us; the launch traced here: 201 us
  waiting for transfers between devices  82 us (41%)
  Pallas kernels  43.9 us (22%)
  starting transfers between devices  30.3 us (15%)
  blocking collectives  24.3 us (12%)
  local copies, waits for them, and re-layouts  18.3 us (9%)
    ppermute x9, waiting for transfers between devices, turned(): lax.ppermute(v[turn], 'y', [(i, (i + turn) % CHIPS) for i in range(CHIPS)])  45.5 us
    all_to_all x1, blocking collectives, shards(): lax.all_to_all(v, ('x', 'z'), split_axis=0, concat_axis=0, tiled=True)  24.3 us
    all_to_all x1, waiting for transfers between devices, shards(): lax.all_to_all(v, ('x', 'z'), split_axis=0, concat_axis=0, tiled=True)  20.7 us
    pallas_call x1, Pallas kernels, finish(): pl.pallas_call(finish_kernel, grid_spec=pltpu.PrefetchScalarGridSpec(num_...  15.3 us
    unnamed x53, local copies, waits for them, and re-layouts  13.6 us
    pallas_call x1, Pallas kernels, within(): pl.pallas_call(within_kernel, grid=(GROUPS,), in_specs=[by_column, by_col...  11.1 us
    all_to_all x1, starting transfers between devices, shards(): lax.all_to_all(v, ('x', 'z'), split_axis=0, concat_axis=0, tiled=True)  10.8 us
    ppermute x9, starting transfers between devices, turned(): lax.ppermute(v[turn], 'y', [(i, (i + turn) % CHIPS) for i in range(CHIPS)])  10.4 us
  transfers between devices with their start and end apart: 14, of which 13 were waited for; matrix products, arithmetic and copies ran while one was open for 2% of the time, Pallas kernels for 6%

profile of v5, /device:TPU:33, one launch (start us, length us, event | category | flops | bytes accessed | tf_op | source)
XLA Modules:
  0.0 201.2 jit_solution(11149701762675877124)
XLA Ops:
  0.6 0.0 copy-start.13
  0.6 0.9 copy-done.13
  1.5 0.7 copy-done.21
  2.2 0.8 pack.1
  3.0 5.1 %all-to-all-start = ((f32[8,2,16,192]{3,2,1,0:T(8,128)}), f32[8,2,16,192]{3,2,1,0:T(8,128)S(1)}, u32[]{:S(2)}, u32[]{:S(2)}) async-start(f32[8,2,16,192]{3,2,1,0:T(8,128)} %pack.1), calls=%async_computation | async-start | bytes 524288 | tf_op jit(solution)/shard_map/all_to_all | solution.py:438
  8.1 0.8 constant_dynamic-slice_fusion.1
  9.0 0.7 copy.21.bt_ref
  9.7 0.7 copy.22.ct_ref
  10.5 0.1 pad_add_fusion.core_ref.place.place_ref
  10.5 4.1 %all-to-all-done.got_ref = f32[8,2,16,192]{3,2,1,0:T(8,128)S(1)} async-done(((f32[8,2,16,192]{3,2,1,0:T(8,128)}), f32[8,2,16,192]{3,2,1,0:T(8,128)S(1)}, u32[]{:S(2)}, u32[]{:S(2)}) %all-to-all-start) | async-done | bytes 196640 | tf_op jit(solution)/shard_map/all_to_all | solution.py:438
  14.6 1.3 decays.1
  16.0 0.0 copy-start.7
  16.0 0.9 copy-done.7
  16.9 9.4 %chunk_states.1 = (f32[4,2,128,640]{3,2,1,0:T(8,128)}, f32[4,2,128,640]{3,2,1,0:T(8,128)}) custom-call(s32[2]{0:T(128)} %copy-done.17, bf16[192,5120]{1,0:T(8,128)(2,1)} %x_ref.4, bf16[192,5120]{1,0:T(8,128)(2,1)} %dy_ref.4, f32[8,192,16]{2,1,0:T(8,128)} %copy-done.7, bf16[128,192]{1,0:T(8,128)(2,1)} %copy.21.bt_ref, bf16[128,192]{1,0:T(8,128)(2,1)} %copy.22.ct_ref), custom_call_target="tpu_custom_call" | custom-call | tf_op jit(solution)/shard_map/chunk_states/pallas_call | solution.py:212
  26.3 1.1 collective-permute-start
  27.3 4.7 %collective-permute-done.come_ref = f32[4,2,128,640]{3,2,1,0:T(8,128)S(1)} collective-permute-done((f32[4,2,128,640]{3,2,1,0:T(8,128)}, f32[4,2,128,640]{3,2,1,0:T(8,128)S(1)}, u32[]{:S(2)}, u32[]{:S(2)}) %collective-permute-start) | collective-permute-done | bytes 2621472 | tf_op jit(solution)/shard_map/ppermute | solution.py:428
  32.1 2.7 %copy-done = f32[4,2,128,640]{3,2,1,0:T(8,128)S(1)} copy-done((f32[4,2,128,640]{3,2,1,0:T(8,128)S(1)}, f32[4,2,128,640]{3,2,1,0:T(8,128)}, u32[]{:S(2)}) %copy-start) | copy-done | bytes 2621464
  34.8 0.6 copy-done.18
  35.4 0.9 join.1
  36.3 0.4 collective-permute-start.1
  36.7 1.8 collective-permute-start.2
  38.4 0.7 collective-permute-start.3
  39.2 0.0 copy-start.14
  39.2 11.1 %within_chunk.1 = (f32[192,5120]{1,0:T(8,128)S(1)}, f32[192,5120]{1,0:T(8,128)S(1)}, f32[192,128]{1,0:T(8,128)S(1)}, f32[192,128]{1,0:T(8,128)S(1)}) custom-call(bf16[192,5120]{1,0:T(8,128)(2,1)S(1)} %copy-done.3, bf16[192,5120]{1,0:T(8,128)(2,1)S(1)} %copy-done.4, f32[8,192,16]{2,1,0:T(8,128)S(1)} %copy-done.8, ...), custom_call_target="tpu_custom_call" | custom-call | flops 20000000000 | bytes 12000000 | tf_op jit(solution)/shard_map/within_chunk/pallas_call | solution.py:108
  50.3 1.9 copy-done.5
  52.1 1.9 copy-done.6
  54.0 0.6 copy-done.15
  54.7 0.3 owner_decays.1.d_ref
  54.9 0.0 collective-permute-done.1.r1
  54.9 12.1 %collective-permute-done.2.r2 = f32[2,128,640]{2,1,0:T(8,128)S(1)} collective-permute-done((f32[2,128,640]{2,1,0:T(8,128)S(1)}, f32[2,128,640]{2,1,0:T(8,128)S(1)}, u32[]{:S(2)}, u32[]{:S(2)}) %collective-permute-start.2) | collective-permute-done | bytes 655392 | tf_op jit(solution)/shard_map/ppermute | solution.py:407
  67.0 0.9 collective-permute-done.3.r3
  67.9 1.0 totals.1
  68.9 0.0 copy-start.10
  69.0 0.9 copy-done.10
  69.8 10.8 %all-to-all-start.1 = ((f32[32,8,768]{2,1,0:T(8,128)}), f32[32,8,768]{2,1,0:T(8,128)S(1)}, u32[]{:S(2)}, u32[]{:S(2)}) async-start(f32[32,8,768]{2,1,0:T(8,128)} %copy-done.10), calls=%async_computation.1 | async-start | bytes 1572864 | tf_op jit(solution)/shard_map/all_to_all | solution.py:429
  80.6 20.7 %all-to-all-done.1.p_ref = f32[32,8,768]{2,1,0:T(8,128)S(1)} async-done(((f32[32,8,768]{2,1,0:T(8,128)}), f32[32,8,768]{2,1,0:T(8,128)S(1)}, u32[]{:S(2)}, u32[]{:S(2)}) %all-to-all-start.1) | async-done | bytes 786464 | tf_op jit(solution)/shard_map/all_to_all | solution.py:429
  101.3 0.1 chain.1
  101.4 24.3 %all_to_all.15.edge_ref = f32[32,8,640]{2,1,0:T(8,128)S(1)} all-to-all(f32[32,8,640]{2,1,0:T(8,128)S(1)} %chain.1), channel_id=1, replica_groups=mesh['x'=4,'z'=8,'y'=4,'core'=2] {'x','z'}, dimensions={0} | all-to-all | bytes 1310720 | tf_op jit(solution)/shard_map/all_to_all | solution.py:429
  125.7 1.2 entering.1
  126.9 1.8 collective-permute-start.4
  128.7 3.1 %collective-permute-start.5 = (bf16[2,192,640]{2,1,0:T(8,128)(2,1)S(1)}, bf16[2,192,640]{2,1,0:T(8,128)(2,1)S(1)}, u32[]{:S(2)}, u32[]{:S(2)}) collective-permute-start(bf16[2,192,640]{2,1,0:T(8,128)(2,1)S(1)} %get-tuple-element.70), channel_id=1, source_target_pairs={{0,4},{2,6},{4,0},{6,2},{1,5},{3,7},{5,1},{7,3},{8,12},{10,14},{12... | collective-permute-start | bytes 1474568 | tf_op jit(solution)/shard_map/ppermute | solution.py:407
  131.8 7.1 %collective-permute-done.4.r1 = bf16[2,192,640]{2,1,0:T(8,128)(2,1)S(1)} collective-permute-done((bf16[2,192,640]{2,1,0:T(8,128)(2,1)S(1)}, bf16[2,192,640]{2,1,0:T(8,128)(2,1)S(1)}, u32[]{:S(2)}, u32[]{:S(2)}) %collective-permute-start.4) | collective-permute-done | bytes 491552 | tf_op jit(solution)/shard_map/ppermute | solution.py:407
  138.8 11.4 %collective-permute-done.5.r2 = bf16[2,192,640]{2,1,0:T(8,128)(2,1)S(1)} collective-permute-done((bf16[2,192,640]{2,1,0:T(8,128)(2,1)S(1)}, bf16[2,192,640]{2,1,0:T(8,128)(2,1)S(1)}, u32[]{:S(2)}, u32[]{:S(2)}) %collective-permute-start.5) | collective-permute-done | bytes 491552 | tf_op jit(solution)/shard_map/ppermute | solution.py:407
  150.3 2.2 %collective-permute-done.6.r3 = bf16[2,192,640]{2,1,0:T(8,128)(2,1)S(1)} collective-permute-done((bf16[2,192,640]{2,1,0:T(8,128)(2,1)S(1)}, bf16[2,192,640]{2,1,0:T(8,128)(2,1)S(1)}, u32[]{:S(2)}, u32[]{:S(2)}) %collective-permute-start.6) | collective-permute-done | bytes 491552 | tf_op jit(solution)/shard_map/ppermute | solution.py:407
  152.5 2.5 %fork.1 = (f32[4,2,128,640]{3,2,1,0:T(8,128)S(1)}, f32[4,2,128,640]{3,2,1,0:T(8,128)S(1)}) custom-call(s32[2]{0:T(128)S(1)} %copy-done.19, bf16[2,192,640]{2,1,0:T(8,128)(2,1)S(1)} %get-tuple-element.68.r0, bf16[2,192,640]{2,1,0:T(8,128)(2,1)S(1)} %collective-permute-done.4.r1, bf16[2,192,640]{2,1,0:T(8,128)(2,1)S(1)} %collective-permute-done.5.r2, ...), custom_call_target="tpu_custom_call" | custom-call | tf_op jit(solution)/shard_map/fork/pallas_call | solution.py:138
  155.0 1.6 copy-done.9
  156.6 2.0 %collective-permute-start.7 = (f32[4,2,128,640]{3,2,1,0:T(8,128)S(1)}, f32[4,2,128,640]{3,2,1,0:T(8,128)}, u32[]{:S(2)}, u32[]{:S(2)}) collective-permute-start(f32[4,2,128,640]{3,2,1,0:T(8,128)S(1)} %get-tuple-element.73), channel_id=1, source_target_pairs={{0,1},{1,0},{2,3},{3,2},{4,5},{5,4},{6,7},{7,6},{8,9},{9,8},{10,11... | collective-permute-start | bytes 7864328 | tf_op jit(solution)/shard_map/ppermute | solution.py:428
  158.6 4.7 %collective-permute-done.7.come_ref = f32[4,2,128,640]{3,2,1,0:T(8,128)} collective-permute-done((f32[4,2,128,640]{3,2,1,0:T(8,128)S(1)}, f32[4,2,128,640]{3,2,1,0:T(8,128)}, u32[]{:S(2)}, u32[]{:S(2)}) %collective-permute-start.7) | collective-permute-done | bytes 2621472 | tf_op jit(solution)/shard_map/ppermute | solution.py:428
  163.2 15.3 %finish.1 = (bf16[192,5120]{1,0:T(8,128)(2,1)}, bf16[192,5120]{1,0:T(8,128)(2,1)}, f32[448,128]{1,0:T(8,128)}, f32[448,128]{1,0:T(8,128)}, f32[448,128]{1,0:T(8,128)}, /*index=5*/f32[448,128]{1,0:T(8,128)}) custom-call(s32[2]{0:T(128)} %copy-done.17, bf16[192,5120]{1,0:T(8,128)(2,1)} %x_ref.4, bf16[192,5120]{1,0:T(8,128)(2,1)} %dy_ref.4, ...), custom_call_target="tpu_custom_call" | custom-call | tf_op jit(solution)/shard_map/finish/pallas_call | solution.py:381
  178.6 2.0 collective-permute-start.8
  180.6 0.7 collective-permute-start.10
  181.2 1.0 bitcast_dynamic-update-slice_fusion.6
  182.2 3.5 %collective-permute-done.8 = f32[448,128]{1,0:T(8,128)S(1)} collective-permute-done((f32[448,128]{1,0:T(8,128)}, f32[448,128]{1,0:T(8,128)S(1)}, u32[]{:S(2)}, u32[]{:S(2)}) %collective-permute-start.8) | collective-permute-done | bytes 229408 | tf_op jit(solution)/shard_map/ppermute | solution.py:407
  185.7 3.1 %collective-permute-done.9 = f32[448,128]{1,0:T(8,128)S(1)} collective-permute-done((f32[448,128]{1,0:T(8,128)}, f32[448,128]{1,0:T(8,128)S(1)}, u32[]{:S(2)}, u32[]{:S(2)}) %collective-permute-start.9) | collective-permute-done | bytes 229408 | tf_op jit(solution)/shard_map/ppermute | solution.py:407
  188.9 5.2 %collective-permute-done.10 = f32[448,128]{1,0:T(8,128)S(1)} collective-permute-done((f32[448,128]{1,0:T(8,128)}, f32[448,128]{1,0:T(8,128)S(1)}, u32[]{:S(2)}, u32[]{:S(2)}) %collective-permute-start.10) | collective-permute-done | bytes 229408 | tf_op jit(solution)/shard_map/ppermute | solution.py:407
  194.2 0.1 constant_dynamic-slice_fusion
  194.3 0.9 collective-permute-start.11
  195.2 2.2 %collective-permute-done.11 = f32[4,448,128]{2,1,0:T(8,128)} collective-permute-done((f32[4,448,128]{2,1,0:T(8,128)S(1)}, f32[4,448,128]{2,1,0:T(8,128)}, u32[]{:S(2)}, u32[]{:S(2)}) %collective-permute-start.11) | collective-permute-done | bytes 917536 | tf_op jit(solution)/shard_map/ppermute | solution.py:415
  197.4 1.3 select_bitcast_fusion.1
  198.7 0.1 pad_maximum_fusion
  198.9 0.1 copy.23
  199.1 1.3 fusion
  200.4 0.1 copy.25
  200.4 0.7 reshape.36
  (46 shorter events, 0.2 us)
Async XLA Ops:
  0.6 0.9 copy-start.13
  1.5 0.7 copy-start.21
  3.0 11.6 %all-to-all-start = ((f32[8,2,16,192]{3,2,1,0:T(8,128)}), f32[8,2,16,192]{3,2,1,0:T(8,128)S(1)}, u32[]{:S(2)}, u32[]{:S(2)}) async-start(f32[8,2,16,192]{3,2,1,0:T(8,128)} %pack.1), calls=%async_computation | async-start | bytes 524288 | tf_op jit(solution)/shard_map/all_to_all | solution.py:438
  9.0 30.2 %copy-start.11 = (bf16[192,128]{1,0:T(8,128)(2,1)}, bf16[192,128]{1,0:T(8,128)(2,1)S(1)}, u32[]{:S(2)}) copy-start(bf16[192,128]{1,0:T(8,128)(2,1)S(1)} %get-tuple-element.87.c_ref) | copy-start | bytes 147460
  9.0 30.2 %copy-start.12 = (bf16[192,128]{1,0:T(8,128)(2,1)}, bf16[192,128]{1,0:T(8,128)(2,1)S(1)}, u32[]{:S(2)}) copy-start(bf16[192,128]{1,0:T(8,128)(2,1)S(1)} %get-tuple-element.88.b_ref) | copy-start | bytes 147460
  10.5 6.3 %copy-start.17 = (s32[2]{0:T(128)}, s32[2]{0:T(128)S(1)}, u32[]{:S(2)}) copy-start(s32[2]{0:T(128)S(1)} %pad_add_fusion.core_ref.place.place_ref) | copy-start | bytes 28
  16.0 0.9 copy-start.7
  16.9 9.4 %copy-start.20 = (f32[8,1,640]{2,1,0:T(1,128)}, f32[8,1,640]{2,1,0:T(1,128)S(1)}, u32[]{:S(2)}) copy-start(f32[8,1,640]{2,1,0:T(1,128)S(1)} %get-tuple-element.74.gain_ref) | copy-start | bytes 61444
  26.3 5.8 %collective-permute-start = (f32[4,2,128,640]{3,2,1,0:T(8,128)}, f32[4,2,128,640]{3,2,1,0:T(8,128)S(1)}, u32[]{:S(2)}, u32[]{:S(2)}) collective-permute-start(f32[4,2,128,640]{3,2,1,0:T(8,128)} %get-tuple-element.46), channel_id=1, source_target_pairs={{0,1},{1,0},{2,3},{3,2},{4,5},{5,4},{6,7},{7,6},{8,9},{9,8},{10,11... | collective-permute-start | bytes 7864328 | tf_op jit(solution)/shard_map/ppermute | solution.py:428
  32.1 4.2 %copy-start.2 = (f32[4,2,128,640]{3,2,1,0:T(8,128)}, f32[4,2,128,640]{3,2,1,0:T(8,128)S(1)}, u32[]{:S(2)}) copy-start(f32[4,2,128,640]{3,2,1,0:T(8,128)S(1)} %collective-permute-done.come_ref) | copy-start | bytes 7864324
  32.1 2.7 %copy-start = (f32[4,2,128,640]{3,2,1,0:T(8,128)S(1)}, f32[4,2,128,640]{3,2,1,0:T(8,128)}, u32[]{:S(2)}) copy-start(f32[4,2,128,640]{3,2,1,0:T(8,128)} %get-tuple-element.45.keep_ref) | copy-start | bytes 7864324
  34.8 0.6 copy-start.18
  35.4 3.8 %copy-start.3 = (bf16[192,5120]{1,0:T(8,128)(2,1)S(1)}, bf16[192,5120]{1,0:T(8,128)(2,1)}, u32[]{:S(2)}) copy-start(bf16[192,5120]{1,0:T(8,128)(2,1)} %x_ref.4) | copy-start | bytes 5898244
  35.4 3.8 %copy-start.4 = (bf16[192,5120]{1,0:T(8,128)(2,1)S(1)}, bf16[192,5120]{1,0:T(8,128)(2,1)}, u32[]{:S(2)}) copy-start(bf16[192,5120]{1,0:T(8,128)(2,1)} %dy_ref.4) | copy-start | bytes 5898244
  35.4 3.8 %copy-start.8 = (f32[8,192,16]{2,1,0:T(8,128)S(1)}, f32[8,192,16]{2,1,0:T(8,128)}, u32[]{:S(2)}) copy-start(f32[8,192,16]{2,1,0:T(8,128)} %copy-done.7) | copy-start | bytes 294916
  36.3 18.6 %collective-permute-start.1 = (f32[2,128,640]{2,1,0:T(8,128)S(1)}, f32[2,128,640]{2,1,0:T(8,128)S(1)}, u32[]{:S(2)}, u32[]{:S(2)}) collective-permute-start(f32[2,128,640]{2,1,0:T(8,128)S(1)} %get-tuple-element.56), channel_id=1, source_target_pairs={{0,2},{2,4},{4,6},{6,0},{1,3},{3,5},{5,7},{7,1},{8,10},{10,12},{12... | collective-permute-start | bytes 1966088 | tf_op jit(solution)/shard_map/ppermute | solution.py:407
  36.7 30.4 %collective-permute-start.2 = (f32[2,128,640]{2,1,0:T(8,128)S(1)}, f32[2,128,640]{2,1,0:T(8,128)S(1)}, u32[]{:S(2)}, u32[]{:S(2)}) collective-permute-start(f32[2,128,640]{2,1,0:T(8,128)S(1)} %get-tuple-element.57), channel_id=1, source_target_pairs={{0,4},{2,6},{4,0},{6,2},{1,5},{3,7},{5,1},{7,3},{8,12},{10,14},{12... | collective-permute-start | bytes 1966088 | tf_op jit(solution)/shard_map/ppermute | solution.py:407
  38.4 29.5 %collective-permute-start.3 = (f32[2,128,640]{2,1,0:T(8,128)S(1)}, f32[2,128,640]{2,1,0:T(8,128)S(1)}, u32[]{:S(2)}, u32[]{:S(2)}) collective-permute-start(f32[2,128,640]{2,1,0:T(8,128)S(1)} %get-tuple-element.58), channel_id=1, source_target_pairs={{0,6},{2,0},{4,2},{6,4},{1,7},{3,1},{5,3},{7,5},{8,14},{10,8},{12,... | collective-permute-start | bytes 1966088 | tf_op jit(solution)/shard_map/ppermute | solution.py:407
  39.2 15.5 %copy-start.14 = (f32[1536,10]{0,1:T(8,128)S(1)}, f32[1536,10]{0,1:T(8,128)}, u32[]{:S(2)}) copy-start(f32[1536,10]{0,1:T(8,128)} %param.10) | copy-start | bytes 184324
  50.2 1.9 copy-start.5
  52.1 1.9 copy-start.6
  54.0 0.6 copy-start.15
  54.7 14.3 %copy-start.16 = (f32[192,128]{1,0:T(8,128)}, f32[192,128]{1,0:T(8,128)S(1)}, u32[]{:S(2)}) copy-start(f32[192,128]{1,0:T(8,128)S(1)} %get-tuple-element.76.dc0_ref) | copy-start | bytes 294916
  68.9 0.9 copy-start.10
  69.8 55.8 %copy-start.19 = (s32[2]{0:T(128)S(1)}, s32[2]{0:T(128)}, u32[]{:S(2)}) copy-start(s32[2]{0:T(128)} %copy-done.17) | copy-start | bytes 28
  69.8 31.4 %all-to-all-start.1 = ((f32[32,8,768]{2,1,0:T(8,128)}), f32[32,8,768]{2,1,0:T(8,128)S(1)}, u32[]{:S(2)}, u32[]{:S(2)}) async-start(f32[32,8,768]{2,1,0:T(8,128)} %copy-done.10), calls=%async_computation.1 | async-start | bytes 1572864 | tf_op jit(solution)/shard_map/all_to_all | solution.py:429
  125.7 26.8 %copy-start.1 = (f32[4,2,128,640]{3,2,1,0:T(8,128)S(1)}, f32[4,2,128,640]{3,2,1,0:T(8,128)}, u32[]{:S(2)}) copy-start(f32[4,2,128,640]{3,2,1,0:T(8,128)} %get-tuple-element.45.keep_ref) | copy-start | bytes 7864324
  126.9 11.9 %collective-permute-start.4 = (bf16[2,192,640]{2,1,0:T(8,128)(2,1)S(1)}, bf16[2,192,640]{2,1,0:T(8,128)(2,1)S(1)}, u32[]{:S(2)}, u32[]{:S(2)}) collective-permute-start(bf16[2,192,640]{2,1,0:T(8,128)(2,1)S(1)} %get-tuple-element.69), channel_id=1, source_target_pairs={{0,2},{2,4},{4,6},{6,0},{1,3},{3,5},{5,7},{7,1},{8,10},{10,12},{12... | collective-permute-start | bytes 1474568 | tf_op jit(solution)/shard_map/ppermute | solution.py:407
  128.7 21.6 %collective-permute-start.5 = (bf16[2,192,640]{2,1,0:T(8,128)(2,1)S(1)}, bf16[2,192,640]{2,1,0:T(8,128)(2,1)S(1)}, u32[]{:S(2)}, u32[]{:S(2)}) collective-permute-start(bf16[2,192,640]{2,1,0:T(8,128)(2,1)S(1)} %get-tuple-element.70), channel_id=1, source_target_pairs={{0,4},{2,6},{4,0},{6,2},{1,5},{3,7},{5,1},{7,3},{8,12},{10,14},{12... | collective-permute-start | bytes 1474568 | tf_op jit(solution)/shard_map/ppermute | solution.py:407
  131.8 20.7 %collective-permute-start.6 = (bf16[2,192,640]{2,1,0:T(8,128)(2,1)S(1)}, bf16[2,192,640]{2,1,0:T(8,128)(2,1)S(1)}, u32[]{:S(2)}, u32[]{:S(2)}) collective-permute-start(bf16[2,192,640]{2,1,0:T(8,128)(2,1)S(1)} %get-tuple-element.71), channel_id=1, source_target_pairs={{0,6},{2,0},{4,2},{6,4},{1,7},{3,1},{5,3},{7,5},{8,14},{10,8},{12,... | collective-permute-start | bytes 1474568 | tf_op jit(solution)/shard_map/ppermute | solution.py:407
  155.0 1.6 copy-start.9
  156.6 6.7 %collective-permute-start.7 = (f32[4,2,128,640]{3,2,1,0:T(8,128)S(1)}, f32[4,2,128,640]{3,2,1,0:T(8,128)}, u32[]{:S(2)}, u32[]{:S(2)}) collective-permute-start(f32[4,2,128,640]{3,2,1,0:T(8,128)S(1)} %get-tuple-element.73), channel_id=1, source_target_pairs={{0,1},{1,0},{2,3},{3,2},{4,5},{5,4},{6,7},{7,6},{8,9},{9,8},{10,11... | collective-permute-start | bytes 7864328 | tf_op jit(solution)/shard_map/ppermute | solution.py:428
  178.6 15.5 %copy-start.22 = (f32[448,128]{1,0:T(8,128)S(1)}, f32[448,128]{1,0:T(8,128)}, u32[]{:S(2)}) copy-start(f32[448,128]{1,0:T(8,128)} %get-tuple-element.79) | copy-start | bytes 688132
  178.6 7.1 %collective-permute-start.8 = (f32[448,128]{1,0:T(8,128)}, f32[448,128]{1,0:T(8,128)S(1)}, u32[]{:S(2)}, u32[]{:S(2)}) collective-permute-start(f32[448,128]{1,0:T(8,128)} %get-tuple-element.80), channel_id=1, source_target_pairs={{0,6},{2,0},{4,2},{6,4},{1,7},{3,1},{5,3},{7,5},{8,14},{10,8},{12,... | collective-permute-start | bytes 688136 | tf_op jit(solution)/shard_map/ppermute | solution.py:407
  180.6 8.3 %collective-permute-start.9 = (f32[448,128]{1,0:T(8,128)}, f32[448,128]{1,0:T(8,128)S(1)}, u32[]{:S(2)}, u32[]{:S(2)}) collective-permute-start(f32[448,128]{1,0:T(8,128)} %get-tuple-element.81), channel_id=1, source_target_pairs={{0,4},{2,6},{4,0},{6,2},{1,5},{3,7},{5,1},{7,3},{8,12},{10,14},{12... | collective-permute-start | bytes 688136 | tf_op jit(solution)/shard_map/ppermute | solution.py:407
  180.6 13.5 %collective-permute-start.10 = (f32[448,128]{1,0:T(8,128)}, f32[448,128]{1,0:T(8,128)S(1)}, u32[]{:S(2)}, u32[]{:S(2)}) collective-permute-start(f32[448,128]{1,0:T(8,128)} %get-tuple-element.82), channel_id=1, source_target_pairs={{0,2},{2,4},{4,6},{6,0},{1,3},{3,5},{5,7},{7,1},{8,10},{10,12},{12... | collective-permute-start | bytes 688136 | tf_op jit(solution)/shard_map/ppermute | solution.py:407
  194.3 3.1 %collective-permute-start.11 = (f32[4,448,128]{2,1,0:T(8,128)S(1)}, f32[4,448,128]{2,1,0:T(8,128)}, u32[]{:S(2)}, u32[]{:S(2)}) collective-permute-start(f32[4,448,128]{2,1,0:T(8,128)S(1)} %constant_dynamic-slice_fusion), channel_id=1, source_target_pairs={{0,1},{1,0},{2,3},{3,2},{4,5},{5,4},{6,7},{7,6},{8,9},{9,8},{10,11... | collective-permute-start | bytes 2752520 | tf_op jit(solution)/shard_map/ppermute | solution.py:415
